TPU v7x, 32 devices: a whole 2x2x4 slice. The times are simulated.
32 devices in a mesh: swap: 8 (over z, y), blk: 4 (over x, core).
Axes of the slice: x: 2, y: 2, z: 4, core: 2. Of those that a mesh axis runs over, the one named last changes fastest.
Arguments:
- queries: bfloat16 [4096, 4096], P(('blk', 'swap')), may hold values from -6 to 6
- keys: bfloat16 [4096, 512], P(('blk', 'swap')), may hold values from -6 to 6
- values: bfloat16 [4096, 512], P(('blk', 'swap')), may hold values from -6 to 6
- grad_out: bfloat16 [4096, 4096], P(('blk', 'swap')), may hold values from -6 to 6
- doc_ids: int32 [4096], replicated, may hold values from 0 to 4095, as said below
Outputs:
- grad_queries: bfloat16 [4096, 4096], P(('blk', 'swap'))
- grad_keys: bfloat16 [4096, 512], P(('blk', 'swap'))
- grad_values: bfloat16 [4096, 512], P(('blk', 'swap'))
Inputs may be any that keep to these rules, and one draw needn't show every extreme that they name: `doc_ids`: each token's label is the position of the first token of its document, so labels never fall along the sequence; each document holds 1 to 1024 tokens, the last token is a document of its own, and in every draw a document of exactly 1024 tokens ends on the first token of some block of 1024 tokens after the first block.
All inputs are finite; a program needn't handle non-finite values.
Results may differ from a plain program's by a relative error of at most 0.0058.
Values may be sent and summed in bfloat16 or wider, within the bound.
No kernel may reach another device: no remote copies, remote signals or barrier semaphores. Data moves between devices by JAX's collectives and lax.ppermute only.
A program may use at most 64 MiB of HBM per device.

v0:
```python
import math

import jax
import jax.numpy as jnp
from jax import lax
from jax.sharding import PartitionSpec as P

HEAD_DIM = 128
MOST = 1024


masked_value = -1e30


def passed_along(block, axis, distance):
    devices = range(lax.axis_size(axis))
    route = [(i - distance, i) for i in devices if i - distance in devices]
    return lax.ppermute(block, axis, route)


def body(queries, keys, values, grad_out, doc_ids):
    inv_root = 1.0 / math.sqrt(HEAD_DIM)
    tok_rows = queries.shape[0]
    swap_size = lax.axis_size("swap")
    head_total = queries.shape[1] // HEAD_DIM
    kv_total = keys.shape[1] // HEAD_DIM
    heads_here = head_total // swap_size
    repeats = swap_size // kv_total
    seq_blk = tok_rows * swap_size
    k_slots = jnp.repeat(keys.reshape(tok_rows, kv_total, HEAD_DIM), repeats, axis=1).reshape(
        tok_rows, swap_size * HEAD_DIM
    )
    v_slots = jnp.repeat(values.reshape(tok_rows, kv_total, HEAD_DIM), repeats, axis=1).reshape(
        tok_rows, swap_size * HEAD_DIM
    )
    q_heads, g_heads, k_block, v_block = (
        lax.all_to_all(queries, "swap", split_axis=1, concat_axis=0, tiled=True),
        lax.all_to_all(grad_out, "swap", split_axis=1, concat_axis=0, tiled=True),
        lax.all_to_all(k_slots, "swap", split_axis=1, concat_axis=0, tiled=True),
        lax.all_to_all(v_slots, "swap", split_axis=1, concat_axis=0, tiled=True),
    )
    rim_k, rim_v = passed_along((k_block, v_block), "blk", 1)
    rim_len = rim_k.shape[0]
    k_all = jnp.concatenate([rim_k, k_block], 0)
    v_all = jnp.concatenate([rim_v, v_block], 0)
    block_start = lax.axis_index("blk") * seq_blk
    doc_padded = jnp.concatenate([jnp.full((MOST,), -1, jnp.int32), doc_ids], 0)
    tile_rows = min(512, seq_blk)
    key_width = MOST + tile_rows
    tile_count = seq_blk // tile_rows
    q_place = jnp.arange(tile_rows, dtype=jnp.int32)
    k_place = jnp.arange(key_width, dtype=jnp.int32) - MOST

    def tile_step(step_index, running):
        dq_acc, dk_acc, dv_acc = running
        tile_start = step_index * tile_rows
        key_start = rim_len + tile_start - MOST
        q_tile = lax.dynamic_slice_in_dim(q_heads, tile_start, tile_rows, 0).reshape(
            tile_rows, heads_here, HEAD_DIM
        )
        g_tile = lax.dynamic_slice_in_dim(g_heads, tile_start, tile_rows, 0).reshape(
            tile_rows, heads_here, HEAD_DIM
        )
        k_tile = lax.dynamic_slice_in_dim(k_all, key_start, key_width, 0)
        v_tile = lax.dynamic_slice_in_dim(v_all, key_start, key_width, 0)
        q_docs = lax.dynamic_slice_in_dim(doc_ids, block_start + tile_start, tile_rows, 0)
        k_docs = lax.dynamic_slice_in_dim(doc_padded, block_start + tile_start, key_width, 0)
        allowed = (k_place[None, :] <= q_place[:, None]) & (k_docs[None, :] == q_docs[:, None])
        scores = (
            jnp.einsum("qhd,kd->hqk", q_tile, k_tile, preferred_element_type=jnp.float32) * inv_root
        )
        scores = jnp.where(allowed, scores, masked_value)
        row_max = jnp.max(scores, axis=-1, keepdims=True)
        raised = jnp.exp(scores - row_max)
        weights = raised / jnp.sum(raised, axis=-1, keepdims=True)
        weights_b = weights.astype(jnp.bfloat16)
        attended = jnp.einsum("hqk,kd->qhd", weights_b, v_tile, preferred_element_type=jnp.float32)
        row_dot = jnp.sum(g_tile.astype(jnp.float32) * attended, axis=-1)
        dweights = jnp.einsum("qhd,kd->hqk", g_tile, v_tile, preferred_element_type=jnp.float32)
        d_scores = (weights * (dweights - jnp.transpose(row_dot)[:, :, None])).astype(jnp.bfloat16)
        dq_tile = (
            jnp.einsum("hqk,kd->qhd", d_scores, k_tile, preferred_element_type=jnp.float32)
            * inv_root
        )
        dq_tile = dq_tile.astype(jnp.bfloat16).reshape(tile_rows, heads_here * HEAD_DIM)
        dk_tile = (
            jnp.einsum("hqk,qhd->kd", d_scores, q_tile, preferred_element_type=jnp.float32)
            * inv_root
        )
        dv_tile = jnp.einsum("hqk,qhd->kd", weights_b, g_tile, preferred_element_type=jnp.float32)
        dq_acc = lax.dynamic_update_slice_in_dim(dq_acc, dq_tile, tile_start, 0)
        dk_acc = lax.dynamic_update_slice_in_dim(
            dk_acc,
            lax.dynamic_slice_in_dim(dk_acc, key_start, key_width, 0) + dk_tile,
            key_start,
            0,
        )
        dv_acc = lax.dynamic_update_slice_in_dim(
            dv_acc,
            lax.dynamic_slice_in_dim(dv_acc, key_start, key_width, 0) + dv_tile,
            key_start,
            0,
        )
        return (dq_acc, dk_acc, dv_acc)

    dq_start = jnp.zeros((seq_blk, heads_here * HEAD_DIM), jnp.bfloat16)
    kv_start = jnp.zeros((rim_len + seq_blk, HEAD_DIM), jnp.float32)
    dq_heads, dk_acc, dv_acc = lax.fori_loop(
        0, tile_count, tile_step, (dq_start, kv_start, kv_start)
    )
    back_k, back_v = passed_along((dk_acc[:rim_len], dv_acc[:rim_len]), "blk", -1)
    offset = seq_blk - rim_len
    own_k = dk_acc[rim_len:].at[offset:].add(back_k)
    own_v = dv_acc[rim_len:].at[offset:].add(back_v)
    grad_queries = lax.all_to_all(dq_heads, "swap", split_axis=0, concat_axis=1, tiled=True)
    k_home, v_home = (
        lax.all_to_all(own_k, "swap", split_axis=0, concat_axis=1, tiled=True),
        lax.all_to_all(own_v, "swap", split_axis=0, concat_axis=1, tiled=True),
    )
    grad_keys = (
        k_home.reshape(tok_rows, kv_total, repeats, HEAD_DIM)
        .sum(axis=2)
        .reshape(tok_rows, kv_total * HEAD_DIM)
        .astype(jnp.bfloat16)
    )
    grad_values = (
        v_home.reshape(tok_rows, kv_total, repeats, HEAD_DIM)
        .sum(axis=2)
        .reshape(tok_rows, kv_total * HEAD_DIM)
        .astype(jnp.bfloat16)
    )
    return (grad_queries, grad_keys, grad_values)


def solution(mesh):
    return jax.shard_map(
        body,
        mesh=mesh,
        in_specs=(
            P(("blk", "swap"), None),
            P(("blk", "swap"), None),
            P(("blk", "swap"), None),
            P(("blk", "swap"), None),
            P(),
        ),
        out_specs=(P(("blk", "swap"), None), P(("blk", "swap"), None), P(("blk", "swap"), None)),
        check_vma=False,
    )
```

profile of v0, /device:TPU:1, one launch (start us, length us, event | category | flops | bytes accessed | tf_op | source)
XLA Modules:
  0.0 242.1 jit_solution(3763470644782248310)
XLA Ops:
  2.3 6.4 %all-to-all-start = ((bf16[128,8,128]{2,0,1:T(8,128)(2,1)}), bf16[128,8,128]{2,0,1:T(8,128)(2,1)S(1)}, u32[]{:S(2)}, u32[]{:S(2)}) async-start(bf16[128,8,128]{2,0,1:T(8,128)(2,1)} %bitcast), calls=%async_computation | async-start | bytes 524288 | tf_op jit(solution)/shard_map/all_to_all | solution.py:39
  9.6 6.4 %all-to-all-done = bf16[128,8,128]{2,0,1:T(8,128)(2,1)S(1)} async-done(((bf16[128,8,128]{2,0,1:T(8,128)(2,1)}), bf16[128,8,128]{2,0,1:T(8,128)(2,1)S(1)}, u32[]{:S(2)}, u32[]{:S(2)}) %all-to-all-start) | async-done | bytes 262176 | tf_op jit(solution)/shard_map/all_to_all | solution.py:39
  16.8 4.8 %all-to-all-start.2 = ((bf16[128,8,128]{2,0,1:T(8,128)(2,1)}), bf16[128,8,128]{2,0,1:T(8,128)(2,1)S(1)}, u32[]{:S(2)}, u32[]{:S(2)}) async-start(bf16[128,8,128]{2,0,1:T(8,128)(2,1)} %bitcast.6), calls=%async_computation.2 | async-start | bytes 524288 | tf_op jit(solution)/shard_map/all_to_all | solution.py:40
  21.6 2.3 copy.53
  23.8 4.9 %all-to-all-done.2 = bf16[128,8,128]{2,0,1:T(8,128)(2,1)S(1)} async-done(((bf16[128,8,128]{2,0,1:T(8,128)(2,1)}), bf16[128,8,128]{2,0,1:T(8,128)(2,1)S(1)}, u32[]{:S(2)}, u32[]{:S(2)}) %all-to-all-start.2) | async-done | bytes 262176 | tf_op jit(solution)/shard_map/all_to_all | solution.py:40
  28.8 4.8 %all-to-all-start.1 = ((bf16[128,8,512]{0,2,1:T(8,128)(2,1)}), bf16[128,8,512]{0,2,1:T(8,128)(2,1)S(1)}, u32[]{:S(2)}, u32[]{:S(2)}) async-start(bf16[128,8,512]{0,2,1:T(8,128)(2,1)} %bitcast.3), calls=%async_computation.1 | async-start | bytes 2097152 | tf_op jit(solution)/shard_map/all_to_all | solution.py:37
  33.6 2.3 copy.56
  35.9 22.3 %all-to-all-done.1 = bf16[128,8,512]{0,2,1:T(8,128)(2,1)S(1)} async-done(((bf16[128,8,512]{0,2,1:T(8,128)(2,1)}), bf16[128,8,512]{0,2,1:T(8,128)(2,1)S(1)}, u32[]{:S(2)}, u32[]{:S(2)}) %all-to-all-start.1) | async-done | bytes 1048608 | tf_op jit(solution)/shard_map/all_to_all | solution.py:37
  58.1 5.0 %all-to-all-start.3 = ((bf16[128,8,512]{0,2,1:T(8,128)(2,1)}), bf16[128,8,512]{0,2,1:T(8,128)(2,1)}, u32[]{:S(2)}, u32[]{:S(2)}) async-start(bf16[128,8,512]{0,2,1:T(8,128)(2,1)} %bitcast.9), calls=%async_computation.3 | async-start | bytes 2097152 | tf_op jit(solution)/shard_map/all_to_all | solution.py:38
  63.1 4.7 %collective-permute-start.1 = (bf16[1024,128]{1,0:T(8,128)(2,1)S(1)}, bf16[1024,128]{1,0:T(8,128)(2,1)S(1)}, u32[]{:S(2)}, u32[]{:S(2)}) collective-permute-start(bf16[1024,128]{1,0:T(8,128)(2,1)S(1)} %bitcast.160), channel_id=1, source_target_pairs={{0,1},{1,2},{2,3},{4,5},{5,6},{6,7},{8,9},{9,10},{10,11},{12,13},{... | collective-permute-start | bytes 786440 | tf_op jit(solution)/shard_map/ppermute | solution.py:18
  67.8 1.9 collective-permute-start
  71.9 2.0 collective-permute-done
  73.9 1.4 copy.54
  75.3 12.4 %all-to-all-done.3 = bf16[128,8,512]{0,2,1:T(8,128)(2,1)} async-done(((bf16[128,8,512]{0,2,1:T(8,128)(2,1)}), bf16[128,8,512]{0,2,1:T(8,128)(2,1)}, u32[]{:S(2)}, u32[]{:S(2)}) %all-to-all-start.3) | async-done | bytes 1048608 | tf_op jit(solution)/shard_map/all_to_all | solution.py:38
  87.7 2.3 copy.57
  92.0 1.1 broadcast_in_dim.63
  93.1 75.9 %while.26 = (s32[]{:T(128)}, bf16[1024,512]{1,0:T(8,128)(2,1)}, f32[2048,128]{1,0:T(8,128)}, f32[2048,128]{1,0:T(8,128)}, bf16[2048,128]{1,0:T(8,128)(2,1)S(1)},...) while((s32[]{:T(128)}, bf16[1024,512]{1,0:T(8,128)(2,1)}, ...), condition=%wide.region_4.5_spmd.clone, body=%wide.region_0.4_spmd.clone.sunk | while | flops 4873847808 | bytes 137441872 | solution.py:108
  93.9 1.2 fusion.81
  95.2 1.3 constant_dynamic-slice_fusion.3
  97.7 1.8 fusion.80
  99.4 8.9 %fusion.82 = (f32[4,512]{1,0:T(4,128)S(1)}, f32[4,512,1536]{1,2,0:T(8,128)}) fusion(f32[1536,512,4]{1,0,2:T(8,128)S(1)} %fusion.80, pred[512,1536]{0,1:T(8,128)(4,1)S(1)} %fusion.81), kind=kOutput, calls=%fused_computation.55.clone.1 | output fusion | flops 18875904 | bytes 25960448 | tf_op jit(solution)/shard_map/while/body/eval_jaxpr/sub | solution.py:74
  108.3 6.4 %fusion.83 = bf16[4,512,1536]{1,2,0:T(8,128)(2,1)S(1)} fusion(f32[4,512,1536]{1,2,0:T(8,128)} %get-tuple-element.588, f32[4,512]{1,0:T(4,128)S(1)} %get-tuple-element.589), kind=kLoop, calls=%fused_computation.13.clone.1 | loop fusion | flops 6291456 | bytes 18882560 | tf_op jit(solution)/shard_map/while/body/eval_jaxpr/convert_element_type | solution.py:76
  114.8 2.3 fusion.84
  117.1 4.0 %fusion.88 = f32[2048,128]{1,0:T(8,128)} fusion(f32[2048,128]{1,0:T(8,128)} %get-tuple-element.611, s32[]{:T(128)S(6)} %select_n.95, bf16[4,512,1536]{1,2,0:T(8,128)(2,1)S(1)} %fusion.83, bf16[512,4,128]{0,2,1:T(8,128)(2,1)} %bitcast.148), kind=kOutput, calls=%fused_computation.22.clone.1 | convolution fusion | flops 805502976 | bytes 8388612 | tf_op jit(solution)/shard_map/while/body/eval_jaxpr/hqk,qhd->kd/dot_general | solution.py:90
  121.1 5.9 %fusion.85 = bf16[4,512,1536]{1,2,0:T(8,128)(2,1)S(1)} fusion(bf16[512,4,128]{0,2,1:T(8,128)(2,1)S(1)} %bitcast.149, f32[4,512]{1,0:T(4,128)S(1)} %bitcast.164, f32[4,512,1536]{1,2,0:T(8,128)} %get-tuple-element.588, f32[4,512]{1,0:T(4,128)S(1)} %get-tuple-element.589, bf16[2048,128]{1,0:T(8,128)(2,1)S(1)} %copy-done.8, s32[]{:T(128)S(6)} %select_n.95), kind=kOutput, calls=%fused_computation.5.clone.1 | convolution fusion | flops 817889280 | bytes 19808260 | tf_op jit(solution)/shard_map/while/body/eval_jaxpr/qhd,kd->hqk/dot_general | solution.py:79
  127.0 1.9 fusion.87
  131.9 1.2 fusion.81
  133.1 1.3 constant_dynamic-slice_fusion.3
  135.6 1.8 fusion.80
  137.4 8.9 %fusion.82 = (f32[4,512]{1,0:T(4,128)S(1)}, f32[4,512,1536]{1,2,0:T(8,128)}) fusion(f32[1536,512,4]{1,0,2:T(8,128)S(1)} %fusion.80, pred[512,1536]{0,1:T(8,128)(4,1)S(1)} %fusion.81), kind=kOutput, calls=%fused_computation.55.clone.1 | output fusion | flops 18875904 | bytes 25960448 | tf_op jit(solution)/shard_map/while/body/eval_jaxpr/sub | solution.py:74
  146.3 6.4 %fusion.83 = bf16[4,512,1536]{1,2,0:T(8,128)(2,1)S(1)} fusion(f32[4,512,1536]{1,2,0:T(8,128)} %get-tuple-element.588, f32[4,512]{1,0:T(4,128)S(1)} %get-tuple-element.589), kind=kLoop, calls=%fused_computation.13.clone.1 | loop fusion | flops 6291456 | bytes 18882560 | tf_op jit(solution)/shard_map/while/body/eval_jaxpr/convert_element_type | solution.py:76
  152.7 2.3 fusion.84
  155.0 4.0 %fusion.88 = f32[2048,128]{1,0:T(8,128)} fusion(f32[2048,128]{1,0:T(8,128)} %get-tuple-element.611, s32[]{:T(128)S(6)} %select_n.95, bf16[4,512,1536]{1,2,0:T(8,128)(2,1)S(1)} %fusion.83, bf16[512,4,128]{0,2,1:T(8,128)(2,1)} %bitcast.148), kind=kOutput, calls=%fused_computation.22.clone.1 | convolution fusion | flops 805502976 | bytes 8388612 | tf_op jit(solution)/shard_map/while/body/eval_jaxpr/hqk,qhd->kd/dot_general | solution.py:90
  159.1 5.9 %fusion.85 = bf16[4,512,1536]{1,2,0:T(8,128)(2,1)S(1)} fusion(bf16[512,4,128]{0,2,1:T(8,128)(2,1)S(1)} %bitcast.149, f32[4,512]{1,0:T(4,128)S(1)} %bitcast.164, f32[4,512,1536]{1,2,0:T(8,128)} %get-tuple-element.588, f32[4,512]{1,0:T(4,128)S(1)} %get-tuple-element.589, bf16[2048,128]{1,0:T(8,128)(2,1)S(1)} %copy-done.8, s32[]{:T(128)S(6)} %select_n.95), kind=kOutput, calls=%fused_computation.5.clone.1 | convolution fusion | flops 817889280 | bytes 19808260 | tf_op jit(solution)/shard_map/while/body/eval_jaxpr/qhd,kd->hqk/dot_general | solution.py:79
  165.0 1.9 fusion.87
  169.0 1.1 slice.41
  170.0 4.4 %collective-permute-start.2 = (f32[1024,128]{1,0:T(8,128)S(1)}, f32[1024,128]{1,0:T(8,128)S(1)}, u32[]{:S(2)}, u32[]{:S(2)}) collective-permute-start(f32[1024,128]{1,0:T(8,128)S(1)} %slice.41), channel_id=1, source_target_pairs={{1,0},{2,1},{3,2},{5,4},{6,5},{7,6},{9,8},{10,9},{11,10},{13,12},{... | collective-permute-start | bytes 1572872 | tf_op jit(solution)/shard_map/ppermute | solution.py:18
  174.4 8.0 %collective-permute-done.2 = f32[1024,128]{1,0:T(8,128)S(1)} collective-permute-done((f32[1024,128]{1,0:T(8,128)S(1)}, f32[1024,128]{1,0:T(8,128)S(1)}, u32[]{:S(2)}, u32[]{:S(2)}) %collective-permute-start.2) | collective-permute-done | bytes 524320 | tf_op jit(solution)/shard_map/ppermute | solution.py:18
  182.4 1.9 slice_add_fusion.1
  184.3 3.5 %all-to-all-start.5 = ((f32[8,128,128]{2,1,0:T(8,128)}), f32[8,128,128]{2,1,0:T(8,128)S(1)}, u32[]{:S(2)}, u32[]{:S(2)}) async-start(f32[8,128,128]{2,1,0:T(8,128)} %bitcast.15), calls=%async_computation.5 | async-start | bytes 1048576 | tf_op jit(solution)/shard_map/all_to_all | solution.py:117
  187.8 1.1 slice.43
  188.9 1.9 collective-permute-start.3
  190.8 8.6 %collective-permute-done.3 = f32[1024,128]{1,0:T(8,128)S(1)} collective-permute-done((f32[1024,128]{1,0:T(8,128)S(1)}, f32[1024,128]{1,0:T(8,128)S(1)}, u32[]{:S(2)}, u32[]{:S(2)}) %collective-permute-start.3) | collective-permute-done | bytes 524320 | tf_op jit(solution)/shard_map/ppermute | solution.py:18
  199.4 1.1 slice_add_fusion
  200.5 14.4 %all_to_all.127 = f32[8,128,128]{2,1,0:T(8,128)S(1)} all-to-all(f32[8,128,128]{2,1,0:T(8,128)S(1)} %bitcast.157), channel_id=1, replica_groups=mesh['swap'=8,'blk'=4] {'swap'}, dimensions={0} | all-to-all | bytes 1048576 | tf_op jit(solution)/shard_map/all_to_all | solution.py:118
  214.9 3.6 %all-to-all-start.4 = ((bf16[8,128,512]{2,1,0:T(8,128)(2,1)}), bf16[8,128,512]{2,1,0:T(8,128)(2,1)S(1)}, u32[]{:S(2)}, u32[]{:S(2)}) async-start(bf16[8,128,512]{2,1,0:T(8,128)(2,1)} %bitcast.155), calls=%async_computation.4 | async-start | bytes 2097152 | tf_op jit(solution)/shard_map/all_to_all | solution.py:115
  220.3 19.8 %all-to-all-done.4 = bf16[8,128,512]{2,1,0:T(8,128)(2,1)S(1)} async-done(((bf16[8,128,512]{2,1,0:T(8,128)(2,1)}), bf16[8,128,512]{2,1,0:T(8,128)(2,1)S(1)}, u32[]{:S(2)}, u32[]{:S(2)}) %all-to-all-start.4) | async-done | bytes 1048608 | tf_op jit(solution)/shard_map/all_to_all | solution.py:115
  240.8 1.3 copy.64
  (68 shorter events, 18.5 us)
Async XLA Ops:
  0.6 0.9 copy-start
  2.3 13.7 %all-to-all-start = ((bf16[128,8,128]{2,0,1:T(8,128)(2,1)}), bf16[128,8,128]{2,0,1:T(8,128)(2,1)S(1)}, u32[]{:S(2)}, u32[]{:S(2)}) async-start(bf16[128,8,128]{2,0,1:T(8,128)(2,1)} %bitcast), calls=%async_computation | async-start | bytes 524288 | tf_op jit(solution)/shard_map/all_to_all | solution.py:39
  16.8 12.0 %all-to-all-start.2 = ((bf16[128,8,128]{2,0,1:T(8,128)(2,1)}), bf16[128,8,128]{2,0,1:T(8,128)(2,1)S(1)}, u32[]{:S(2)}, u32[]{:S(2)}) async-start(bf16[128,8,128]{2,0,1:T(8,128)(2,1)} %bitcast.6), calls=%async_computation.2 | async-start | bytes 524288 | tf_op jit(solution)/shard_map/all_to_all | solution.py:40
  28.8 29.4 %all-to-all-start.1 = ((bf16[128,8,512]{0,2,1:T(8,128)(2,1)}), bf16[128,8,512]{0,2,1:T(8,128)(2,1)S(1)}, u32[]{:S(2)}, u32[]{:S(2)}) async-start(bf16[128,8,512]{0,2,1:T(8,128)(2,1)} %bitcast.3), calls=%async_computation.1 | async-start | bytes 2097152 | tf_op jit(solution)/shard_map/all_to_all | solution.py:37
  58.1 29.5 %all-to-all-start.3 = ((bf16[128,8,512]{0,2,1:T(8,128)(2,1)}), bf16[128,8,512]{0,2,1:T(8,128)(2,1)}, u32[]{:S(2)}, u32[]{:S(2)}) async-start(bf16[128,8,512]{0,2,1:T(8,128)(2,1)} %bitcast.9), calls=%async_computation.3 | async-start | bytes 2097152 | tf_op jit(solution)/shard_map/all_to_all | solution.py:38
  63.1 8.0 %collective-permute-start.1 = (bf16[1024,128]{1,0:T(8,128)(2,1)S(1)}, bf16[1024,128]{1,0:T(8,128)(2,1)S(1)}, u32[]{:S(2)}, u32[]{:S(2)}) collective-permute-start(bf16[1024,128]{1,0:T(8,128)(2,1)S(1)} %bitcast.160), channel_id=1, source_target_pairs={{0,1},{1,2},{2,3},{4,5},{5,6},{6,7},{8,9},{9,10},{10,11},{12,13},{... | collective-permute-start | bytes 786440 | tf_op jit(solution)/shard_map/ppermute | solution.py:18
  67.8 6.1 %collective-permute-start = (bf16[1024,128]{1,0:T(8,128)(2,1)S(1)}, bf16[1024,128]{1,0:T(8,128)(2,1)S(1)}, u32[]{:S(2)}, u32[]{:S(2)}) collective-permute-start(bf16[1024,128]{1,0:T(8,128)(2,1)S(1)} %bitcast.158), channel_id=1, source_target_pairs={{0,1},{1,2},{2,3},{4,5},{5,6},{6,7},{8,9},{9,10},{10,11},{12,13},{... | collective-permute-start | bytes 786440 | tf_op jit(solution)/shard_map/ppermute | solution.py:18
  93.1 15.3 %copy-start.4 = (bf16[2048,128]{1,0:T(8,128)(2,1)}, bf16[2048,128]{1,0:T(8,128)(2,1)S(1)}, u32[]{:S(2)}) copy-start(bf16[2048,128]{1,0:T(8,128)(2,1)S(1)} %get-tuple-element.630) | copy-start | bytes 1572868 | tf_op jit(solution)/shard_map/while
  97.7 10.7 %copy-start.2 = (bf16[512,512]{0,1:T(8,128)(2,1)}, bf16[512,512]{0,1:T(8,128)(2,1)S(1)}, u32[]{:S(2)}) copy-start(bf16[512,512]{0,1:T(8,128)(2,1)S(1)} %copy.89) | copy-start | bytes 1572868 | tf_op jit(solution)/shard_map/while
  114.8 6.3 %copy-start.1 = (bf16[512,512]{0,1:T(8,128)(2,1)S(1)}, bf16[512,512]{0,1:T(8,128)(2,1)}, u32[]{:S(2)}) copy-start(bf16[512,512]{0,1:T(8,128)(2,1)} %copy.88) | copy-start | bytes 1572868 | tf_op jit(solution)/shard_map/while
  114.8 6.3 %copy-start.8 = (bf16[2048,128]{1,0:T(8,128)(2,1)S(1)}, bf16[2048,128]{1,0:T(8,128)(2,1)}, u32[]{:S(2)}) copy-start(bf16[2048,128]{1,0:T(8,128)(2,1)} %get-tuple-element.635) | copy-start | bytes 1572868 | tf_op jit(solution)/shard_map/while
  121.1 5.9 %copy-start.3 = (bf16[512,512]{0,1:T(8,128)(2,1)S(1)}, bf16[512,512]{0,1:T(8,128)(2,1)}, u32[]{:S(2)}) copy-start(bf16[512,512]{0,1:T(8,128)(2,1)} %copy-done.2) | copy-start | bytes 1572868 | tf_op jit(solution)/shard_map/while
  121.1 5.9 %copy-start.6 = (f32[2048,128]{1,0:T(8,128)S(1)}, f32[2048,128]{1,0:T(8,128)}, u32[]{:S(2)}) copy-start(f32[2048,128]{1,0:T(8,128)} %get-tuple-element.610) | copy-start | bytes 3145732 | tf_op jit(solution)/shard_map/while
  121.1 7.8 %copy-start.5 = (bf16[2048,128]{1,0:T(8,128)(2,1)S(1)}, bf16[2048,128]{1,0:T(8,128)(2,1)}, u32[]{:S(2)}) copy-start(bf16[2048,128]{1,0:T(8,128)(2,1)} %copy-done.4) | copy-start | bytes 1572868 | tf_op jit(solution)/shard_map/while
  128.9 1.1 copy-start.7
  131.0 15.3 %copy-start.4 = (bf16[2048,128]{1,0:T(8,128)(2,1)}, bf16[2048,128]{1,0:T(8,128)(2,1)S(1)}, u32[]{:S(2)}) copy-start(bf16[2048,128]{1,0:T(8,128)(2,1)S(1)} %get-tuple-element.630) | copy-start | bytes 1572868 | tf_op jit(solution)/shard_map/while
  135.6 10.7 %copy-start.2 = (bf16[512,512]{0,1:T(8,128)(2,1)}, bf16[512,512]{0,1:T(8,128)(2,1)S(1)}, u32[]{:S(2)}) copy-start(bf16[512,512]{0,1:T(8,128)(2,1)S(1)} %copy.89) | copy-start | bytes 1572868 | tf_op jit(solution)/shard_map/while
  152.7 6.3 %copy-start.1 = (bf16[512,512]{0,1:T(8,128)(2,1)S(1)}, bf16[512,512]{0,1:T(8,128)(2,1)}, u32[]{:S(2)}) copy-start(bf16[512,512]{0,1:T(8,128)(2,1)} %copy.88) | copy-start | bytes 1572868 | tf_op jit(solution)/shard_map/while
  152.7 6.3 %copy-start.8 = (bf16[2048,128]{1,0:T(8,128)(2,1)S(1)}, bf16[2048,128]{1,0:T(8,128)(2,1)}, u32[]{:S(2)}) copy-start(bf16[2048,128]{1,0:T(8,128)(2,1)} %get-tuple-element.635) | copy-start | bytes 1572868 | tf_op jit(solution)/shard_map/while
  159.0 5.9 %copy-start.3 = (bf16[512,512]{0,1:T(8,128)(2,1)S(1)}, bf16[512,512]{0,1:T(8,128)(2,1)}, u32[]{:S(2)}) copy-start(bf16[512,512]{0,1:T(8,128)(2,1)} %copy-done.2) | copy-start | bytes 1572868 | tf_op jit(solution)/shard_map/while
  159.0 5.9 %copy-start.6 = (f32[2048,128]{1,0:T(8,128)S(1)}, f32[2048,128]{1,0:T(8,128)}, u32[]{:S(2)}) copy-start(f32[2048,128]{1,0:T(8,128)} %get-tuple-element.610) | copy-start | bytes 3145732 | tf_op jit(solution)/shard_map/while
  159.0 7.8 %copy-start.5 = (bf16[2048,128]{1,0:T(8,128)(2,1)S(1)}, bf16[2048,128]{1,0:T(8,128)(2,1)}, u32[]{:S(2)}) copy-start(bf16[2048,128]{1,0:T(8,128)(2,1)} %copy-done.4) | copy-start | bytes 1572868 | tf_op jit(solution)/shard_map/while
  166.8 1.1 copy-start.7
  170.0 12.4 %collective-permute-start.2 = (f32[1024,128]{1,0:T(8,128)S(1)}, f32[1024,128]{1,0:T(8,128)S(1)}, u32[]{:S(2)}, u32[]{:S(2)}) collective-permute-start(f32[1024,128]{1,0:T(8,128)S(1)} %slice.41), channel_id=1, source_target_pairs={{1,0},{2,1},{3,2},{5,4},{6,5},{7,6},{9,8},{10,9},{11,10},{13,12},{... | collective-permute-start | bytes 1572872 | tf_op jit(solution)/shard_map/ppermute | solution.py:18
  184.3 16.2 %all-to-all-start.5 = ((f32[8,128,128]{2,1,0:T(8,128)}), f32[8,128,128]{2,1,0:T(8,128)S(1)}, u32[]{:S(2)}, u32[]{:S(2)}) async-start(f32[8,128,128]{2,1,0:T(8,128)} %bitcast.15), calls=%async_computation.5 | async-start | bytes 1048576 | tf_op jit(solution)/shard_map/all_to_all | solution.py:117
  188.9 10.5 %collective-permute-start.3 = (f32[1024,128]{1,0:T(8,128)S(1)}, f32[1024,128]{1,0:T(8,128)S(1)}, u32[]{:S(2)}, u32[]{:S(2)}) collective-permute-start(f32[1024,128]{1,0:T(8,128)S(1)} %slice.43), channel_id=1, source_target_pairs={{1,0},{2,1},{3,2},{5,4},{6,5},{7,6},{9,8},{10,9},{11,10},{13,12},{... | collective-permute-start | bytes 1572872 | tf_op jit(solution)/shard_map/ppermute | solution.py:18
  214.9 25.3 %all-to-all-start.4 = ((bf16[8,128,512]{2,1,0:T(8,128)(2,1)}), bf16[8,128,512]{2,1,0:T(8,128)(2,1)S(1)}, u32[]{:S(2)}, u32[]{:S(2)}) async-start(bf16[8,128,512]{2,1,0:T(8,128)(2,1)} %bitcast.155), calls=%async_computation.4 | async-start | bytes 2097152 | tf_op jit(solution)/shard_map/all_to_all | solution.py:115
where the time goes:
time: 243 us; the launch traced here: 242 us
  waiting for transfers between devices  85 us (35%)
  starting transfers between devices  41 us (17%)
  other arithmetic  37 us (15%)
  matrix products  33.7 us (14%)
  local copies, waits for them, and re-layouts  30.1 us (12%)
  blocking collectives  14.4 us (6%)
    all_to_all x1, waiting for transfers between devices, body(): lax.all_to_all(queries, 'swap', split_axis=1, concat_axis=0, tiled=True)  22.3 us
    all_to_all x1, waiting for transfers between devices, body(): lax.all_to_all(dq_heads, 'swap', split_axis=0, concat_axis=1, tiled=True)  19.8 us
    ppermute x4, waiting for transfers between devices, passed_along(): return lax.ppermute(block, axis, route)  19.1 us
    sub x2, other arithmetic, tile_step(): raised = jnp.exp(scores - row_max)  17.8 us
    all_to_all x1, blocking collectives, body(): lax.all_to_all(own_v, 'swap', split_axis=0, concat_axis=1, tiled=True)  14.4 us
    ppermute x4, starting transfers between devices, passed_along(): return lax.ppermute(block, axis, route)  12.9 us
    convert_element_type x2, other arithmetic, tile_step(): weights_b = weights.astype(jnp.bfloat16)  12.8 us
    all_to_all x1, waiting for transfers between devices, body(): lax.all_to_all(grad_out, 'swap', split_axis=1, concat_axis=0, tiled=True)  12.4 us
  transfers between devices with their start and end apart: 10, of which 9 were waited for; matrix products, arithmetic and copies ran while one was open for 5% of the time, Pallas kernels for 0%

commit v1 on v0

v1 whole, which is shorter than its diff:
```python
import functools
import math

import jax
import jax.numpy as jnp
from jax import lax
from jax.experimental import pallas as pl
from jax.experimental.pallas import tpu as pltpu
from jax.sharding import PartitionSpec as P

HEAD_DIM = 128
MOST = 1024
BF16 = jnp.bfloat16
F32 = jnp.float32
LOG2E = 1.4426950408889634
MIB = 1024 * 1024

NN = (((1,), (0,)), ((), ()))
NT = (((1,), (1,)), ((), ()))
TN = (((0,), (0,)), ((), ()))


def dot(a, b, dims):
    return lax.dot_general(a, b, dims, preferred_element_type=F32)


def vmem_call(kernel, out_shapes, args, scratch=(), hbm=(), smem=(), after=(), through=(), mib=8, flops=0, name=None):
    def space(i):
        return pltpu.SMEM if i in smem else pl.ANY if i in hbm else pltpu.VMEM

    specs = [pl.BlockSpec(memory_space=space(i)) for i in range(len(args))]
    specs += [pl.BlockSpec(memory_space=pl.ANY)] * (len(after) + len(through))
    outs = [pl.BlockSpec(memory_space=pltpu.VMEM)] * len(out_shapes)
    outs += [pl.BlockSpec(memory_space=pl.ANY)] * len(through)
    n_args, n_out = len(args), len(out_shapes)
    n_in, n_made = len(specs), len(outs)

    def run(*refs):
        kernel(*refs[:n_args], *refs[n_in : n_in + n_out], *refs[n_in + n_made :])

    return pl.pallas_call(
        run,
        out_shape=list(out_shapes) + [jax.ShapeDtypeStruct(t.shape, t.dtype) for t in through],
        in_specs=specs,
        out_specs=outs,
        input_output_aliases={n_args + len(after) + i: n_out + i for i in range(len(through))},
        scratch_shapes=list(scratch),
        compiler_params=pltpu.CompilerParams(vmem_limit_bytes=mib * MIB),
        cost_estimate=pl.CostEstimate(flops=flops, bytes_accessed=0, transcendentals=0),
        name=name,
    )(*args, *after, *through)


def place():
    blk, swap = lax.axis_index("blk"), lax.axis_index("swap")
    return lax.rem(blk, 2), lax.rem(swap, 2), lax.div(swap, 2)


def quarters():
    core, y, _ = place()
    return [2 * core + y, 2 * (1 - core) + y, 2 * core + 1 - y, 2 * (1 - core) + 1 - y]


def split_kernel(a_ref, b_ref, *rest):
    outs, sems = rest[:-1], rest[-1]
    width = a_ref.shape[1] // 4
    copies = []
    for quarter, out in zip(quarters(), outs):
        columns = pl.ds(pl.multiple_of(quarter * width, 128), width)
        for src, place_out in ((a_ref, slice(0, width)), (b_ref, slice(width, 2 * width))):
            copies.append(
                pltpu.make_async_copy(src.at[:, columns], out.at[:, place_out], sems.at[len(copies)])
            )
    for copy in copies:
        copy.start()
    for copy in copies:
        copy.wait()


def select_chunks(blocks, own, by_core, by_y, by_diag):
    core, y, _ = place()
    rows = own.shape[0]
    here = pl.ds(pl.multiple_of(y * rows, rows), rows)
    there = pl.ds(pl.multiple_of((1 - y) * rows, rows), rows)
    for c in (0, 1):

        @pl.when(core == c)
        def _(c=c):
            blocks[c][here, :] = own[...]
            blocks[c][there, :] = by_y[...]
            blocks[1 - c][here, :] = by_core[...]
            blocks[1 - c][there, :] = by_diag[...]


def fill_payloads(n_out, up, down, outs):
    _, _, z = place()
    for k, out in enumerate(outs, 1):

        @pl.when(z + k < n_out)
        def _(out=out):
            out[...] = up[...]

        @pl.when(z + k >= n_out)
        def _(out=out):
            out[...] = down[...]


def first_payload_kernel(n_out, own, by_core, by_y, by_diag, even, odd, *outs):
    select_chunks((even, odd), own, by_core, by_y, by_diag)
    fill_payloads(n_out, odd, even, outs)


def second_payload_kernel(n_out, even, rim, *outs):
    fill_payloads(n_out, even, rim, outs)


def attend_kernel(odd, second, n_slots, seq_blk, own, by_core, by_y, by_diag, starts, doc_scalars, *rest):
    slots, rest = rest[:n_slots], rest[n_slots:]
    if second:
        dq_first, dq_outs, rest = rest[0], rest[1:5], rest[5:]
        rest, dq_out = rest[:-1], rest[-1]
    else:
        dq_out, rest = rest[0], rest[1:]
    sums, rest = rest[:n_slots], rest[n_slots:]
    q_rows, g_rows, q_cols, g_cols, kv, scores, dweights, dq_cols, acc = rest
    core, y, z = place()
    tok = own.shape[0]
    width = own.shape[1] // 2
    heads = width // HEAD_DIM
    pair = 2 * tok
    window = (n_slots - 1) * pair
    inv_root = 1.0 / math.sqrt(HEAD_DIM)
    scale = inv_root * LOG2E
    block = 2 * lax.div(lax.axis_index("blk"), 2) + odd
    pair_start = block * seq_blk + z * pair

    def stack(unit, src):
        for h in range(heads):
            rows = slice(h * tok, (h + 1) * tok)
            cols = slice(h * HEAD_DIM, (h + 1) * HEAD_DIM)
            q_rows[unit, rows, :] = src[:, cols]
            g_rows[unit, rows, :] = src[:, width + h * HEAD_DIM : width + (h + 1) * HEAD_DIM]

    @pl.when(core == odd)
    def _():
        stack(y, own)
        stack(1 - y, by_y)

    @pl.when(core != odd)
    def _():
        stack(y, by_core)
        stack(1 - y, by_diag)

    for i, slot in enumerate(slots):
        kv[i * pair : (i + 1) * pair, :] = slot[...]
    acc[...] = jnp.zeros_like(acc)

    for unit in (0, 1):
        first = pair_start + unit * tok
        base = first - window
        lo = starts[pl.ds(lax.div(first, 128), 1), :]
        t = lax.broadcasted_iota(jnp.int32, (1, tok), 1)
        key_place = lax.broadcasted_iota(jnp.int32, (tok, tok), 0)
        begin = lax.div(doc_scalars[first] - base, tok)
        count = window // tok + 1

        q_cols[...] = q_rows[unit].T
        g_cols[...] = g_rows[unit].T

        def key_rows(j):
            return pl.ds(pl.multiple_of(j * tok + unit * tok, tok), tok)

        def own_rows(j):
            return pl.ds(pl.multiple_of(j * tok, tok), tok)

        def score_step(j, top):
            place_j = key_place + (base + j * tok)
            allowed = (place_j >= lo) & (place_j <= t + first)
            bias = jnp.where(allowed, 0.0, -1e30).astype(F32)
            s = dot(kv[key_rows(j), :HEAD_DIM], q_cols[...], NN)
            s = s + jnp.concatenate([bias] * heads, axis=1)
            scores[own_rows(j), :] = s
            return jnp.maximum(top, jnp.max(s, axis=0, keepdims=True))

        top = lax.fori_loop(begin, count, score_step, jnp.full((1, heads * tok), -3e38, F32))

        def weight_step(j, running):
            total, rowdot = running
            p = jnp.exp2((scores[own_rows(j), :] - top) * scale)
            d = dot(kv[key_rows(j), HEAD_DIM:], g_cols[...], NN)
            scores[own_rows(j), :] = p
            dweights[own_rows(j), :] = d
            return (
                total + jnp.sum(p, axis=0, keepdims=True),
                rowdot + jnp.sum(p * d, axis=0, keepdims=True),
            )

        zero = jnp.zeros((1, heads * tok), F32)
        total, rowdot = lax.fori_loop(begin, count, weight_step, (zero, zero))
        inv_total = 1.0 / total
        rowdot = rowdot * inv_total
        dq_cols[...] = jnp.zeros_like(dq_cols)

        def grad_step(j, carry):
            w = scores[own_rows(j), :] * inv_total
            ds = (w * (dweights[own_rows(j), :] - rowdot)).astype(BF16)
            rows = key_rows(j)
            acc[rows, :HEAD_DIM] += dot(ds, q_rows[unit], NN)
            acc[rows, HEAD_DIM:] += dot(w.astype(BF16), g_rows[unit], NN)
            dq_cols[...] += dot(kv[rows, :HEAD_DIM], ds, TN)
            return carry

        lax.fori_loop(begin, count, grad_step, 0)
        dq = (dq_cols[...] * inv_root).T
        for h in range(heads):
            dq_out[unit * tok : (unit + 1) * tok, h * HEAD_DIM : (h + 1) * HEAD_DIM] = dq[
                h * tok : (h + 1) * tok, :
            ].astype(BF16)

    for i, out in enumerate(sums):
        rows = slice(i * pair, (i + 1) * pair)
        out[:, :HEAD_DIM] = (acc[rows, :HEAD_DIM] * inv_root).astype(out.dtype)
        out[:, HEAD_DIM:] = acc[rows, HEAD_DIM:].astype(out.dtype)

    if second:
        for out, c, yy in zip(dq_outs, (core, 1 - core, core, 1 - core), (y, y, 1 - y, 1 - y)):
            chunk = pl.ds(pl.multiple_of(yy * tok, tok), tok)

            @pl.when(c == odd)
            def _(out=out, chunk=chunk):
                out[...] = dq_out[chunk, :]

            @pl.when(c != odd)
            def _(out=out, chunk=chunk):
                out[...] = dq_first[chunk, :]


def add_terms(n_out, up, down, terms):
    _, _, z = place()
    for k, term in enumerate(terms, 1):
        value = term[...].astype(F32)
        wrapped = (z + k >= n_out).astype(F32)
        up = up + value * (1.0 - wrapped)
        down = down + value * wrapped
    return up, down


def even_sum_kernel(n_out, n_terms, own_up, *refs):
    terms, own_down, up_out, down_out = refs[:n_terms], refs[n_terms:-2], refs[-2], refs[-1]
    down = own_down[0][...] if own_down else jnp.zeros(up_out.shape, F32)
    up, down = add_terms(n_out, own_up[...], down, terms)
    up_out[...] = up
    down_out[...] = down.astype(down_out.dtype)


def home_kernel(n_out, n_terms, odd_up, even_total, rim, *refs):
    terms, refs = refs[:n_terms], refs[n_terms:]
    own_down, outs, total = refs[:-5], refs[-5:-1], refs[-1]
    tok = odd_up.shape[0] // 2
    down = own_down[0][...] if own_down else jnp.zeros(odd_up.shape, F32)
    up, down = add_terms(n_out, odd_up[...], down, terms)
    total[0] = even_total[...] + down
    total[1] = up + rim[...].astype(F32)
    core, y, _ = place()
    for out, c, yy in zip(outs, (core, 1 - core, core, 1 - core), (y, y, 1 - y, 1 - y)):
        out[...] = total[c, pl.ds(pl.multiple_of(yy * tok, tok), tok), :].astype(out.dtype)


def finish_kernel(*refs):
    dq, kv, (q_out, k_out, v_out) = refs[:4], refs[4:8], refs[8:]
    q_width = dq[0].shape[1]
    kv_width = kv[0].shape[1] // 2
    for quarter, dq_part, kv_part in zip(quarters(), dq, kv):
        q_out[:, pl.ds(pl.multiple_of(quarter * q_width, 128), q_width)] = dq_part[...]
        columns = pl.ds(pl.multiple_of(quarter * kv_width, 128), kv_width)
        k_out[:, columns] = kv_part[:, :kv_width].astype(BF16)
        v_out[:, columns] = kv_part[:, kv_width:].astype(BF16)


def body(queries, keys, values, grad_out, doc_ids):
    tok = queries.shape[0]
    n_blk, n_swap = lax.axis_size("blk"), lax.axis_size("swap")
    n_out = n_swap // 2
    seq_blk = tok * n_swap
    pair = 2 * tok
    far = -(-MOST // pair)
    q_width, kv_width = queries.shape[1] // 4, keys.shape[1] // 4
    both = ("swap", "blk")
    devices = [(b, s) for b in range(n_blk) for s in range(n_swap)]

    def index(b, s):
        return s * n_blk + b

    routes = [
        [(index(b, s), index(b ^ 1, s)) for b, s in devices],
        [(index(b, s), index(b, s ^ 1)) for b, s in devices],
        [(index(b, s), index(b ^ 1, s ^ 1)) for b, s in devices],
    ]

    def to_partners(parts):
        return [lax.ppermute(part, both, route) for part, route in zip(parts, routes)]

    def along_z(part, k):
        route = [(s, 2 * ((s // 2 + k) % n_out) + s % 2) for s in range(n_swap)]
        return lax.ppermute(part, "swap", route)

    def along_x(part, step):
        return lax.ppermute(
            part, "blk", [(b, b + step) for b in range(n_blk) if 0 <= b + step < n_blk]
        )

    def shape(rows, cols, dtype=BF16):
        return jax.ShapeDtypeStruct((rows, cols), dtype)

    def split(a, b, width, name):
        return vmem_call(
            split_kernel,
            [shape(tok, 2 * width)] * 4,
            (a, b),
            scratch=[pltpu.SemaphoreType.DMA((8,))],
            hbm=(0, 1),
            name=name,
        )

    kv_parts = split(keys, values, kv_width, "split_kv")
    kv_recv = to_partners(kv_parts[1:])
    qg_parts = split(queries, grad_out, q_width, "split_qg")

    block_shape = shape(pair, 2 * kv_width)
    shifts = [k for k in range(1, far + 1) if k < n_out]
    made = vmem_call(
        functools.partial(first_payload_kernel, n_out),
        [block_shape] * (2 + len(shifts)),
        (kv_parts[0], *kv_recv),
        through=qg_parts,
        name="payload_odd",
    )
    even, odd, odd_pay, qg_parts = made[0], made[1], made[2:-4], made[-4:]
    rim = along_x(odd, 2)
    odd_got = [along_z(part, k) for k, part in zip(shifts, odd_pay)]
    qg_recv = to_partners(qg_parts[1:])
    even_pay = vmem_call(
        functools.partial(second_payload_kernel, n_out),
        [block_shape] * len(shifts),
        (even, rim),
        name="payload_even",
    )
    even_got = [along_z(part, k) for k, part in zip(shifts, even_pay)]

    starts = doc_ids.reshape(-1, 128)
    n_slots = far + 1
    rows = (q_width // HEAD_DIM) * tok
    sum_dtypes = [F32 if (i == far or far - i == n_out) else BF16 for i in range(n_slots)]
    sum_shapes = [shape(pair, 2 * kv_width, dtype) for dtype in sum_dtypes]

    def attend(which, slots, dq_first=None):
        second = dq_first is not None
        dq_shapes = [shape(tok, q_width)] * 4 if second else [shape(pair, q_width)]
        return vmem_call(
            functools.partial(attend_kernel, which, second, n_slots, seq_blk),
            dq_shapes + sum_shapes,
            (qg_parts[0], *qg_recv, starts, doc_ids, *slots) + ((dq_first,) if second else ()),
            scratch=[
                pltpu.VMEM((2, rows, HEAD_DIM), BF16),
                pltpu.VMEM((2, rows, HEAD_DIM), BF16),
                pltpu.VMEM((HEAD_DIM, rows), BF16),
                pltpu.VMEM((HEAD_DIM, rows), BF16),
                pltpu.VMEM((n_slots * pair, 2 * kv_width), BF16),
                pltpu.VMEM((MOST + tok, rows), F32),
                pltpu.VMEM((MOST + tok, rows), F32),
                pltpu.VMEM((HEAD_DIM, rows), F32),
                pltpu.VMEM((n_slots * pair, 2 * kv_width), F32),
            ]
            + ([pltpu.VMEM((pair, q_width), BF16)] if second else []),
            smem=(5,),
            mib=24,
            flops=6_000_000_000,
            name="attend_odd" if which else "attend_even",
        )

    def slots_of(up, down, got):
        return [down if k == n_out else got[k - 1] for k in range(far, 0, -1)] + [up]

    def sent(sums):
        return [sums[far - k] for k in shifts]

    def own_down(sums):
        return [sums[0]] if far == n_out else []

    def back_along_z(parts):
        return [along_z(part, n_out - k) for k, part in zip(shifts, parts)]

    dq_even, *even_sums = attend(0, slots_of(even, rim, even_got))
    even_back = back_along_z(sent(even_sums))
    made = attend(1, slots_of(odd, even, odd_got), dq_even)
    dq_parts, odd_sums = made[:4], made[4:]
    dq_recv = to_partners(dq_parts[1:])
    even_total, rim_total, *odd_sent = vmem_call(
        functools.partial(even_sum_kernel, n_out, len(shifts)),
        [shape(pair, 2 * kv_width, F32), block_shape],
        (even_sums[far], *even_back, *own_down(even_sums)),
        through=sent(odd_sums),
        name="even_sum",
    )
    rim_home = along_x(rim_total, -2)
    odd_back = back_along_z(odd_sent)
    home = vmem_call(
        functools.partial(home_kernel, n_out, len(shifts)),
        [shape(tok, 2 * kv_width, F32)] + [shape(tok, 2 * kv_width)] * 3,
        (odd_sums[far], even_total, rim_home, *odd_back, *own_down(odd_sums)),
        scratch=[pltpu.VMEM((2, pair, 2 * kv_width), F32)],
        name="home",
    )
    kv_home = to_partners(home[1:])
    return vmem_call(
        finish_kernel,
        [shape(*queries.shape), shape(*keys.shape), shape(*values.shape)],
        (dq_parts[0], *dq_recv, home[0], *kv_home),
        name="finish",
    )


def solution(mesh):
    spec = P(("blk", "swap"), None)
    return jax.shard_map(
        lambda *args: tuple(body(*args)),
        mesh=mesh,
        in_specs=(spec, spec, spec, spec, P()),
        out_specs=(spec, spec, spec),
        check_vma=False,
    )
```

time: 243 us -> 89.4 us (0.37)
  the two profiles are of different devices: /device:TPU:1 before, /device:TPU:3 now
where the time goes in v1:
time: 89.4 us; the launch traced here: 89 us
  starting transfers between devices  33.3 us (37%)
  waiting for transfers between devices  31.5 us (35%)
  Pallas kernels  19.2 us (21%)
  local copies, waits for them, and re-layouts  4.25 us (5%)
    ppermute x12, waiting for transfers between devices, along_z(): return lax.ppermute(part, 'swap', route)  21.4 us
    pallas_call x9, Pallas kernels, vmem_call(): pl.pallas_call(run, out_shape=list(out_shapes) + [jax.ShapeDtypeStruct(t....  19.2 us
    ppermute x12, starting transfers between devices, to_partners(): lax.ppermute(part, both, route)  11.9 us
    ppermute x12, starting transfers between devices, along_z(): return lax.ppermute(part, 'swap', route)  11.3 us
    ppermute x2, starting transfers between devices, along_x(): lax.ppermute(part, 'blk', [(b, b + step) for b in range(n_blk) if 0 <= b...  10 us
    ppermute x2, waiting for transfers between devices, along_x(): lax.ppermute(part, 'blk', [(b, b + step) for b in range(n_blk) if 0 <= b...  5.65 us
    ppermute x12, waiting for transfers between devices, to_partners(): lax.ppermute(part, both, route)  4.43 us
    unnamed x10, local copies, waits for them, and re-layouts  4.25 us
  transfers between devices with their start and end apart: 26, of which 8 were waited for; matrix products, arithmetic and copies ran while one was open for 0% of the time, Pallas kernels for 20%

profile of v1, /device:TPU:3, one launch (start us, length us, event | category | flops | bytes accessed | tf_op | source)
XLA Modules:
  0.0 89.0 jit_solution(14776717891433288253)
XLA Ops:
  0.6 0.9 %copy-done.2 = bf16[128,512]{1,0:T(8,128)(2,1)S(1)} copy-done((bf16[128,512]{1,0:T(8,128)(2,1)S(1)}, bf16[128,512]{1,0:T(8,128)(2,1)}, u32[]{:S(2)}) %copy-start.2) | copy-done | bytes 131096
  1.5 0.9 %copy-done.3 = bf16[128,512]{1,0:T(8,128)(2,1)S(1)} copy-done((bf16[128,512]{1,0:T(8,128)(2,1)S(1)}, bf16[128,512]{1,0:T(8,128)(2,1)}, u32[]{:S(2)}) %copy-start.3) | copy-done | bytes 131096
  2.4 0.1 split_kv.1
  2.6 0.7 collective-permute-start
  3.3 1.3 %collective-permute-start.1 = (bf16[128,256]{1,0:T(8,128)(2,1)S(1)}, bf16[128,256]{1,0:T(8,128)(2,1)S(1)}, u32[]{:S(2)}, u32[]{:S(2)}) collective-permute-start(bf16[128,256]{1,0:T(8,128)(2,1)S(1)} %get-tuple-element.49), channel_id=1, source_target_pairs={{0,4},{4,0},{8,12},{12,8},{16,20},{20,16},{24,28},{28,24},{1,5},{5... | collective-permute-start | bytes 196616 | tf_op jit(solution)/shard_map/ppermute | solution.py:301
  4.6 0.5 collective-permute-start.2
  5.0 1.2 %copy-done = bf16[128,4096]{1,0:T(8,128)(2,1)S(1)} copy-done((bf16[128,4096]{1,0:T(8,128)(2,1)S(1)}, bf16[128,4096]{1,0:T(8,128)(2,1)}, u32[]{:S(2)}) %copy-start) | copy-done | bytes 1048600
  6.3 1.2 %copy-done.1 = bf16[128,4096]{1,0:T(8,128)(2,1)S(1)} copy-done((bf16[128,4096]{1,0:T(8,128)(2,1)S(1)}, bf16[128,4096]{1,0:T(8,128)(2,1)}, u32[]{:S(2)}) %copy-start.1) | copy-done | bytes 1048600
  7.5 0.2 split_qg.1
  7.7 0.0 collective-permute-done.refs_1_
  7.7 0.0 collective-permute-done.1.refs_2_
  7.8 0.9 collective-permute-done.2.refs_3_
  8.6 0.1 payload_odd.1
  8.7 0.4 collective-permute-start.3
  9.1 1.1 %collective-permute-start.4 = (bf16[128,2048]{1,0:T(8,128)(2,1)S(1)}, bf16[128,2048]{1,0:T(8,128)(2,1)S(1)}, u32[]{:S(2)}, u32[]{:S(2)}) collective-permute-start(bf16[128,2048]{1,0:T(8,128)(2,1)S(1)} %get-tuple-element.57), channel_id=1, source_target_pairs={{0,4},{4,0},{8,12},{12,8},{16,20},{20,16},{24,28},{28,24},{1,5},{5... | collective-permute-start | bytes 1572872 | tf_op jit(solution)/shard_map/ppermute | solution.py:301
  10.2 0.7 collective-permute-start.5
  10.9 1.3 %collective-permute-start.9 = (bf16[256,256]{1,0:T(8,128)(2,1)S(1)}, bf16[256,256]{1,0:T(8,128)(2,1)S(1)}, u32[]{:S(2)}, u32[]{:S(2)}) collective-permute-start(bf16[256,256]{1,0:T(8,128)(2,1)S(1)} %get-tuple-element.63.refs_10_), channel_id=1, source_target_pairs={{0,2},{1,3},{4,6},{5,7},{8,10},{9,11},{12,14},{13,15},{16,18},{17,... | collective-permute-start | bytes 393224 | tf_op jit(solution)/shard_map/ppermute | solution.py:308
  12.2 5.6 %collective-permute-done.9.refs_1_.refs_6_ = bf16[256,256]{1,0:T(8,128)(2,1)S(1)} collective-permute-done((bf16[256,256]{1,0:T(8,128)(2,1)S(1)}, bf16[256,256]{1,0:T(8,128)(2,1)S(1)}, u32[]{:S(2)}, u32[]{:S(2)}) %collective-permute-start.9) | collective-permute-done | bytes 131104 | tf_op jit(solution)/shard_map/ppermute | solution.py:308
  17.9 3.4 %collective-permute-start.10 = (bf16[256,256]{1,0:T(8,128)(2,1)S(1)}, bf16[256,256]{1,0:T(8,128)(2,1)S(1)}, u32[]{:S(2)}, u32[]{:S(2)}) collective-permute-start(bf16[256,256]{1,0:T(8,128)(2,1)S(1)} %get-tuple-element.64), channel_id=1, source_target_pairs={{0,24},{4,28},{8,0},{12,4},{16,8},{20,12},{24,16},{28,20},{1,25},{... | collective-permute-start | bytes 393224 | tf_op jit(solution)/shard_map/ppermute | solution.py:305
  21.3 0.0 collective-permute-start.11
  21.3 2.0 %collective-permute-done.10.refs_7_ = bf16[256,256]{1,0:T(8,128)(2,1)S(1)} collective-permute-done((bf16[256,256]{1,0:T(8,128)(2,1)S(1)}, bf16[256,256]{1,0:T(8,128)(2,1)S(1)}, u32[]{:S(2)}, u32[]{:S(2)}) %collective-permute-start.10) | collective-permute-done | bytes 131104 | tf_op jit(solution)/shard_map/ppermute | solution.py:305
  23.2 0.2 collective-permute-start.12
  23.4 7.3 %collective-permute-done.11.refs_8_ = bf16[256,256]{1,0:T(8,128)(2,1)S(1)} collective-permute-done((bf16[256,256]{1,0:T(8,128)(2,1)S(1)}, bf16[256,256]{1,0:T(8,128)(2,1)S(1)}, u32[]{:S(2)}, u32[]{:S(2)}) %collective-permute-start.11) | collective-permute-done | bytes 131104 | tf_op jit(solution)/shard_map/ppermute | solution.py:305
  30.7 1.8 %collective-permute-start.6 = (bf16[256,256]{1,0:T(8,128)(2,1)S(1)}, bf16[256,256]{1,0:T(8,128)(2,1)S(1)}, u32[]{:S(2)}, u32[]{:S(2)}) collective-permute-start(bf16[256,256]{1,0:T(8,128)(2,1)S(1)} %get-tuple-element.60), channel_id=1, source_target_pairs={{0,24},{4,28},{8,0},{12,4},{16,8},{20,12},{24,16},{28,20},{1,25},{... | collective-permute-start | bytes 393224 | tf_op jit(solution)/shard_map/ppermute | solution.py:305
  32.4 0.0 collective-permute-done.12.refs_9_
  32.4 2.1 %collective-permute-start.7 = (bf16[256,256]{1,0:T(8,128)(2,1)S(1)}, bf16[256,256]{1,0:T(8,128)(2,1)S(1)}, u32[]{:S(2)}, u32[]{:S(2)}) collective-permute-start(bf16[256,256]{1,0:T(8,128)(2,1)S(1)} %get-tuple-element.61), channel_id=1, source_target_pairs={{0,16},{4,20},{8,24},{12,28},{16,0},{20,4},{24,8},{28,12},{1,17},{... | collective-permute-start | bytes 393224 | tf_op jit(solution)/shard_map/ppermute | solution.py:305
  34.5 11.0 %attend_even.1 = (bf16[256,1024]{1,0:T(8,128)(2,1)S(1)}, f32[256,256]{1,0:T(8,128)S(1)}, bf16[256,256]{1,0:T(8,128)(2,1)S(1)}, bf16[256,256]{1,0:T(8,128)(2,1)S(...) custom-call(bf16[128,2048]{1,0:T(8,128)(2,1)S(1)} %get-tuple-element.55.refs_0_, ...), custom_call_target="tpu_custom_call" | custom-call | flops 6000000000 | tf_op jit(solution)/shard_map/attend_even/pallas_call | solution.py:41
  45.5 0.1 collective-permute-start.16
  45.6 0.1 collective-permute-start.17
  45.7 1.4 %collective-permute-start.18 = (bf16[256,256]{1,0:T(8,128)(2,1)S(1)}, bf16[256,256]{1,0:T(8,128)(2,1)S(1)}, u32[]{:S(2)}, u32[]{:S(2)}) collective-permute-start(bf16[256,256]{1,0:T(8,128)(2,1)S(1)} %get-tuple-element.76), channel_id=1, source_target_pairs={{0,8},{4,12},{8,16},{12,20},{16,24},{20,28},{24,0},{28,4},{1,9},{5... | collective-permute-start | bytes 393224 | tf_op jit(solution)/shard_map/ppermute | solution.py:305
  47.0 6.1 %attend_odd.1 = (bf16[128,1024]{1,0:T(8,128)(2,1)S(1)}, bf16[128,1024]{1,0:T(8,128)(2,1)S(1)}, bf16[128,1024]{1,0:T(8,128)(2,1)S(1)}, bf16[128,1024]{1,0:T(8,128...) custom-call(bf16[128,2048]{1,0:T(8,128)(2,1)S(1)} %get-tuple-element, ...), custom_call_target="tpu_custom_call" | custom-call | flops 6000000000 | tf_op jit(solution)/shard_map/attend_odd/pallas_call | solution.py:41
  53.2 3.4 %collective-permute-done.17.refs_2_ = bf16[256,256]{1,0:T(8,128)(2,1)S(1)} collective-permute-done((bf16[256,256]{1,0:T(8,128)(2,1)S(1)}, bf16[256,256]{1,0:T(8,128)(2,1)S(1)}, u32[]{:S(2)}, u32[]{:S(2)}) %collective-permute-start.17) | collective-permute-done | bytes 131104 | tf_op jit(solution)/shard_map/ppermute | solution.py:305
  56.6 0.2 even_sum.1
  56.7 8.7 %collective-permute-start.19 = (bf16[256,256]{1,0:T(8,128)(2,1)S(1)}, bf16[256,256]{1,0:T(8,128)(2,1)S(1)}, u32[]{:S(2)}, u32[]{:S(2)}) collective-permute-start(bf16[256,256]{1,0:T(8,128)(2,1)S(1)} %get-tuple-element.82), channel_id=1, source_target_pairs={{2,0},{3,1},{6,4},{7,5},{10,8},{11,9},{14,12},{15,13},{18,16},{19,... | collective-permute-start | bytes 393224 | tf_op jit(solution)/shard_map/ppermute | solution.py:308
  65.5 0.1 collective-permute-start.20
  65.6 2.6 %collective-permute-start.13 = (bf16[128,1024]{1,0:T(8,128)(2,1)S(1)}, bf16[128,1024]{1,0:T(8,128)(2,1)S(1)}, u32[]{:S(2)}, u32[]{:S(2)}) collective-permute-start(bf16[128,1024]{1,0:T(8,128)(2,1)S(1)} %get-tuple-element.69), channel_id=1, source_target_pairs={{0,1},{4,5},{8,9},{12,13},{16,17},{20,21},{24,25},{28,29},{1,0},{5... | collective-permute-start | bytes 786440 | tf_op jit(solution)/shard_map/ppermute | solution.py:301
  68.1 1.1 %collective-permute-start.14 = (bf16[128,1024]{1,0:T(8,128)(2,1)S(1)}, bf16[128,1024]{1,0:T(8,128)(2,1)S(1)}, u32[]{:S(2)}, u32[]{:S(2)}) collective-permute-start(bf16[128,1024]{1,0:T(8,128)(2,1)S(1)} %get-tuple-element.70), channel_id=1, source_target_pairs={{0,4},{4,0},{8,12},{12,8},{16,20},{20,16},{24,28},{28,24},{1,5},{5... | collective-permute-start | bytes 786440 | tf_op jit(solution)/shard_map/ppermute | solution.py:301
  69.2 0.5 collective-permute-start.15
  69.8 0.8 collective-permute-start.21
  70.6 1.6 %collective-permute-start.22 = (bf16[256,256]{1,0:T(8,128)(2,1)S(1)}, bf16[256,256]{1,0:T(8,128)(2,1)S(1)}, u32[]{:S(2)}, u32[]{:S(2)}) collective-permute-start(bf16[256,256]{1,0:T(8,128)(2,1)S(1)} %get-tuple-element.85), channel_id=1, source_target_pairs={{0,8},{4,12},{8,16},{12,20},{16,24},{20,28},{24,0},{28,4},{1,9},{5... | collective-permute-start | bytes 393224 | tf_op jit(solution)/shard_map/ppermute | solution.py:305
  72.2 8.8 %collective-permute-done.21.refs_4_ = bf16[256,256]{1,0:T(8,128)(2,1)S(1)} collective-permute-done((bf16[256,256]{1,0:T(8,128)(2,1)S(1)}, bf16[256,256]{1,0:T(8,128)(2,1)S(1)}, u32[]{:S(2)}, u32[]{:S(2)}) %collective-permute-start.21) | collective-permute-done | bytes 131104 | tf_op jit(solution)/shard_map/ppermute | solution.py:305
  80.9 0.3 home.1
  81.3 1.3 %collective-permute-start.23 = (bf16[128,256]{1,0:T(8,128)(2,1)S(1)}, bf16[128,256]{1,0:T(8,128)(2,1)S(1)}, u32[]{:S(2)}, u32[]{:S(2)}) collective-permute-start(bf16[128,256]{1,0:T(8,128)(2,1)S(1)} %get-tuple-element.88), channel_id=1, source_target_pairs={{0,1},{4,5},{8,9},{12,13},{16,17},{20,21},{24,25},{28,29},{1,0},{5... | collective-permute-start | bytes 196616 | tf_op jit(solution)/shard_map/ppermute | solution.py:301
  82.6 1.1 %collective-permute-start.24 = (bf16[128,256]{1,0:T(8,128)(2,1)S(1)}, bf16[128,256]{1,0:T(8,128)(2,1)S(1)}, u32[]{:S(2)}, u32[]{:S(2)}) collective-permute-start(bf16[128,256]{1,0:T(8,128)(2,1)S(1)} %get-tuple-element.89), channel_id=1, source_target_pairs={{0,4},{4,0},{8,12},{12,8},{16,20},{20,16},{24,28},{28,24},{1,5},{5... | collective-permute-start | bytes 196616 | tf_op jit(solution)/shard_map/ppermute | solution.py:301
  83.7 0.6 collective-permute-start.25
  84.3 1.9 %collective-permute-done.24.refs_6_ = bf16[128,256]{1,0:T(8,128)(2,1)S(1)} collective-permute-done((bf16[128,256]{1,0:T(8,128)(2,1)S(1)}, bf16[128,256]{1,0:T(8,128)(2,1)S(1)}, u32[]{:S(2)}, u32[]{:S(2)}) %collective-permute-start.24) | collective-permute-done | bytes 65568 | tf_op jit(solution)/shard_map/ppermute | solution.py:301
  86.2 1.6 %collective-permute-done.25.refs_7_ = bf16[128,256]{1,0:T(8,128)(2,1)S(1)} collective-permute-done((bf16[128,256]{1,0:T(8,128)(2,1)S(1)}, bf16[128,256]{1,0:T(8,128)(2,1)S(1)}, u32[]{:S(2)}, u32[]{:S(2)}) %collective-permute-start.25) | collective-permute-done | bytes 65568 | tf_op jit(solution)/shard_map/ppermute | solution.py:301
  87.8 1.2 %finish.1 = (bf16[128,4096]{1,0:T(8,128)(2,1)}, bf16[128,512]{1,0:T(8,128)(2,1)}, bf16[128,512]{1,0:T(8,128)(2,1)}) custom-call(bf16[128,1024]{1,0:T(8,128)(2,1)S(1)} %get-tuple-element.68.refs_0_, bf16[128,1024]{1,0:T(8,128)(2,1)S(1)} %collective-permute-done.13.refs_1_, bf16[128,1024]{1,0:T(8,128)(2,1)S(1)} %collective-permute-done.14.refs_2_, ...), custom_call_target="tpu_custom_call" | custom-call | tf_op jit(solution)/shard_map/finish/pallas_call | solution.py:41
  (23 shorter events, 0.1 us)
Async XLA Ops:
  0.6 0.9 %copy-start.2 = (bf16[128,512]{1,0:T(8,128)(2,1)S(1)}, bf16[128,512]{1,0:T(8,128)(2,1)}, u32[]{:S(2)}) copy-start(bf16[128,512]{1,0:T(8,128)(2,1)} %refs_0_.2) | copy-start | bytes 393220
  1.5 0.9 %copy-start.3 = (bf16[128,512]{1,0:T(8,128)(2,1)S(1)}, bf16[128,512]{1,0:T(8,128)(2,1)}, u32[]{:S(2)}) copy-start(bf16[128,512]{1,0:T(8,128)(2,1)} %refs_1_.2) | copy-start | bytes 393220
  2.6 5.1 %collective-permute-start = (bf16[128,256]{1,0:T(8,128)(2,1)S(1)}, bf16[128,256]{1,0:T(8,128)(2,1)S(1)}, u32[]{:S(2)}, u32[]{:S(2)}) collective-permute-start(bf16[128,256]{1,0:T(8,128)(2,1)S(1)} %get-tuple-element.48), channel_id=1, source_target_pairs={{0,1},{4,5},{8,9},{12,13},{16,17},{20,21},{24,25},{28,29},{1,0},{5... | collective-permute-start | bytes 196616 | tf_op jit(solution)/shard_map/ppermute | solution.py:301
  3.3 4.4 %collective-permute-start.1 = (bf16[128,256]{1,0:T(8,128)(2,1)S(1)}, bf16[128,256]{1,0:T(8,128)(2,1)S(1)}, u32[]{:S(2)}, u32[]{:S(2)}) collective-permute-start(bf16[128,256]{1,0:T(8,128)(2,1)S(1)} %get-tuple-element.49), channel_id=1, source_target_pairs={{0,4},{4,0},{8,12},{12,8},{16,20},{20,16},{24,28},{28,24},{1,5},{5... | collective-permute-start | bytes 196616 | tf_op jit(solution)/shard_map/ppermute | solution.py:301
  4.6 4.0 %collective-permute-start.2 = (bf16[128,256]{1,0:T(8,128)(2,1)S(1)}, bf16[128,256]{1,0:T(8,128)(2,1)S(1)}, u32[]{:S(2)}, u32[]{:S(2)}) collective-permute-start(bf16[128,256]{1,0:T(8,128)(2,1)S(1)} %get-tuple-element.50), channel_id=1, source_target_pairs={{0,5},{4,1},{8,13},{12,9},{16,21},{20,17},{24,29},{28,25},{1,4},{5... | collective-permute-start | bytes 196616 | tf_op jit(solution)/shard_map/ppermute | solution.py:301
  5.0 1.2 %copy-start = (bf16[128,4096]{1,0:T(8,128)(2,1)S(1)}, bf16[128,4096]{1,0:T(8,128)(2,1)}, u32[]{:S(2)}) copy-start(bf16[128,4096]{1,0:T(8,128)(2,1)} %refs_0_.3) | copy-start | bytes 3145732
  6.3 1.2 %copy-start.1 = (bf16[128,4096]{1,0:T(8,128)(2,1)S(1)}, bf16[128,4096]{1,0:T(8,128)(2,1)}, u32[]{:S(2)}) copy-start(bf16[128,4096]{1,0:T(8,128)(2,1)} %refs_1_.3) | copy-start | bytes 3145732
  8.7 25.8 %collective-permute-start.3 = (bf16[128,2048]{1,0:T(8,128)(2,1)S(1)}, bf16[128,2048]{1,0:T(8,128)(2,1)S(1)}, u32[]{:S(2)}, u32[]{:S(2)}) collective-permute-start(bf16[128,2048]{1,0:T(8,128)(2,1)S(1)} %get-tuple-element.56), channel_id=1, source_target_pairs={{0,1},{4,5},{8,9},{12,13},{16,17},{20,21},{24,25},{28,29},{1,0},{5... | collective-permute-start | bytes 1572872 | tf_op jit(solution)/shard_map/ppermute | solution.py:301
  9.1 25.4 %collective-permute-start.4 = (bf16[128,2048]{1,0:T(8,128)(2,1)S(1)}, bf16[128,2048]{1,0:T(8,128)(2,1)S(1)}, u32[]{:S(2)}, u32[]{:S(2)}) collective-permute-start(bf16[128,2048]{1,0:T(8,128)(2,1)S(1)} %get-tuple-element.57), channel_id=1, source_target_pairs={{0,4},{4,0},{8,12},{12,8},{16,20},{20,16},{24,28},{28,24},{1,5},{5... | collective-permute-start | bytes 1572872 | tf_op jit(solution)/shard_map/ppermute | solution.py:301
  10.2 24.3 %collective-permute-start.5 = (bf16[128,2048]{1,0:T(8,128)(2,1)S(1)}, bf16[128,2048]{1,0:T(8,128)(2,1)S(1)}, u32[]{:S(2)}, u32[]{:S(2)}) collective-permute-start(bf16[128,2048]{1,0:T(8,128)(2,1)S(1)} %get-tuple-element.58), channel_id=1, source_target_pairs={{0,5},{4,1},{8,13},{12,9},{16,21},{20,17},{24,29},{28,25},{1,4},{5... | collective-permute-start | bytes 1572872 | tf_op jit(solution)/shard_map/ppermute | solution.py:301
  10.9 6.9 %collective-permute-start.9 = (bf16[256,256]{1,0:T(8,128)(2,1)S(1)}, bf16[256,256]{1,0:T(8,128)(2,1)S(1)}, u32[]{:S(2)}, u32[]{:S(2)}) collective-permute-start(bf16[256,256]{1,0:T(8,128)(2,1)S(1)} %get-tuple-element.63.refs_10_), channel_id=1, source_target_pairs={{0,2},{1,3},{4,6},{5,7},{8,10},{9,11},{12,14},{13,15},{16,18},{17,... | collective-permute-start | bytes 393224 | tf_op jit(solution)/shard_map/ppermute | solution.py:308
  17.8 16.7 %copy-start.4 = (s32[4096]{0:T(1024)S(1)}, s32[4096]{0:T(1024)}, u32[]{:S(2)}) copy-start(s32[4096]{0:T(1024)} %refs_5_.3) | copy-start | bytes 49156
  17.9 5.3 %collective-permute-start.10 = (bf16[256,256]{1,0:T(8,128)(2,1)S(1)}, bf16[256,256]{1,0:T(8,128)(2,1)S(1)}, u32[]{:S(2)}, u32[]{:S(2)}) collective-permute-start(bf16[256,256]{1,0:T(8,128)(2,1)S(1)} %get-tuple-element.64), channel_id=1, source_target_pairs={{0,24},{4,28},{8,0},{12,4},{16,8},{20,12},{24,16},{28,20},{1,25},{... | collective-permute-start | bytes 393224 | tf_op jit(solution)/shard_map/ppermute | solution.py:305
  21.3 9.4 %collective-permute-start.11 = (bf16[256,256]{1,0:T(8,128)(2,1)S(1)}, bf16[256,256]{1,0:T(8,128)(2,1)S(1)}, u32[]{:S(2)}, u32[]{:S(2)}) collective-permute-start(bf16[256,256]{1,0:T(8,128)(2,1)S(1)} %get-tuple-element.65), channel_id=1, source_target_pairs={{0,16},{4,20},{8,24},{12,28},{16,0},{20,4},{24,8},{28,12},{1,17},{... | collective-permute-start | bytes 393224 | tf_op jit(solution)/shard_map/ppermute | solution.py:305
  23.2 9.2 %collective-permute-start.12 = (bf16[256,256]{1,0:T(8,128)(2,1)S(1)}, bf16[256,256]{1,0:T(8,128)(2,1)S(1)}, u32[]{:S(2)}, u32[]{:S(2)}) collective-permute-start(bf16[256,256]{1,0:T(8,128)(2,1)S(1)} %get-tuple-element.66), channel_id=1, source_target_pairs={{0,8},{4,12},{8,16},{12,20},{16,24},{20,28},{24,0},{28,4},{1,9},{5... | collective-permute-start | bytes 393224 | tf_op jit(solution)/shard_map/ppermute | solution.py:305
  30.7 15.0 %collective-permute-start.6 = (bf16[256,256]{1,0:T(8,128)(2,1)S(1)}, bf16[256,256]{1,0:T(8,128)(2,1)S(1)}, u32[]{:S(2)}, u32[]{:S(2)}) collective-permute-start(bf16[256,256]{1,0:T(8,128)(2,1)S(1)} %get-tuple-element.60), channel_id=1, source_target_pairs={{0,24},{4,28},{8,0},{12,4},{16,8},{20,12},{24,16},{28,20},{1,25},{... | collective-permute-start | bytes 393224 | tf_op jit(solution)/shard_map/ppermute | solution.py:305
  32.4 14.6 %collective-permute-start.7 = (bf16[256,256]{1,0:T(8,128)(2,1)S(1)}, bf16[256,256]{1,0:T(8,128)(2,1)S(1)}, u32[]{:S(2)}, u32[]{:S(2)}) collective-permute-start(bf16[256,256]{1,0:T(8,128)(2,1)S(1)} %get-tuple-element.61), channel_id=1, source_target_pairs={{0,16},{4,20},{8,24},{12,28},{16,0},{20,4},{24,8},{28,12},{1,17},{... | collective-permute-start | bytes 393224 | tf_op jit(solution)/shard_map/ppermute | solution.py:305
  34.5 12.6 %collective-permute-start.8 = (bf16[256,256]{1,0:T(8,128)(2,1)S(1)}, bf16[256,256]{1,0:T(8,128)(2,1)S(1)}, u32[]{:S(2)}, u32[]{:S(2)}) collective-permute-start(bf16[256,256]{1,0:T(8,128)(2,1)S(1)} %get-tuple-element.62), channel_id=1, source_target_pairs={{0,8},{4,12},{8,16},{12,20},{16,24},{20,28},{24,0},{28,4},{1,9},{5... | collective-permute-start | bytes 393224 | tf_op jit(solution)/shard_map/ppermute | solution.py:305
  45.5 7.6 %collective-permute-start.16 = (bf16[256,256]{1,0:T(8,128)(2,1)S(1)}, bf16[256,256]{1,0:T(8,128)(2,1)S(1)}, u32[]{:S(2)}, u32[]{:S(2)}) collective-permute-start(bf16[256,256]{1,0:T(8,128)(2,1)S(1)} %get-tuple-element.74), channel_id=1, source_target_pairs={{0,24},{4,28},{8,0},{12,4},{16,8},{20,12},{24,16},{28,20},{1,25},{... | collective-permute-start | bytes 393224 | tf_op jit(solution)/shard_map/ppermute | solution.py:305
  45.6 11.0 %collective-permute-start.17 = (bf16[256,256]{1,0:T(8,128)(2,1)S(1)}, bf16[256,256]{1,0:T(8,128)(2,1)S(1)}, u32[]{:S(2)}, u32[]{:S(2)}) collective-permute-start(bf16[256,256]{1,0:T(8,128)(2,1)S(1)} %get-tuple-element.75), channel_id=1, source_target_pairs={{0,16},{4,20},{8,24},{12,28},{16,0},{20,4},{24,8},{28,12},{1,17},{... | collective-permute-start | bytes 393224 | tf_op jit(solution)/shard_map/ppermute | solution.py:305
  45.7 10.9 %collective-permute-start.18 = (bf16[256,256]{1,0:T(8,128)(2,1)S(1)}, bf16[256,256]{1,0:T(8,128)(2,1)S(1)}, u32[]{:S(2)}, u32[]{:S(2)}) collective-permute-start(bf16[256,256]{1,0:T(8,128)(2,1)S(1)} %get-tuple-element.76), channel_id=1, source_target_pairs={{0,8},{4,12},{8,16},{12,20},{16,24},{20,28},{24,0},{28,4},{1,9},{5... | collective-permute-start | bytes 393224 | tf_op jit(solution)/shard_map/ppermute | solution.py:305
  56.7 13.0 %collective-permute-start.19 = (bf16[256,256]{1,0:T(8,128)(2,1)S(1)}, bf16[256,256]{1,0:T(8,128)(2,1)S(1)}, u32[]{:S(2)}, u32[]{:S(2)}) collective-permute-start(bf16[256,256]{1,0:T(8,128)(2,1)S(1)} %get-tuple-element.82), channel_id=1, source_target_pairs={{2,0},{3,1},{6,4},{7,5},{10,8},{11,9},{14,12},{15,13},{18,16},{19,... | collective-permute-start | bytes 393224 | tf_op jit(solution)/shard_map/ppermute | solution.py:308
  65.5 5.1 %collective-permute-start.20 = (bf16[256,256]{1,0:T(8,128)(2,1)S(1)}, bf16[256,256]{1,0:T(8,128)(2,1)S(1)}, u32[]{:S(2)}, u32[]{:S(2)}) collective-permute-start(bf16[256,256]{1,0:T(8,128)(2,1)S(1)} %get-tuple-element.83), channel_id=1, source_target_pairs={{0,24},{4,28},{8,0},{12,4},{16,8},{20,12},{24,16},{28,20},{1,25},{... | collective-permute-start | bytes 393224 | tf_op jit(solution)/shard_map/ppermute | solution.py:305
  65.6 18.1 %collective-permute-start.13 = (bf16[128,1024]{1,0:T(8,128)(2,1)S(1)}, bf16[128,1024]{1,0:T(8,128)(2,1)S(1)}, u32[]{:S(2)}, u32[]{:S(2)}) collective-permute-start(bf16[128,1024]{1,0:T(8,128)(2,1)S(1)} %get-tuple-element.69), channel_id=1, source_target_pairs={{0,1},{4,5},{8,9},{12,13},{16,17},{20,21},{24,25},{28,29},{1,0},{5... | collective-permute-start | bytes 786440 | tf_op jit(solution)/shard_map/ppermute | solution.py:301
  68.1 16.2 %collective-permute-start.14 = (bf16[128,1024]{1,0:T(8,128)(2,1)S(1)}, bf16[128,1024]{1,0:T(8,128)(2,1)S(1)}, u32[]{:S(2)}, u32[]{:S(2)}) collective-permute-start(bf16[128,1024]{1,0:T(8,128)(2,1)S(1)} %get-tuple-element.70), channel_id=1, source_target_pairs={{0,4},{4,0},{8,12},{12,8},{16,20},{20,16},{24,28},{28,24},{1,5},{5... | collective-permute-start | bytes 786440 | tf_op jit(solution)/shard_map/ppermute | solution.py:301
  69.2 15.1 %collective-permute-start.15 = (bf16[128,1024]{1,0:T(8,128)(2,1)S(1)}, bf16[128,1024]{1,0:T(8,128)(2,1)S(1)}, u32[]{:S(2)}, u32[]{:S(2)}) collective-permute-start(bf16[128,1024]{1,0:T(8,128)(2,1)S(1)} %get-tuple-element.71), channel_id=1, source_target_pairs={{0,5},{4,1},{8,13},{12,9},{16,21},{20,17},{24,29},{28,25},{1,4},{5... | collective-permute-start | bytes 786440 | tf_op jit(solution)/shard_map/ppermute | solution.py:301
  69.8 11.2 %collective-permute-start.21 = (bf16[256,256]{1,0:T(8,128)(2,1)S(1)}, bf16[256,256]{1,0:T(8,128)(2,1)S(1)}, u32[]{:S(2)}, u32[]{:S(2)}) collective-permute-start(bf16[256,256]{1,0:T(8,128)(2,1)S(1)} %get-tuple-element.84), channel_id=1, source_target_pairs={{0,16},{4,20},{8,24},{12,28},{16,0},{20,4},{24,8},{28,12},{1,17},{... | collective-permute-start | bytes 393224 | tf_op jit(solution)/shard_map/ppermute | solution.py:305
  70.6 10.4 %collective-permute-start.22 = (bf16[256,256]{1,0:T(8,128)(2,1)S(1)}, bf16[256,256]{1,0:T(8,128)(2,1)S(1)}, u32[]{:S(2)}, u32[]{:S(2)}) collective-permute-start(bf16[256,256]{1,0:T(8,128)(2,1)S(1)} %get-tuple-element.85), channel_id=1, source_target_pairs={{0,8},{4,12},{8,16},{12,20},{16,24},{20,28},{24,0},{28,4},{1,9},{5... | collective-permute-start | bytes 393224 | tf_op jit(solution)/shard_map/ppermute | solution.py:305
  81.3 3.0 %collective-permute-start.23 = (bf16[128,256]{1,0:T(8,128)(2,1)S(1)}, bf16[128,256]{1,0:T(8,128)(2,1)S(1)}, u32[]{:S(2)}, u32[]{:S(2)}) collective-permute-start(bf16[128,256]{1,0:T(8,128)(2,1)S(1)} %get-tuple-element.88), channel_id=1, source_target_pairs={{0,1},{4,5},{8,9},{12,13},{16,17},{20,21},{24,25},{28,29},{1,0},{5... | collective-permute-start | bytes 196616 | tf_op jit(solution)/shard_map/ppermute | solution.py:301
  82.6 3.7 %collective-permute-start.24 = (bf16[128,256]{1,0:T(8,128)(2,1)S(1)}, bf16[128,256]{1,0:T(8,128)(2,1)S(1)}, u32[]{:S(2)}, u32[]{:S(2)}) collective-permute-start(bf16[128,256]{1,0:T(8,128)(2,1)S(1)} %get-tuple-element.89), channel_id=1, source_target_pairs={{0,4},{4,0},{8,12},{12,8},{16,20},{20,16},{24,28},{28,24},{1,5},{5... | collective-permute-start | bytes 196616 | tf_op jit(solution)/shard_map/ppermute | solution.py:301
  83.7 4.1 %collective-permute-start.25 = (bf16[128,256]{1,0:T(8,128)(2,1)S(1)}, bf16[128,256]{1,0:T(8,128)(2,1)S(1)}, u32[]{:S(2)}, u32[]{:S(2)}) collective-permute-start(bf16[128,256]{1,0:T(8,128)(2,1)S(1)} %get-tuple-element.90), channel_id=1, source_target_pairs={{0,5},{4,1},{8,13},{12,9},{16,21},{20,17},{24,29},{28,25},{1,4},{5... | collective-permute-start | bytes 196616 | tf_op jit(solution)/shard_map/ppermute | solution.py:301

commit v2 on v1

v2 whole, which is shorter than its diff:
```python
import functools
import math

import jax
import jax.numpy as jnp
from jax import lax
from jax.experimental import pallas as pl
from jax.experimental.pallas import tpu as pltpu
from jax.sharding import PartitionSpec as P

HEAD_DIM = 128
MOST = 1024
BF16 = jnp.bfloat16
F32 = jnp.float32
LOG2E = 1.4426950408889634
MIB = 1024 * 1024

NN = (((1,), (0,)), ((), ()))
NT = (((1,), (1,)), ((), ()))
TN = (((0,), (0,)), ((), ()))


def dot(a, b, dims):
    return lax.dot_general(a, b, dims, preferred_element_type=F32)


def vmem_call(kernel, out_shapes, args, scratch=(), hbm=(), smem=(), after=(), through=(), mib=8, flops=0, name=None):
    def space(i):
        return pltpu.SMEM if i in smem else pltpu.HBM if i in hbm else pltpu.VMEM

    specs = [pl.BlockSpec(memory_space=space(i)) for i in range(len(args))]
    specs += [pl.BlockSpec(memory_space=pl.ANY)] * (len(after) + len(through))
    outs = [pl.BlockSpec(memory_space=pltpu.VMEM)] * len(out_shapes)
    outs += [pl.BlockSpec(memory_space=pl.ANY)] * len(through)
    n_args, n_out = len(args), len(out_shapes)
    n_in, n_made = len(specs), len(outs)

    def run(*refs):
        kernel(*refs[:n_args], *refs[n_in : n_in + n_out], *refs[n_in + n_made :])

    return pl.pallas_call(
        run,
        out_shape=list(out_shapes) + [jax.ShapeDtypeStruct(t.shape, t.dtype) for t in through],
        in_specs=specs,
        out_specs=outs,
        input_output_aliases={n_args + len(after) + i: n_out + i for i in range(len(through))},
        scratch_shapes=list(scratch),
        compiler_params=pltpu.CompilerParams(vmem_limit_bytes=mib * MIB),
        cost_estimate=pl.CostEstimate(flops=flops, bytes_accessed=0, transcendentals=0),
        name=name,
    )(*args, *after, *through)


def place():
    blk, swap = lax.axis_index("blk"), lax.axis_index("swap")
    return lax.rem(blk, 2), lax.rem(swap, 2), lax.div(swap, 2)


def quarters():
    core, y, _ = place()
    return [2 * core + y, 2 * (1 - core) + y, 2 * core + 1 - y, 2 * (1 - core) + 1 - y]


def split_kernel(groups, a_ref, b_ref, *rest):
    outs, sems = rest[:-1], rest[-1]
    width = a_ref.shape[1] // 4
    numbers = quarters()
    copies = []
    for group, out in zip(groups, outs):
        for i, member in enumerate(group(numbers)):
            columns = pl.ds(pl.multiple_of(member * width, 128), width)
            for j, src in enumerate((a_ref, b_ref)):
                dst = out.at[:, (2 * i + j) * width : (2 * i + j + 1) * width]
                copies.append(pltpu.make_async_copy(src.at[:, columns], dst, sems.at[len(copies)]))
    for copy in copies:
        copy.start()
    for copy in copies:
        copy.wait()


def choose_kernel(mine, got, *outs):
    core, y, _ = place()
    width = mine.shape[1] // 2
    for odd, (keep, send) in zip((1, 0), (outs[:2], outs[2:])):
        for out, yy in ((keep, y), (send, 1 - y)):
            columns = pl.ds(pl.multiple_of(yy * width, 128), width)

            @pl.when(core == odd)
            def _(out=out, columns=columns):
                out[...] = mine[:, columns]

            @pl.when(core != odd)
            def _(out=out, columns=columns):
                out[...] = got[:, columns]


def select_chunks(blocks, own, by_core, by_y, by_diag):
    core, y, _ = place()
    rows = own.shape[0]
    here = pl.ds(pl.multiple_of(y * rows, rows), rows)
    there = pl.ds(pl.multiple_of((1 - y) * rows, rows), rows)
    for c in (0, 1):

        @pl.when(core == c)
        def _(c=c):
            blocks[c][here, :] = own[...]
            blocks[c][there, :] = by_y[...]
            blocks[1 - c][here, :] = by_core[...]
            blocks[1 - c][there, :] = by_diag[...]


def fill_payloads(n_out, up, down, outs):
    _, _, z = place()
    for k, out in enumerate(outs, 1):

        @pl.when(z + k < n_out)
        def _(out=out):
            out[...] = up[...]

        @pl.when(z + k >= n_out)
        def _(out=out):
            out[...] = down[...]


def payload_kernel(n_out, n_shifts, own, by_core, by_y, by_diag, even, odd, *outs):
    select_chunks((even, odd), own, by_core, by_y, by_diag)
    fill_payloads(n_out, odd, even, outs[:n_shifts])
    fill_payloads(n_out, even, odd, outs[n_shifts:])


def attend_kernel(odd, n_slots, seq_blk, keep, by_y, starts, doc_scalars, *rest):
    slots, rest = rest[:n_slots], rest[n_slots:]
    dq_keep, dq_send, rest = rest[0], rest[1], rest[2:]
    sums, rest = rest[:n_slots], rest[n_slots:]
    q_rows, g_rows, keys, vals, scores, dweights, dq_cols, acc, stats, dq_both = rest
    _, y, z = place()
    tok = keep.shape[0]
    width = keep.shape[1] // 2
    heads = width // HEAD_DIM
    pair = 2 * tok
    window = (n_slots - 1) * pair
    inv_root = 1.0 / math.sqrt(HEAD_DIM)
    scale = inv_root * LOG2E
    block = 2 * lax.div(lax.axis_index("blk"), 2) + odd
    first = block * seq_blk + z * pair
    base = first - window
    step_cols = 2 * tok
    n_steps = 2 * width // step_cols

    def stack(unit, src):
        for h in range(heads):
            rows = pl.ds(pl.multiple_of(unit * width + h * tok, tok), tok)
            q_rows[rows, :HEAD_DIM] = src[:, h * HEAD_DIM : (h + 1) * HEAD_DIM]
            g_rows[rows, :] = src[:, width + h * HEAD_DIM : width + (h + 1) * HEAD_DIM]

    stack(y, keep)
    stack(1 - y, by_y)
    unity = (
        lax.broadcasted_iota(jnp.int32, (tok, tok), 0) == lax.broadcasted_iota(jnp.int32, (tok, tok), 1)
    )
    unity = jnp.where(unity, 1.0, 0.0).astype(BF16)
    for h in range(2 * heads):
        rows = slice(h * tok, (h + 1) * tok)
        q_rows[rows, HEAD_DIM:] = unity
    for i, slot in enumerate(slots):
        rows = slice(i * pair, (i + 1) * pair)
        for unit in (0, 1):
            keys[unit, rows, :HEAD_DIM] = slot[:, :HEAD_DIM]
        vals[rows, :] = slot[:, HEAD_DIM:]

    begin = lax.div(doc_scalars[first] - base, pair)

    def rows_of(j):
        return pl.ds(pl.multiple_of(j * pair, pair), pair)

    def cols_of(n):
        return slice(n * step_cols, (n + 1) * step_cols)

    def unit_of(n):
        return n * step_cols // width

    def fold(op, x):
        return op(x.reshape(x.shape[0] // 8, 8, x.shape[1]), axis=0)

    stats[0] = jnp.full(stats.shape[1:], -3e38, F32)
    stats[1] = jnp.zeros(stats.shape[1:], F32)
    stats[2] = jnp.zeros(stats.shape[1:], F32)
    dq_cols[...] = jnp.zeros_like(dq_cols)
    t = lax.broadcasted_iota(jnp.int32, (1, tok), 1)
    key_place = lax.broadcasted_iota(jnp.int32, (pair, tok), 0)
    lows = [starts[pl.ds(lax.div(first, 128) + unit, 1), :] for unit in (0, 1)]

    def score_step(j, carry):
        place_j = key_place + (base + j * pair)
        for unit in (0, 1):
            allowed = (place_j >= lows[unit]) & (place_j <= t + (first + unit * tok))
            keys[unit, rows_of(j), HEAD_DIM:] = jnp.where(allowed, 0.0, -1e30).astype(BF16)
        for n in range(n_steps):
            s = dot(keys[unit_of(n), rows_of(j), :], q_rows[cols_of(n), :], NT)
            scores[rows_of(j), cols_of(n)] = s
            stats[0, :, cols_of(n)] = jnp.maximum(stats[0, :, cols_of(n)], fold(jnp.max, s))
        return carry

    lax.fori_loop(begin, n_slots, score_step, 0)
    for n in range(n_steps):
        top = jnp.max(stats[0, :, cols_of(n)], axis=0, keepdims=True)
        stats[0, :, cols_of(n)] = jnp.broadcast_to(top, (8, step_cols))

    def weight_step(j, carry):
        for n in range(n_steps):
            p = jnp.exp2((scores[rows_of(j), cols_of(n)] - stats[0, 0:1, cols_of(n)]) * scale)
            scores[rows_of(j), cols_of(n)] = p
            stats[1, :, cols_of(n)] += fold(jnp.sum, p)
            dweights[rows_of(j), cols_of(n)] = dot(vals[rows_of(j), :], g_rows[cols_of(n), :], NT)
        return carry

    lax.fori_loop(begin, n_slots, weight_step, 0)
    for n in range(n_steps):
        inv = 1.0 / jnp.sum(stats[1, :, cols_of(n)], axis=0, keepdims=True)
        stats[1, :, cols_of(n)] = jnp.broadcast_to(inv, (8, step_cols))

    def value_step(j, carry):
        total = jnp.zeros((pair, HEAD_DIM), F32)
        for n in range(n_steps):
            d = dweights[rows_of(j), cols_of(n)]
            w = scores[rows_of(j), cols_of(n)] * stats[1, 0:1, cols_of(n)]
            wb = w.astype(BF16)
            total = total + dot(wb, g_rows[cols_of(n), :], NN)
            scores[rows_of(j), cols_of(n)] = w
            stats[2, :, cols_of(n)] += fold(jnp.sum, wb.astype(F32) * d)
        acc[rows_of(j), HEAD_DIM:] = total
        return carry

    lax.fori_loop(begin, n_slots, value_step, 0)
    for n in range(n_steps):
        rowdot = jnp.sum(stats[2, :, cols_of(n)], axis=0, keepdims=True)
        stats[2, :, cols_of(n)] = jnp.broadcast_to(rowdot, (8, step_cols))

    def grad_step(j, carry):
        total = jnp.zeros((pair, HEAD_DIM), F32)
        k_cols = keys[0, rows_of(j), :HEAD_DIM].T
        for n in range(n_steps):
            rest = dweights[rows_of(j), cols_of(n)] - stats[2, 0:1, cols_of(n)]
            ds = (scores[rows_of(j), cols_of(n)] * rest).astype(BF16)
            total = total + dot(ds, q_rows[cols_of(n), :HEAD_DIM], NN)
            dq_cols[:, cols_of(n)] += dot(k_cols, ds, NN)
        acc[rows_of(j), :HEAD_DIM] = total * inv_root
        return carry

    lax.fori_loop(begin, n_slots, grad_step, 0)

    for h in range(2 * heads):
        unit, head = h // heads, h % heads
        dq = (dq_cols[:, h * tok : (h + 1) * tok] * inv_root).T
        dq_both[unit, :, head * HEAD_DIM : (head + 1) * HEAD_DIM] = dq.astype(BF16)
    dq_keep[...] = dq_both[y]
    dq_send[...] = dq_both[1 - y]

    for i, out in enumerate(sums):

        @pl.when(i >= begin)
        def _(i=i, out=out):
            out[...] = acc[i * pair : (i + 1) * pair, :].astype(out.dtype)

        @pl.when(i < begin)
        def _(out=out):
            out[...] = jnp.zeros_like(out)


def add_terms(n_out, up, down, terms):
    _, _, z = place()
    for k, term in enumerate(terms, 1):
        value = term[...].astype(F32)
        wrapped = (z + k >= n_out).astype(F32)
        up = up + value * (1.0 - wrapped)
        down = down + value * wrapped
    return up, down


def odd_sum_kernel(n_out, n_terms, own_odd, *refs):
    terms, own_even, (odd_out, even_out) = refs[:n_terms], refs[n_terms:-2], refs[-2:]
    even = own_even[0][...] if own_even else jnp.zeros(even_out.shape, F32)
    odd_out[...], even_out[...] = add_terms(n_out, own_odd[...], even, terms)


def home_kernel(n_out, n_terms, own_even, odd_total, even_total, *refs):
    terms, refs = refs[:n_terms], refs[n_terms:]
    rim, outs, total = refs[:-5], refs[-5:-1], refs[-1]
    tok = own_even.shape[0] // 2
    odd = odd_total[...]
    if rim:
        odd = odd + rim[0][...].astype(F32)
    total[0], total[1] = add_terms(n_out, own_even[...] + even_total[...], odd, terms)
    core, y, _ = place()
    for out, c, yy in zip(outs, (core, 1 - core, core, 1 - core), (y, y, 1 - y, 1 - y)):
        out[...] = total[c, pl.ds(pl.multiple_of(yy * tok, tok), tok), :].astype(out.dtype)


def cross_kernel(odd_keep, odd_got, even_keep, even_got, out):
    core, y, _ = place()
    width = odd_keep.shape[1]
    for c, keep, got in ((0, odd_keep, odd_got), (1, even_keep, even_got)):

        @pl.when(core == c)
        def _(keep=keep, got=got):
            out[:, pl.ds(pl.multiple_of(y * width, 128), width)] = keep[...]
            out[:, pl.ds(pl.multiple_of((1 - y) * width, 128), width)] = got[...]


def finish_kernel(odd_keep, odd_got, even_keep, even_got, crossed, *refs):
    parts, (out, k_out, v_out) = refs[:4], refs[4:]
    core, y, _ = place()
    width = odd_keep.shape[1]

    def columns(quarter, count=1, size=width):
        return pl.ds(pl.multiple_of(quarter * size, 128), count * size)

    for c, keep, got in ((0, even_keep, even_got), (1, odd_keep, odd_got)):

        @pl.when(core == c)
        def _(keep=keep, got=got):
            out[:, columns(2 * core + y)] = keep[...]
            out[:, columns(2 * core + 1 - y)] = got[...]

    out[:, columns(2 * (1 - core), 2)] = crossed[...]
    kv_width = parts[0].shape[1] // 2
    for quarter, part in zip(quarters(), parts):
        k_out[:, columns(quarter, 1, kv_width)] = part[:, :kv_width].astype(BF16)
        v_out[:, columns(quarter, 1, kv_width)] = part[:, kv_width:].astype(BF16)


def body(queries, keys, values, grad_out, doc_ids):
    tok = queries.shape[0]
    n_blk, n_swap = lax.axis_size("blk"), lax.axis_size("swap")
    n_out = n_swap // 2
    seq_blk = tok * n_swap
    pair = 2 * tok
    far = -(-MOST // pair)
    q_width, kv_width = queries.shape[1] // 4, keys.shape[1] // 4
    both = ("swap", "blk")
    devices = [(b, s) for b in range(n_blk) for s in range(n_swap)]

    def index(b, s):
        return s * n_blk + b

    routes = [
        [(index(b, s), index(b ^ 1, s)) for b, s in devices],
        [(index(b, s), index(b, s ^ 1)) for b, s in devices],
        [(index(b, s), index(b ^ 1, s ^ 1)) for b, s in devices],
    ]

    def to_partners(parts):
        return [lax.ppermute(part, both, route) for part, route in zip(parts, routes)]

    def odd_route(k):
        return [(index(b, s), index(b, 2 * ((s // 2 + k) % n_out) + s % 2)) for b, s in devices]

    def even_route(k):
        route = []
        for b, s in devices:
            step, z = divmod(s // 2 + k, n_out)
            if b + 2 * step < n_blk:
                route.append((index(b, s), index(b + 2 * step, 2 * z + s % 2)))
        return route

    def along_z(parts, route_of, back=False):
        got = []
        for k, part in zip(shifts, parts):
            route = route_of(k)
            got.append(lax.ppermute(part, both, [(b, a) for a, b in route] if back else route))
        return got

    def along_x(part, step):
        return lax.ppermute(
            part, "blk", [(b, b + step) for b in range(n_blk) if 0 <= b + step < n_blk]
        )

    def shape(rows, cols, dtype=BF16):
        return jax.ShapeDtypeStruct((rows, cols), dtype)

    def split(a, b, width, groups, name, after=()):
        return vmem_call(
            functools.partial(split_kernel, groups),
            [shape(tok, 8 * width // len(groups))] * len(groups),
            (a, b),
            scratch=[pltpu.SemaphoreType.DMA((8,))],
            hbm=(0, 1),
            after=after,
            name=name,
        )

    shifts = [k for k in range(1, far + 1) if k < n_out]
    whole_ring = far == n_out
    block_shape = shape(pair, 2 * kv_width)
    sum_shape = shape(pair, 2 * kv_width, F32)

    one_each = [lambda numbers, i=i: [numbers[i]] for i in range(4)]
    by_core = [lambda numbers: [numbers[0] // 2 * 2 + i for i in (0, 1)], lambda numbers: [numbers[1] // 2 * 2 + i for i in (0, 1)]]
    kv_parts = split(keys, values, kv_width, one_each, "split_kv")
    kv_recv = to_partners(kv_parts[1:])
    mine, other = split(queries, grad_out, q_width, by_core, "split_qg")
    *made, other = vmem_call(
        functools.partial(payload_kernel, n_out, len(shifts)),
        [block_shape] * (2 + 2 * len(shifts)),
        (kv_parts[0], *kv_recv),
        through=(other,),
        name="payload",
    )
    crossed = lax.ppermute(other, both, routes[0])
    odd_qg, odd_send, even_qg, even_send = vmem_call(
        choose_kernel, [shape(tok, 2 * q_width)] * 4, (mine, crossed), after=(made[0],), name="choose_qg"
    )
    even, odd, *pays = made
    odd_got = along_z(pays[: len(shifts)], odd_route)
    odd_qg = (odd_qg, lax.ppermute(odd_send, both, routes[1]))
    even_got = along_z(pays[len(shifts) :], even_route)
    even_qg = (even_qg, lax.ppermute(even_send, both, routes[1]))
    rim = along_x(odd, 2) if whole_ring else None

    starts = doc_ids.reshape(-1, 128)
    n_slots = far + 1
    rows = 2 * (q_width // HEAD_DIM) * tok
    sum_shapes = [
        sum_shape if i == far or (i == 0 and whole_ring and which) else block_shape
        for which in (0, 1)
        for i in range(n_slots)
    ]

    def attend(which, slots, qg, after=()):
        return vmem_call(
            functools.partial(attend_kernel, which, n_slots, seq_blk),
            [shape(tok, q_width)] * 2 + sum_shapes[which * n_slots : (which + 1) * n_slots],
            (*qg, starts, doc_ids, *slots),
            scratch=[
                pltpu.VMEM((rows, 2 * HEAD_DIM), BF16),
                pltpu.VMEM((rows, HEAD_DIM), BF16),
                pltpu.VMEM((2, n_slots * pair, 2 * HEAD_DIM), BF16),
                pltpu.VMEM((n_slots * pair, HEAD_DIM), BF16),
                pltpu.VMEM((n_slots * pair, rows), F32),
                pltpu.VMEM((n_slots * pair, rows), F32),
                pltpu.VMEM((HEAD_DIM, rows), F32),
                pltpu.VMEM((n_slots * pair, 2 * HEAD_DIM), F32),
                pltpu.VMEM((3, 8, rows), F32),
                pltpu.VMEM((2, tok, q_width), BF16),
            ],
            smem=(3,),
            after=after,
            mib=32,
            flops=6_000_000_000,
            name="attend_odd" if which else "attend_even",
        )

    def slots_of(up, down, got):
        return [down if k == n_out else got[k - 1] for k in range(far, 0, -1)] + [up]

    def sent(sums):
        return [sums[far - k] for k in shifts]

    dq_odd, dq_odd_send, *odd_sums = attend(1, slots_of(odd, even, odd_got), odd_qg)
    odd_back = along_z(sent(odd_sums), odd_route, back=True)
    dq_even, dq_send, *even_sums = attend(0, slots_of(even, rim, even_got), even_qg, (dq_odd,))
    dq_odd_got = lax.ppermute(dq_odd_send, both, routes[1])
    odd_total, even_total, dq_send, *even_sent = vmem_call(
        functools.partial(odd_sum_kernel, n_out, len(shifts)),
        [sum_shape, sum_shape],
        (odd_sums[far], *odd_back, *([odd_sums[0]] if whole_ring else [])),
        after=(dq_odd_got,),
        through=[dq_send, *sent(even_sums)],
        name="odd_sum",
    )
    dq_even_got = lax.ppermute(dq_send, both, routes[1])
    even_back = along_z(even_sent, even_route, back=True)
    rim_home = (along_x(even_sums[0], -2),) if whole_ring else ()
    home = vmem_call(
        functools.partial(home_kernel, n_out, len(shifts)),
        [shape(tok, 2 * kv_width, F32)] + [shape(tok, 2 * kv_width)] * 3,
        (even_sums[far], odd_total, even_total, *even_back, *rim_home),
        scratch=[pltpu.VMEM((2, pair, 2 * kv_width), F32)],
        name="home",
    )
    kv_home = to_partners(home[1:])
    dq_parts = (dq_odd, dq_odd_got, dq_even, dq_even_got)
    (dq_cross,) = vmem_call(cross_kernel, [shape(tok, 2 * q_width)], dq_parts, after=(home[0],), name="cross")
    return vmem_call(
        finish_kernel,
        [shape(*queries.shape), shape(*keys.shape), shape(*values.shape)],
        (*dq_parts, lax.ppermute(dq_cross, both, routes[0]), home[0], *kv_home),
        name="finish",
    )


def solution(mesh):
    spec = P(("blk", "swap"), None)
    return jax.shard_map(
        lambda *args: tuple(body(*args)),
        mesh=mesh,
        in_specs=(spec, spec, spec, spec, P()),
        out_specs=(spec, spec, spec),
        check_vma=False,
    )
```

time: 89.4 us -> 85.7 us (0.959); the launches traced: 89 us -> 84.3 us
  waiting for transfers between devices: 31.5 us -> 16.2 us
  starting transfers between devices: 33.3 us -> 39.9 us
  Pallas kernels: 19.2 us -> 22.9 us
    ppermute x12 -> x18, starting transfers between devices: 11.3 us -> 32.8 us  [the longest x12 21.2 us: along_z(): lax.ppermute(part, both, [(b, a) for a, b in route] if back else route)]
    ppermute x12 -> x18, waiting for transfers between devices: 21.4 us -> 11.5 us  [the longest x12 9.13 us: along_z(): lax.ppermute(part, both, [(b, a) for a, b in route] if back else route)]
    ppermute x2, starting transfers between devices: 10 us -> 2.57 us  [along_x(): lax.ppermute(part, 'blk', [(b, b + step) for b in range(n_blk) if 0 <= b...]
    ppermute x12 -> x6, starting transfers between devices: 11.9 us -> 4.59 us  [to_partners(): lax.ppermute(part, both, route)]
    ppermute x2, waiting for transfers between devices: 5.65 us -> 0.01 us  [along_x(): lax.ppermute(part, 'blk', [(b, b + step) for b in range(n_blk) if 0 <= b...]
    pallas_call x9 -> x10, Pallas kernels: 19.2 us -> 22.9 us  [vmem_call(): pl.pallas_call(run, out_shape=list(out_shapes) + [jax.ShapeDtypeStruct(t....]
    ppermute x12 -> x6, waiting for transfers between devices: 4.43 us -> 4.75 us  [to_partners(): lax.ppermute(part, both, route)]
  transfers between devices with their start and end apart: 26 -> 26, of which waited for: 8 -> 8; matrix products, arithmetic and copies ran while one was open for 0% -> 0% of each run, Pallas kernels for 20% -> 25%
where the time goes in v2:
time: 85.7 us; the launch traced here: 84.3 us
  starting transfers between devices  39.9 us (47%)
  Pallas kernels  22.9 us (27%)
  waiting for transfers between devices  16.2 us (19%)
  local copies, waits for them, and re-layouts  4.26 us (5%)
  between operations  0.91 us (1%)
    pallas_call x10, Pallas kernels, vmem_call(): pl.pallas_call(run, out_shape=list(out_shapes) + [jax.ShapeDtypeStruct(t....  22.9 us
    ppermute x12, starting transfers between devices, along_z(): lax.ppermute(part, both, [(b, a) for a, b in route] if back else route)  21.2 us
    ppermute x12, waiting for transfers between devices, along_z(): lax.ppermute(part, both, [(b, a) for a, b in route] if back else route)  9.13 us
    ppermute x1, starting transfers between devices, body(): lax.ppermute(dq_cross, both, routes[0])  8.01 us
    ppermute x6, waiting for transfers between devices, to_partners(): lax.ppermute(part, both, route)  4.75 us
    ppermute x6, starting transfers between devices, to_partners(): lax.ppermute(part, both, route)  4.59 us
    unnamed x10, local copies, waits for them, and re-layouts  4.26 us
    ppermute x2, starting transfers between devices, along_x(): lax.ppermute(part, 'blk', [(b, b + step) for b in range(n_blk) if 0 <= b...  2.57 us
  transfers between devices with their start and end apart: 26, of which 8 were waited for; matrix products, arithmetic and copies ran while one was open for 0% of the time, Pallas kernels for 25%

profile of v2, /device:TPU:3, one launch (start us, length us, event | category | flops | bytes accessed | tf_op | source)
XLA Modules:
  0.0 84.3 jit_solution(3973226799334335671)
XLA Ops:
  0.6 0.9 %copy-done.2 = bf16[128,512]{1,0:T(8,128)(2,1)S(1)} copy-done((bf16[128,512]{1,0:T(8,128)(2,1)S(1)}, bf16[128,512]{1,0:T(8,128)(2,1)}, u32[]{:S(2)}) %copy-start.2) | copy-done | bytes 131096
  1.5 0.9 %copy-done.3 = bf16[128,512]{1,0:T(8,128)(2,1)S(1)} copy-done((bf16[128,512]{1,0:T(8,128)(2,1)S(1)}, bf16[128,512]{1,0:T(8,128)(2,1)}, u32[]{:S(2)}) %copy-start.3) | copy-done | bytes 131096
  2.4 0.1 split_kv.1
  2.6 0.7 collective-permute-start
  3.3 1.3 %collective-permute-start.1 = (bf16[128,256]{1,0:T(8,128)(2,1)S(1)}, bf16[128,256]{1,0:T(8,128)(2,1)S(1)}, u32[]{:S(2)}, u32[]{:S(2)}) collective-permute-start(bf16[128,256]{1,0:T(8,128)(2,1)S(1)} %get-tuple-element.49), channel_id=1, source_target_pairs={{0,4},{4,0},{8,12},{12,8},{16,20},{20,16},{24,28},{28,24},{1,5},{5... | collective-permute-start | bytes 196616 | tf_op jit(solution)/shard_map/ppermute | solution.py:353
  4.6 0.5 collective-permute-start.2
  5.0 1.2 %copy-done = bf16[128,4096]{1,0:T(8,128)(2,1)S(1)} copy-done((bf16[128,4096]{1,0:T(8,128)(2,1)S(1)}, bf16[128,4096]{1,0:T(8,128)(2,1)}, u32[]{:S(2)}) %copy-start) | copy-done | bytes 1048600
  6.3 1.2 %copy-done.1 = bf16[128,4096]{1,0:T(8,128)(2,1)S(1)} copy-done((bf16[128,4096]{1,0:T(8,128)(2,1)S(1)}, bf16[128,4096]{1,0:T(8,128)(2,1)}, u32[]{:S(2)}) %copy-start.1) | copy-done | bytes 1048600
  7.5 0.2 split_qg.1
  7.7 0.0 collective-permute-done.1.refs_2_
  7.8 0.9 %collective-permute-done.2.refs_3_ = bf16[128,256]{1,0:T(8,128)(2,1)S(1)} collective-permute-done((bf16[128,256]{1,0:T(8,128)(2,1)S(1)}, bf16[128,256]{1,0:T(8,128)(2,1)S(1)}, u32[]{:S(2)}, u32[]{:S(2)}) %collective-permute-start.2) | collective-permute-done | bytes 65568 | tf_op jit(solution)/shard_map/ppermute | solution.py:353
  8.6 0.1 payload.1
  8.7 0.4 collective-permute-start.3
  9.2 2.3 %collective-permute-done.3.refs_1_ = bf16[128,4096]{1,0:T(8,128)(2,1)S(1)} collective-permute-done((bf16[128,4096]{1,0:T(8,128)(2,1)S(1)}, bf16[128,4096]{1,0:T(8,128)(2,1)S(1)}, u32[]{:S(2)}, u32[]{:S(2)}) %collective-permute-start.3) | collective-permute-done | bytes 1048608 | tf_op jit(solution)/shard_map/ppermute | solution.py:409
  11.5 0.2 choose_qg.1
  11.6 0.0 copy-start.4
  11.6 1.2 %collective-permute-start.4 = (bf16[128,2048]{1,0:T(8,128)(2,1)S(1)}, bf16[128,2048]{1,0:T(8,128)(2,1)S(1)}, u32[]{:S(2)}, u32[]{:S(2)}) collective-permute-start(bf16[128,2048]{1,0:T(8,128)(2,1)S(1)} %get-tuple-element.55), channel_id=1, source_target_pairs={{0,4},{4,0},{8,12},{12,8},{16,20},{20,16},{24,28},{28,24},{1,5},{5... | collective-permute-start | bytes 1572872 | tf_op jit(solution)/shard_map/ppermute | solution.py:415
  12.9 3.3 %collective-permute-start.5 = (bf16[256,256]{1,0:T(8,128)(2,1)S(1)}, bf16[256,256]{1,0:T(8,128)(2,1)S(1)}, u32[]{:S(2)}, u32[]{:S(2)}) collective-permute-start(bf16[256,256]{1,0:T(8,128)(2,1)S(1)} %get-tuple-element.56), channel_id=1, source_target_pairs={{0,24},{4,28},{8,0},{12,4},{16,8},{20,12},{24,16},{28,20},{1,25},{... | collective-permute-start | bytes 393224 | tf_op jit(solution)/shard_map/ppermute | solution.py:370
  16.2 0.5 collective-permute-start.7
  16.7 1.3 %collective-permute-start.10 = (bf16[256,256]{1,0:T(8,128)(2,1)S(1)}, bf16[256,256]{1,0:T(8,128)(2,1)S(1)}, u32[]{:S(2)}, u32[]{:S(2)}) collective-permute-start(bf16[256,256]{1,0:T(8,128)(2,1)S(1)} %get-tuple-element.59.refs_8_), channel_id=1, source_target_pairs={{0,2},{1,3},{4,6},{5,7},{8,10},{9,11},{12,14},{13,15},{16,18},{17,... | collective-permute-start | bytes 393224 | tf_op jit(solution)/shard_map/ppermute | solution.py:374
  17.9 0.7 collective-permute-done.5.refs_5_
  18.6 5.9 %collective-permute-start.11 = (bf16[256,256]{1,0:T(8,128)(2,1)S(1)}, bf16[256,256]{1,0:T(8,128)(2,1)S(1)}, u32[]{:S(2)}, u32[]{:S(2)}) collective-permute-start(bf16[256,256]{1,0:T(8,128)(2,1)S(1)} %get-tuple-element.64), channel_id=1, source_target_pairs={{0,24},{4,28},{8,2},{12,6},{16,10},{20,14},{24,18},{28,22},{1,25},... | collective-permute-start | bytes 393224 | tf_op jit(solution)/shard_map/ppermute | solution.py:370
  24.5 2.9 %collective-permute-done.6.refs_6_ = bf16[256,256]{1,0:T(8,128)(2,1)S(1)} collective-permute-done((bf16[256,256]{1,0:T(8,128)(2,1)S(1)}, bf16[256,256]{1,0:T(8,128)(2,1)S(1)}, u32[]{:S(2)}, u32[]{:S(2)}) %collective-permute-start.6) | collective-permute-done | bytes 131104 | tf_op jit(solution)/shard_map/ppermute | solution.py:370
  27.4 1.9 %collective-permute-start.12 = (bf16[256,256]{1,0:T(8,128)(2,1)S(1)}, bf16[256,256]{1,0:T(8,128)(2,1)S(1)}, u32[]{:S(2)}, u32[]{:S(2)}) collective-permute-start(bf16[256,256]{1,0:T(8,128)(2,1)S(1)} %get-tuple-element.65), channel_id=1, source_target_pairs={{0,16},{4,20},{8,24},{12,28},{16,2},{20,6},{24,10},{28,14},{1,17},... | collective-permute-start | bytes 393224 | tf_op jit(solution)/shard_map/ppermute | solution.py:370
  29.3 2.3 %collective-permute-start.13 = (bf16[256,256]{1,0:T(8,128)(2,1)S(1)}, bf16[256,256]{1,0:T(8,128)(2,1)S(1)}, u32[]{:S(2)}, u32[]{:S(2)}) collective-permute-start(bf16[256,256]{1,0:T(8,128)(2,1)S(1)} %get-tuple-element.66), channel_id=1, source_target_pairs={{0,8},{4,12},{8,16},{12,20},{16,24},{20,28},{24,2},{28,6},{1,9},{5... | collective-permute-start | bytes 393224 | tf_op jit(solution)/shard_map/ppermute | solution.py:370
  31.7 0.3 collective-permute-start.9
  32.0 12.4 %attend_odd.1 = (bf16[128,1024]{1,0:T(8,128)(2,1)S(1)}, bf16[128,1024]{1,0:T(8,128)(2,1)S(1)}, f32[256,256]{1,0:T(8,128)S(1)}, bf16[256,256]{1,0:T(8,128)(2,1)S(...) custom-call(bf16[128,2048]{1,0:T(8,128)(2,1)S(1)} %get-tuple-element.54.refs_0_, ...), custom_call_target="tpu_custom_call" | custom-call | flops 6000000000 | tf_op jit(solution)/shard_map/attend_odd/pallas_call | solution.py:41
  44.5 1.3 %collective-permute-start.8 = (bf16[128,1024]{1,0:T(8,128)(2,1)S(1)}, bf16[128,1024]{1,0:T(8,128)(2,1)S(1)}, u32[]{:S(2)}, u32[]{:S(2)}) collective-permute-start(bf16[128,1024]{1,0:T(8,128)(2,1)S(1)} %get-tuple-element.61), channel_id=1, source_target_pairs={{0,4},{4,0},{8,12},{12,8},{16,20},{20,16},{24,28},{28,24},{1,5},{5... | collective-permute-start | bytes 786440 | tf_op jit(solution)/shard_map/ppermute | solution.py:462
  45.8 0.1 collective-permute-start.15
  45.9 1.4 %collective-permute-start.16 = (bf16[256,256]{1,0:T(8,128)(2,1)S(1)}, bf16[256,256]{1,0:T(8,128)(2,1)S(1)}, u32[]{:S(2)}, u32[]{:S(2)}) collective-permute-start(bf16[256,256]{1,0:T(8,128)(2,1)S(1)} %get-tuple-element.71), channel_id=1, source_target_pairs={{24,0},{28,4},{0,8},{4,12},{8,16},{12,20},{16,24},{20,28},{25,1},{... | collective-permute-start | bytes 393224 | tf_op jit(solution)/shard_map/ppermute | solution.py:370
  47.3 8.2 %attend_even.1 = (bf16[128,1024]{1,0:T(8,128)(2,1)S(1)}, bf16[128,1024]{1,0:T(8,128)(2,1)S(1)}, bf16[256,256]{1,0:T(8,128)(2,1)S(1)}, bf16[256,256]{1,0:T(8,128)...) custom-call(bf16[128,2048]{1,0:T(8,128)(2,1)S(1)} %get-tuple-element.62.refs_0_, ...), custom_call_target="tpu_custom_call" | custom-call | flops 6000000000 | tf_op jit(solution)/shard_map/attend_even/pallas_call | solution.py:41
  55.5 0.2 odd_sum.1
  55.7 0.3 collective-permute-start.17
  56.1 1.3 %collective-permute-start.21 = (bf16[256,256]{1,0:T(8,128)(2,1)S(1)}, bf16[256,256]{1,0:T(8,128)(2,1)S(1)}, u32[]{:S(2)}, u32[]{:S(2)}) collective-permute-start(bf16[256,256]{1,0:T(8,128)(2,1)S(1)} %get-tuple-element.84), channel_id=1, source_target_pairs={{2,0},{3,1},{6,4},{7,5},{10,8},{11,9},{14,12},{15,13},{18,16},{19,... | collective-permute-start | bytes 393224 | tf_op jit(solution)/shard_map/ppermute | solution.py:374
  57.3 1.9 %collective-permute-start.18 = (bf16[256,256]{1,0:T(8,128)(2,1)S(1)}, bf16[256,256]{1,0:T(8,128)(2,1)S(1)}, u32[]{:S(2)}, u32[]{:S(2)}) collective-permute-start(bf16[256,256]{1,0:T(8,128)(2,1)S(1)} %get-tuple-element.81), channel_id=1, source_target_pairs={{8,0},{12,4},{16,8},{20,12},{24,16},{28,20},{2,24},{6,28},{9,1},{1... | collective-permute-start | bytes 393224 | tf_op jit(solution)/shard_map/ppermute | solution.py:370
  59.3 1.9 %collective-permute-start.19 = (bf16[256,256]{1,0:T(8,128)(2,1)S(1)}, bf16[256,256]{1,0:T(8,128)(2,1)S(1)}, u32[]{:S(2)}, u32[]{:S(2)}) collective-permute-start(bf16[256,256]{1,0:T(8,128)(2,1)S(1)} %get-tuple-element.82), channel_id=1, source_target_pairs={{16,0},{20,4},{24,8},{28,12},{2,16},{6,20},{10,24},{14,28},{17,1},... | collective-permute-start | bytes 393224 | tf_op jit(solution)/shard_map/ppermute | solution.py:370
  61.2 1.9 %collective-permute-start.20 = (bf16[256,256]{1,0:T(8,128)(2,1)S(1)}, bf16[256,256]{1,0:T(8,128)(2,1)S(1)}, u32[]{:S(2)}, u32[]{:S(2)}) collective-permute-start(bf16[256,256]{1,0:T(8,128)(2,1)S(1)} %get-tuple-element.83), channel_id=1, source_target_pairs={{24,0},{28,4},{2,8},{6,12},{10,16},{14,20},{18,24},{22,28},{25,1},... | collective-permute-start | bytes 393224 | tf_op jit(solution)/shard_map/ppermute | solution.py:370
  63.2 4.1 %collective-permute-done.19.refs_4_ = bf16[256,256]{1,0:T(8,128)(2,1)S(1)} collective-permute-done((bf16[256,256]{1,0:T(8,128)(2,1)S(1)}, bf16[256,256]{1,0:T(8,128)(2,1)S(1)}, u32[]{:S(2)}, u32[]{:S(2)}) %collective-permute-start.19) | collective-permute-done | bytes 131104 | tf_op jit(solution)/shard_map/ppermute | solution.py:370
  67.3 1.4 %collective-permute-done.20.refs_5_ = bf16[256,256]{1,0:T(8,128)(2,1)S(1)} collective-permute-done((bf16[256,256]{1,0:T(8,128)(2,1)S(1)}, bf16[256,256]{1,0:T(8,128)(2,1)S(1)}, u32[]{:S(2)}, u32[]{:S(2)}) %collective-permute-start.20) | collective-permute-done | bytes 131104 | tf_op jit(solution)/shard_map/ppermute | solution.py:370
  68.7 0.3 home.1
  69.0 0.1 cross.1
  69.1 8.0 %collective-permute-start.22 = (bf16[128,2048]{1,0:T(8,128)(2,1)S(1)}, bf16[128,2048]{1,0:T(8,128)(2,1)S(1)}, u32[]{:S(2)}, u32[]{:S(2)}) collective-permute-start(bf16[128,2048]{1,0:T(8,128)(2,1)S(1)} %cross.1), channel_id=1, source_target_pairs={{0,1},{4,5},{8,9},{12,13},{16,17},{20,21},{24,25},{28,29},{1,0},{5... | collective-permute-start | bytes 1572872 | tf_op jit(solution)/shard_map/ppermute | solution.py:487
  77.1 0.1 collective-permute-start.23
  77.2 1.3 %collective-permute-start.24 = (bf16[128,256]{1,0:T(8,128)(2,1)S(1)}, bf16[128,256]{1,0:T(8,128)(2,1)S(1)}, u32[]{:S(2)}, u32[]{:S(2)}) collective-permute-start(bf16[128,256]{1,0:T(8,128)(2,1)S(1)} %get-tuple-element.87), channel_id=1, source_target_pairs={{0,4},{4,0},{8,12},{12,8},{16,20},{20,16},{24,28},{28,24},{1,5},{5... | collective-permute-start | bytes 196616 | tf_op jit(solution)/shard_map/ppermute | solution.py:353
  78.4 0.8 collective-permute-start.25
  79.2 1.0 %collective-permute-done.24.refs_7_ = bf16[128,256]{1,0:T(8,128)(2,1)S(1)} collective-permute-done((bf16[128,256]{1,0:T(8,128)(2,1)S(1)}, bf16[128,256]{1,0:T(8,128)(2,1)S(1)}, u32[]{:S(2)}, u32[]{:S(2)}) %collective-permute-start.24) | collective-permute-done | bytes 65568 | tf_op jit(solution)/shard_map/ppermute | solution.py:353
  80.3 2.8 %collective-permute-done.25.refs_8_ = bf16[128,256]{1,0:T(8,128)(2,1)S(1)} collective-permute-done((bf16[128,256]{1,0:T(8,128)(2,1)S(1)}, bf16[128,256]{1,0:T(8,128)(2,1)S(1)}, u32[]{:S(2)}, u32[]{:S(2)}) %collective-permute-start.25) | collective-permute-done | bytes 65568 | tf_op jit(solution)/shard_map/ppermute | solution.py:353
  83.1 1.2 %finish.1 = (bf16[128,4096]{1,0:T(8,128)(2,1)}, bf16[128,512]{1,0:T(8,128)(2,1)}, bf16[128,512]{1,0:T(8,128)(2,1)}) custom-call(bf16[128,1024]{1,0:T(8,128)(2,1)S(1)} %get-tuple-element.60.refs_9_.refs_0_, bf16[128,1024]{1,0:T(8,128)(2,1)S(1)} %collective-permute-done.8.refs_5_.refs_1_, bf16[128,1024]{1,0:T(8,128)(2,1)S(1)} %get-tuple-element.67.refs_2_, ...), custom_call_target="tpu_custom_call" | custom-call | tf_op jit(solution)/shard_map/finish/pallas_call | solution.py:41
  (24 shorter events, 0.1 us)
Async XLA Ops:
  0.6 0.9 %copy-start.2 = (bf16[128,512]{1,0:T(8,128)(2,1)S(1)}, bf16[128,512]{1,0:T(8,128)(2,1)}, u32[]{:S(2)}) copy-start(bf16[128,512]{1,0:T(8,128)(2,1)} %refs_0_.3) | copy-start | bytes 393220
  1.5 0.9 %copy-start.3 = (bf16[128,512]{1,0:T(8,128)(2,1)S(1)}, bf16[128,512]{1,0:T(8,128)(2,1)}, u32[]{:S(2)}) copy-start(bf16[128,512]{1,0:T(8,128)(2,1)} %refs_1_.3) | copy-start | bytes 393220
  2.6 5.1 %collective-permute-start = (bf16[128,256]{1,0:T(8,128)(2,1)S(1)}, bf16[128,256]{1,0:T(8,128)(2,1)S(1)}, u32[]{:S(2)}, u32[]{:S(2)}) collective-permute-start(bf16[128,256]{1,0:T(8,128)(2,1)S(1)} %get-tuple-element.48), channel_id=1, source_target_pairs={{0,1},{4,5},{8,9},{12,13},{16,17},{20,21},{24,25},{28,29},{1,0},{5... | collective-permute-start | bytes 196616 | tf_op jit(solution)/shard_map/ppermute | solution.py:353
  3.3 4.4 %collective-permute-start.1 = (bf16[128,256]{1,0:T(8,128)(2,1)S(1)}, bf16[128,256]{1,0:T(8,128)(2,1)S(1)}, u32[]{:S(2)}, u32[]{:S(2)}) collective-permute-start(bf16[128,256]{1,0:T(8,128)(2,1)S(1)} %get-tuple-element.49), channel_id=1, source_target_pairs={{0,4},{4,0},{8,12},{12,8},{16,20},{20,16},{24,28},{28,24},{1,5},{5... | collective-permute-start | bytes 196616 | tf_op jit(solution)/shard_map/ppermute | solution.py:353
  4.6 4.0 %collective-permute-start.2 = (bf16[128,256]{1,0:T(8,128)(2,1)S(1)}, bf16[128,256]{1,0:T(8,128)(2,1)S(1)}, u32[]{:S(2)}, u32[]{:S(2)}) collective-permute-start(bf16[128,256]{1,0:T(8,128)(2,1)S(1)} %get-tuple-element.50), channel_id=1, source_target_pairs={{0,5},{4,1},{8,13},{12,9},{16,21},{20,17},{24,29},{28,25},{1,4},{5... | collective-permute-start | bytes 196616 | tf_op jit(solution)/shard_map/ppermute | solution.py:353
  5.0 1.2 %copy-start = (bf16[128,4096]{1,0:T(8,128)(2,1)S(1)}, bf16[128,4096]{1,0:T(8,128)(2,1)}, u32[]{:S(2)}) copy-start(bf16[128,4096]{1,0:T(8,128)(2,1)} %refs_0_.2) | copy-start | bytes 3145732
  6.3 1.2 %copy-start.1 = (bf16[128,4096]{1,0:T(8,128)(2,1)S(1)}, bf16[128,4096]{1,0:T(8,128)(2,1)}, u32[]{:S(2)}) copy-start(bf16[128,4096]{1,0:T(8,128)(2,1)} %refs_1_.2) | copy-start | bytes 3145732
  8.7 2.7 %collective-permute-start.3 = (bf16[128,4096]{1,0:T(8,128)(2,1)S(1)}, bf16[128,4096]{1,0:T(8,128)(2,1)S(1)}, u32[]{:S(2)}, u32[]{:S(2)}) collective-permute-start(bf16[128,4096]{1,0:T(8,128)(2,1)S(1)} %get-tuple-element.52), channel_id=1, source_target_pairs={{0,1},{4,5},{8,9},{12,13},{16,17},{20,21},{24,25},{28,29},{1,0},{5... | collective-permute-start | bytes 3145736 | tf_op jit(solution)/shard_map/ppermute | solution.py:409
  11.6 20.4 %copy-start.4 = (s32[4096]{0:T(1024)S(1)}, s32[4096]{0:T(1024)}, u32[]{:S(2)}) copy-start(s32[4096]{0:T(1024)} %refs_3_.3) | copy-start | bytes 49156
  11.6 20.0 %collective-permute-start.4 = (bf16[128,2048]{1,0:T(8,128)(2,1)S(1)}, bf16[128,2048]{1,0:T(8,128)(2,1)S(1)}, u32[]{:S(2)}, u32[]{:S(2)}) collective-permute-start(bf16[128,2048]{1,0:T(8,128)(2,1)S(1)} %get-tuple-element.55), channel_id=1, source_target_pairs={{0,4},{4,0},{8,12},{12,8},{16,20},{20,16},{24,28},{28,24},{1,5},{5... | collective-permute-start | bytes 1572872 | tf_op jit(solution)/shard_map/ppermute | solution.py:415
  12.9 5.7 %collective-permute-start.5 = (bf16[256,256]{1,0:T(8,128)(2,1)S(1)}, bf16[256,256]{1,0:T(8,128)(2,1)S(1)}, u32[]{:S(2)}, u32[]{:S(2)}) collective-permute-start(bf16[256,256]{1,0:T(8,128)(2,1)S(1)} %get-tuple-element.56), channel_id=1, source_target_pairs={{0,24},{4,28},{8,0},{12,4},{16,8},{20,12},{24,16},{28,20},{1,25},{... | collective-permute-start | bytes 393224 | tf_op jit(solution)/shard_map/ppermute | solution.py:370
  16.2 11.2 %collective-permute-start.6 = (bf16[256,256]{1,0:T(8,128)(2,1)S(1)}, bf16[256,256]{1,0:T(8,128)(2,1)S(1)}, u32[]{:S(2)}, u32[]{:S(2)}) collective-permute-start(bf16[256,256]{1,0:T(8,128)(2,1)S(1)} %get-tuple-element.57), channel_id=1, source_target_pairs={{0,16},{4,20},{8,24},{12,28},{16,0},{20,4},{24,8},{28,12},{1,17},{... | collective-permute-start | bytes 393224 | tf_op jit(solution)/shard_map/ppermute | solution.py:370
  16.2 13.1 %collective-permute-start.7 = (bf16[256,256]{1,0:T(8,128)(2,1)S(1)}, bf16[256,256]{1,0:T(8,128)(2,1)S(1)}, u32[]{:S(2)}, u32[]{:S(2)}) collective-permute-start(bf16[256,256]{1,0:T(8,128)(2,1)S(1)} %get-tuple-element.58), channel_id=1, source_target_pairs={{0,8},{4,12},{8,16},{12,20},{16,24},{20,28},{24,0},{28,4},{1,9},{5... | collective-permute-start | bytes 393224 | tf_op jit(solution)/shard_map/ppermute | solution.py:370
  16.7 27.8 %collective-permute-start.10 = (bf16[256,256]{1,0:T(8,128)(2,1)S(1)}, bf16[256,256]{1,0:T(8,128)(2,1)S(1)}, u32[]{:S(2)}, u32[]{:S(2)}) collective-permute-start(bf16[256,256]{1,0:T(8,128)(2,1)S(1)} %get-tuple-element.59.refs_8_), channel_id=1, source_target_pairs={{0,2},{1,3},{4,6},{5,7},{8,10},{9,11},{12,14},{13,15},{16,18},{17,... | collective-permute-start | bytes 393224 | tf_op jit(solution)/shard_map/ppermute | solution.py:374
  18.6 27.1 %collective-permute-start.11 = (bf16[256,256]{1,0:T(8,128)(2,1)S(1)}, bf16[256,256]{1,0:T(8,128)(2,1)S(1)}, u32[]{:S(2)}, u32[]{:S(2)}) collective-permute-start(bf16[256,256]{1,0:T(8,128)(2,1)S(1)} %get-tuple-element.64), channel_id=1, source_target_pairs={{0,24},{4,28},{8,2},{12,6},{16,10},{20,14},{24,18},{28,22},{1,25},... | collective-permute-start | bytes 393224 | tf_op jit(solution)/shard_map/ppermute | solution.py:370
  27.4 18.4 %collective-permute-start.12 = (bf16[256,256]{1,0:T(8,128)(2,1)S(1)}, bf16[256,256]{1,0:T(8,128)(2,1)S(1)}, u32[]{:S(2)}, u32[]{:S(2)}) collective-permute-start(bf16[256,256]{1,0:T(8,128)(2,1)S(1)} %get-tuple-element.65), channel_id=1, source_target_pairs={{0,16},{4,20},{8,24},{12,28},{16,2},{20,6},{24,10},{28,14},{1,17},... | collective-permute-start | bytes 393224 | tf_op jit(solution)/shard_map/ppermute | solution.py:370
  29.3 16.5 %collective-permute-start.13 = (bf16[256,256]{1,0:T(8,128)(2,1)S(1)}, bf16[256,256]{1,0:T(8,128)(2,1)S(1)}, u32[]{:S(2)}, u32[]{:S(2)}) collective-permute-start(bf16[256,256]{1,0:T(8,128)(2,1)S(1)} %get-tuple-element.66), channel_id=1, source_target_pairs={{0,8},{4,12},{8,16},{12,20},{16,24},{20,28},{24,2},{28,6},{1,9},{5... | collective-permute-start | bytes 393224 | tf_op jit(solution)/shard_map/ppermute | solution.py:370
  31.7 15.6 %collective-permute-start.9 = (bf16[128,2048]{1,0:T(8,128)(2,1)S(1)}, bf16[128,2048]{1,0:T(8,128)(2,1)S(1)}, u32[]{:S(2)}, u32[]{:S(2)}) collective-permute-start(bf16[128,2048]{1,0:T(8,128)(2,1)S(1)} %get-tuple-element.63), channel_id=1, source_target_pairs={{0,4},{4,0},{8,12},{12,8},{16,20},{20,16},{24,28},{28,24},{1,5},{5... | collective-permute-start | bytes 1572872 | tf_op jit(solution)/shard_map/ppermute | solution.py:417
  44.5 11.1 %collective-permute-start.8 = (bf16[128,1024]{1,0:T(8,128)(2,1)S(1)}, bf16[128,1024]{1,0:T(8,128)(2,1)S(1)}, u32[]{:S(2)}, u32[]{:S(2)}) collective-permute-start(bf16[128,1024]{1,0:T(8,128)(2,1)S(1)} %get-tuple-element.61), channel_id=1, source_target_pairs={{0,4},{4,0},{8,12},{12,8},{16,20},{20,16},{24,28},{28,24},{1,5},{5... | collective-permute-start | bytes 786440 | tf_op jit(solution)/shard_map/ppermute | solution.py:462
  45.8 9.7 %collective-permute-start.14 = (bf16[256,256]{1,0:T(8,128)(2,1)S(1)}, bf16[256,256]{1,0:T(8,128)(2,1)S(1)}, u32[]{:S(2)}, u32[]{:S(2)}) collective-permute-start(bf16[256,256]{1,0:T(8,128)(2,1)S(1)} %get-tuple-element.69), channel_id=1, source_target_pairs={{8,0},{12,4},{16,8},{20,12},{24,16},{28,20},{0,24},{4,28},{9,1},{1... | collective-permute-start | bytes 393224 | tf_op jit(solution)/shard_map/ppermute | solution.py:370
  45.8 9.8 %collective-permute-start.15 = (bf16[256,256]{1,0:T(8,128)(2,1)S(1)}, bf16[256,256]{1,0:T(8,128)(2,1)S(1)}, u32[]{:S(2)}, u32[]{:S(2)}) collective-permute-start(bf16[256,256]{1,0:T(8,128)(2,1)S(1)} %get-tuple-element.70), channel_id=1, source_target_pairs={{16,0},{20,4},{24,8},{28,12},{0,16},{4,20},{8,24},{12,28},{17,1},{... | collective-permute-start | bytes 393224 | tf_op jit(solution)/shard_map/ppermute | solution.py:370
  45.9 9.7 %collective-permute-start.16 = (bf16[256,256]{1,0:T(8,128)(2,1)S(1)}, bf16[256,256]{1,0:T(8,128)(2,1)S(1)}, u32[]{:S(2)}, u32[]{:S(2)}) collective-permute-start(bf16[256,256]{1,0:T(8,128)(2,1)S(1)} %get-tuple-element.71), channel_id=1, source_target_pairs={{24,0},{28,4},{0,8},{4,12},{8,16},{12,20},{16,24},{20,28},{25,1},{... | collective-permute-start | bytes 393224 | tf_op jit(solution)/shard_map/ppermute | solution.py:370
  55.7 13.3 %collective-permute-start.17 = (bf16[128,1024]{1,0:T(8,128)(2,1)S(1)}, bf16[128,1024]{1,0:T(8,128)(2,1)S(1)}, u32[]{:S(2)}, u32[]{:S(2)}) collective-permute-start(bf16[128,1024]{1,0:T(8,128)(2,1)S(1)} %get-tuple-element.77), channel_id=1, source_target_pairs={{0,4},{4,0},{8,12},{12,8},{16,20},{20,16},{24,28},{28,24},{1,5},{5... | collective-permute-start | bytes 786440 | tf_op jit(solution)/shard_map/ppermute | solution.py:471
  56.1 7.1 %collective-permute-start.21 = (bf16[256,256]{1,0:T(8,128)(2,1)S(1)}, bf16[256,256]{1,0:T(8,128)(2,1)S(1)}, u32[]{:S(2)}, u32[]{:S(2)}) collective-permute-start(bf16[256,256]{1,0:T(8,128)(2,1)S(1)} %get-tuple-element.84), channel_id=1, source_target_pairs={{2,0},{3,1},{6,4},{7,5},{10,8},{11,9},{14,12},{15,13},{18,16},{19,... | collective-permute-start | bytes 393224 | tf_op jit(solution)/shard_map/ppermute | solution.py:374
  57.3 5.8 %collective-permute-start.18 = (bf16[256,256]{1,0:T(8,128)(2,1)S(1)}, bf16[256,256]{1,0:T(8,128)(2,1)S(1)}, u32[]{:S(2)}, u32[]{:S(2)}) collective-permute-start(bf16[256,256]{1,0:T(8,128)(2,1)S(1)} %get-tuple-element.81), channel_id=1, source_target_pairs={{8,0},{12,4},{16,8},{20,12},{24,16},{28,20},{2,24},{6,28},{9,1},{1... | collective-permute-start | bytes 393224 | tf_op jit(solution)/shard_map/ppermute | solution.py:370
  59.3 8.0 %collective-permute-start.19 = (bf16[256,256]{1,0:T(8,128)(2,1)S(1)}, bf16[256,256]{1,0:T(8,128)(2,1)S(1)}, u32[]{:S(2)}, u32[]{:S(2)}) collective-permute-start(bf16[256,256]{1,0:T(8,128)(2,1)S(1)} %get-tuple-element.82), channel_id=1, source_target_pairs={{16,0},{20,4},{24,8},{28,12},{2,16},{6,20},{10,24},{14,28},{17,1},... | collective-permute-start | bytes 393224 | tf_op jit(solution)/shard_map/ppermute | solution.py:370
  61.2 7.5 %collective-permute-start.20 = (bf16[256,256]{1,0:T(8,128)(2,1)S(1)}, bf16[256,256]{1,0:T(8,128)(2,1)S(1)}, u32[]{:S(2)}, u32[]{:S(2)}) collective-permute-start(bf16[256,256]{1,0:T(8,128)(2,1)S(1)} %get-tuple-element.83), channel_id=1, source_target_pairs={{24,0},{28,4},{2,8},{6,12},{10,16},{14,20},{18,24},{22,28},{25,1},... | collective-permute-start | bytes 393224 | tf_op jit(solution)/shard_map/ppermute | solution.py:370
  69.1 14.0 %collective-permute-start.22 = (bf16[128,2048]{1,0:T(8,128)(2,1)S(1)}, bf16[128,2048]{1,0:T(8,128)(2,1)S(1)}, u32[]{:S(2)}, u32[]{:S(2)}) collective-permute-start(bf16[128,2048]{1,0:T(8,128)(2,1)S(1)} %cross.1), channel_id=1, source_target_pairs={{0,1},{4,5},{8,9},{12,13},{16,17},{20,21},{24,25},{28,29},{1,0},{5... | collective-permute-start | bytes 1572872 | tf_op jit(solution)/shard_map/ppermute | solution.py:487
  77.1 2.1 %collective-permute-start.23 = (bf16[128,256]{1,0:T(8,128)(2,1)S(1)}, bf16[128,256]{1,0:T(8,128)(2,1)S(1)}, u32[]{:S(2)}, u32[]{:S(2)}) collective-permute-start(bf16[128,256]{1,0:T(8,128)(2,1)S(1)} %get-tuple-element.86), channel_id=1, source_target_pairs={{0,1},{4,5},{8,9},{12,13},{16,17},{20,21},{24,25},{28,29},{1,0},{5... | collective-permute-start | bytes 196616 | tf_op jit(solution)/shard_map/ppermute | solution.py:353
  77.2 3.1 %collective-permute-start.24 = (bf16[128,256]{1,0:T(8,128)(2,1)S(1)}, bf16[128,256]{1,0:T(8,128)(2,1)S(1)}, u32[]{:S(2)}, u32[]{:S(2)}) collective-permute-start(bf16[128,256]{1,0:T(8,128)(2,1)S(1)} %get-tuple-element.87), channel_id=1, source_target_pairs={{0,4},{4,0},{8,12},{12,8},{16,20},{20,16},{24,28},{28,24},{1,5},{5... | collective-permute-start | bytes 196616 | tf_op jit(solution)/shard_map/ppermute | solution.py:353
  78.4 4.7 %collective-permute-start.25 = (bf16[128,256]{1,0:T(8,128)(2,1)S(1)}, bf16[128,256]{1,0:T(8,128)(2,1)S(1)}, u32[]{:S(2)}, u32[]{:S(2)}) collective-permute-start(bf16[128,256]{1,0:T(8,128)(2,1)S(1)} %get-tuple-element.88), channel_id=1, source_target_pairs={{0,5},{4,1},{8,13},{12,9},{16,21},{20,17},{24,29},{28,25},{1,4},{5... | collective-permute-start | bytes 196616 | tf_op jit(solution)/shard_map/ppermute | solution.py:353

commit v3 on v2

--- a/solution.py
+++ b/solution.py
@@ -24,7 +24,7 @@
     return lax.dot_general(a, b, dims, preferred_element_type=F32)
 
 
-def vmem_call(kernel, out_shapes, args, scratch=(), hbm=(), smem=(), after=(), through=(), mib=8, flops=0, name=None):
+def vmem_call(kernel, out_shapes, args, scratch=(), hbm=(), smem=(), after=(), through=(), mib=4, flops=0, name=None):
     def space(i):
         return pltpu.SMEM if i in smem else pltpu.HBM if i in hbm else pltpu.VMEM
 
@@ -122,14 +122,28 @@
             out[...] = down[...]
 
 
-def payload_kernel(n_out, n_shifts, own, by_core, by_y, by_diag, even, odd, *outs):
+def payload_kernel(n_out, own, by_core, by_y, by_diag, even, odd, pieces, *outs):
     select_chunks((even, odd), own, by_core, by_y, by_diag)
-    fill_payloads(n_out, odd, even, outs[:n_shifts])
-    fill_payloads(n_out, even, odd, outs[n_shifts:])
-
-
-def attend_kernel(odd, n_slots, seq_blk, keep, by_y, starts, doc_scalars, *rest):
-    slots, rest = rest[:n_slots], rest[n_slots:]
+    _, _, z = place()
+    rows = even.shape[0]
+    for other in range(n_out):
+        where = slice(other * rows, (other + 1) * rows)
+
+        @pl.when(other > z)
+        def _(where=where):
+            pieces[where, :] = odd[...]
+
+        @pl.when(other <= z)
+        def _(where=where):
+            pieces[where, :] = even[...]
+
+    fill_payloads(n_out, even, odd, outs)
+
+
+def attend_kernel(odd, n_out, n_slots, seq_blk, n_given, keep, by_y, starts, doc_scalars, *rest):
+    given, rest = rest[:n_given], rest[n_given:]
+    if not odd:
+        dq_other, rest = rest[0], rest[1:]
     dq_keep, dq_send, rest = rest[0], rest[1], rest[2:]
     sums, rest = rest[:n_slots], rest[n_slots:]
     q_rows, g_rows, keys, vals, scores, dweights, dq_cols, acc, stats, dq_both = rest
@@ -162,13 +176,24 @@
     for h in range(2 * heads):
         rows = slice(h * tok, (h + 1) * tok)
         q_rows[rows, HEAD_DIM:] = unity
-    for i, slot in enumerate(slots):
+    for i in range(n_slots):
         rows = slice(i * pair, (i + 1) * pair)
+        back = n_slots - 1 - i
+        if n_given == n_slots:
+            slot = given[i][...]
+        elif back == 0:
+            slot = given[2][...]
+        elif back == n_out:
+            slot = given[1][...]
+        else:
+            source = lax.rem(z + n_out - back, n_out)
+            slot = given[0][pl.ds(pl.multiple_of(source * pair, pair), pair), :]
         for unit in (0, 1):
             keys[unit, rows, :HEAD_DIM] = slot[:, :HEAD_DIM]
         vals[rows, :] = slot[:, HEAD_DIM:]
 
     begin = lax.div(doc_scalars[first] - base, pair)
+    begin_last = lax.div(doc_scalars[first + tok] - base, pair)
 
     def rows_of(j):
         return pl.ds(pl.multiple_of(j * pair, pair), pair)
@@ -190,38 +215,45 @@
     key_place = lax.broadcasted_iota(jnp.int32, (pair, tok), 0)
     lows = [starts[pl.ds(lax.div(first, 128) + unit, 1), :] for unit in (0, 1)]
 
-    def score_step(j, carry):
+    def columns_of(units):
+        return [n for n in range(n_steps) if unit_of(n) in units]
+
+    def over_slots(step):
+        lax.fori_loop(begin, begin_last, functools.partial(step, (0,)), 0)
+        lax.fori_loop(begin_last, n_slots, functools.partial(step, (0, 1)), 0)
+
+    def score_step(units, j, carry):
         place_j = key_place + (base + j * pair)
-        for unit in (0, 1):
+        for unit in units:
             allowed = (place_j >= lows[unit]) & (place_j <= t + (first + unit * tok))
             keys[unit, rows_of(j), HEAD_DIM:] = jnp.where(allowed, 0.0, -1e30).astype(BF16)
-        for n in range(n_steps):
+        for n in columns_of(units):
             s = dot(keys[unit_of(n), rows_of(j), :], q_rows[cols_of(n), :], NT)
             scores[rows_of(j), cols_of(n)] = s
             stats[0, :, cols_of(n)] = jnp.maximum(stats[0, :, cols_of(n)], fold(jnp.max, s))
         return carry
 
-    lax.fori_loop(begin, n_slots, score_step, 0)
+    over_slots(score_step)
     for n in range(n_steps):
         top = jnp.max(stats[0, :, cols_of(n)], axis=0, keepdims=True)
         stats[0, :, cols_of(n)] = jnp.broadcast_to(top, (8, step_cols))
 
-    def weight_step(j, carry):
-        for n in range(n_steps):
+    def weight_step(units, j, carry):
+        for n in columns_of(units):
             p = jnp.exp2((scores[rows_of(j), cols_of(n)] - stats[0, 0:1, cols_of(n)]) * scale)
             scores[rows_of(j), cols_of(n)] = p
             stats[1, :, cols_of(n)] += fold(jnp.sum, p)
             dweights[rows_of(j), cols_of(n)] = dot(vals[rows_of(j), :], g_rows[cols_of(n), :], NT)
         return carry
 
-    lax.fori_loop(begin, n_slots, weight_step, 0)
+    over_slots(weight_step)
     for n in range(n_steps):
         inv = 1.0 / jnp.sum(stats[1, :, cols_of(n)], axis=0, keepdims=True)
         stats[1, :, cols_of(n)] = jnp.broadcast_to(inv, (8, step_cols))
 
-    def value_step(j, carry):
+    def value_step(units, j, carry):
         total = jnp.zeros((pair, HEAD_DIM), F32)
-        for n in range(n_steps):
+        for n in columns_of(units):
             d = dweights[rows_of(j), cols_of(n)]
             w = scores[rows_of(j), cols_of(n)] * stats[1, 0:1, cols_of(n)]
             wb = w.astype(BF16)
@@ -231,15 +263,15 @@
         acc[rows_of(j), HEAD_DIM:] = total
         return carry
 
-    lax.fori_loop(begin, n_slots, value_step, 0)
+    over_slots(value_step)
     for n in range(n_steps):
         rowdot = jnp.sum(stats[2, :, cols_of(n)], axis=0, keepdims=True)
         stats[2, :, cols_of(n)] = jnp.broadcast_to(rowdot, (8, step_cols))
 
-    def grad_step(j, carry):
+    def grad_step(units, j, carry):
         total = jnp.zeros((pair, HEAD_DIM), F32)
         k_cols = keys[0, rows_of(j), :HEAD_DIM].T
-        for n in range(n_steps):
+        for n in columns_of(units):
             rest = dweights[rows_of(j), cols_of(n)] - stats[2, 0:1, cols_of(n)]
             ds = (scores[rows_of(j), cols_of(n)] * rest).astype(BF16)
             total = total + dot(ds, q_rows[cols_of(n), :HEAD_DIM], NN)
@@ -247,14 +279,16 @@
         acc[rows_of(j), :HEAD_DIM] = total * inv_root
         return carry
 
-    lax.fori_loop(begin, n_slots, grad_step, 0)
+    over_slots(grad_step)
 
     for h in range(2 * heads):
         unit, head = h // heads, h % heads
         dq = (dq_cols[:, h * tok : (h + 1) * tok] * inv_root).T
         dq_both[unit, :, head * HEAD_DIM : (head + 1) * HEAD_DIM] = dq.astype(BF16)
     dq_keep[...] = dq_both[y]
-    dq_send[...] = dq_both[1 - y]
+    dq_send[:tok, :] = dq_both[1 - y]
+    if not odd:
+        dq_send[tok:, :] = dq_other[...]
 
     for i, out in enumerate(sums):
 
@@ -284,8 +318,8 @@
 
 
 def home_kernel(n_out, n_terms, own_even, odd_total, even_total, *refs):
-    terms, refs = refs[:n_terms], refs[n_terms:]
-    rim, outs, total = refs[:-5], refs[-5:-1], refs[-1]
+    outs, total = refs[-5:-1], refs[-1]
+    rim, terms = refs[: -5 - n_terms], refs[-5 - n_terms : -5]
     tok = own_even.shape[0] // 2
     odd = odd_total[...]
     if rim:
@@ -296,9 +330,10 @@
         out[...] = total[c, pl.ds(pl.multiple_of(yy * tok, tok), tok), :].astype(out.dtype)
 
 
-def cross_kernel(odd_keep, odd_got, even_keep, even_got, out):
+def cross_kernel(odd_keep, even_keep, got_ref, out):
     core, y, _ = place()
-    width = odd_keep.shape[1]
+    tok, width = odd_keep.shape
+    even_got, odd_got = got_ref.at[:tok, :], got_ref.at[tok:, :]
     for c, keep, got in ((0, odd_keep, odd_got), (1, even_keep, even_got)):
 
         @pl.when(core == c)
@@ -307,10 +342,11 @@
             out[:, pl.ds(pl.multiple_of((1 - y) * width, 128), width)] = got[...]
 
 
-def finish_kernel(odd_keep, odd_got, even_keep, even_got, crossed, *refs):
+def finish_kernel(odd_keep, even_keep, got_ref, crossed, *refs):
     parts, (out, k_out, v_out) = refs[:4], refs[4:]
     core, y, _ = place()
-    width = odd_keep.shape[1]
+    tok, width = odd_keep.shape
+    even_got, odd_got = got_ref.at[:tok, :], got_ref.at[tok:, :]
 
     def columns(quarter, count=1, size=width):
         return pl.ds(pl.multiple_of(quarter * size, 128), count * size)
@@ -370,6 +406,13 @@
             got.append(lax.ppermute(part, both, [(b, a) for a, b in route] if back else route))
         return got
 
+    def gathered(pieces):
+        groups = [[2 * z + y for z in range(n_out)] for y in (0, 1)]
+        got = lax.all_to_all(
+            pieces.reshape(n_out, pair, -1), "swap", 0, 0, axis_index_groups=groups
+        )
+        return got.reshape(pieces.shape)
+
     def along_x(part, step):
         return lax.ppermute(
             part, "blk", [(b, b + step) for b in range(n_blk) if 0 <= b + step < n_blk]
@@ -396,12 +439,26 @@
 
     one_each = [lambda numbers, i=i: [numbers[i]] for i in range(4)]
     by_core = [lambda numbers: [numbers[0] // 2 * 2 + i for i in (0, 1)], lambda numbers: [numbers[1] // 2 * 2 + i for i in (0, 1)]]
-    kv_parts = split(keys, values, kv_width, one_each, "split_kv")
+    kv_parts = [
+        jnp.concatenate(
+            [lax.dynamic_slice_in_dim(x, quarter * kv_width, kv_width, 1) for x in (keys, values)], 1
+        )
+        for quarter in quarters()
+    ]
     kv_recv = to_partners(kv_parts[1:])
-    mine, other = split(queries, grad_out, q_width, by_core, "split_qg")
+    half = 2 * q_width
+
+    def halves(which):
+        parts = [lax.dynamic_slice_in_dim(x, which * half, half, 1) for x in (queries, grad_out)]
+        return jnp.concatenate(
+            [x[:, i * q_width : (i + 1) * q_width] for i in (0, 1) for x in parts], 1
+        )
+
+    core = place()[0]
+    mine, other = halves(core), halves(1 - core)
     *made, other = vmem_call(
-        functools.partial(payload_kernel, n_out, len(shifts)),
-        [block_shape] * (2 + 2 * len(shifts)),
+        functools.partial(payload_kernel, n_out),
+        [block_shape] * 2 + [shape(n_out * pair, 2 * kv_width)] + [block_shape] * len(shifts),
         (kv_parts[0], *kv_recv),
         through=(other,),
         name="payload",
@@ -410,10 +467,10 @@
     odd_qg, odd_send, even_qg, even_send = vmem_call(
         choose_kernel, [shape(tok, 2 * q_width)] * 4, (mine, crossed), after=(made[0],), name="choose_qg"
     )
-    even, odd, *pays = made
-    odd_got = along_z(pays[: len(shifts)], odd_route)
+    even, odd, odd_pieces, *pays = made
+    odd_got = gathered(odd_pieces)
     odd_qg = (odd_qg, lax.ppermute(odd_send, both, routes[1]))
-    even_got = along_z(pays[len(shifts) :], even_route)
+    even_got = along_z(pays, even_route)
     even_qg = (even_qg, lax.ppermute(even_send, both, routes[1]))
     rim = along_x(odd, 2) if whole_ring else None
 
@@ -426,11 +483,12 @@
         for i in range(n_slots)
     ]
 
-    def attend(which, slots, qg, after=()):
+    def attend(which, slots, qg, dq_other=None):
         return vmem_call(
-            functools.partial(attend_kernel, which, n_slots, seq_blk),
-            [shape(tok, q_width)] * 2 + sum_shapes[which * n_slots : (which + 1) * n_slots],
-            (*qg, starts, doc_ids, *slots),
+            functools.partial(attend_kernel, which, n_out, n_slots, seq_blk, len(slots)),
+            [shape(tok, q_width), shape(tok if which else pair, q_width)]
+            + sum_shapes[which * n_slots : (which + 1) * n_slots],
+            (*qg, starts, doc_ids, *slots) + (() if which else (dq_other,)),
             scratch=[
                 pltpu.VMEM((rows, 2 * HEAD_DIM), BF16),
                 pltpu.VMEM((rows, HEAD_DIM), BF16),
@@ -444,8 +502,7 @@
                 pltpu.VMEM((2, tok, q_width), BF16),
             ],
             smem=(3,),
-            after=after,
-            mib=32,
+            mib=28,
             flops=6_000_000_000,
             name="attend_odd" if which else "attend_even",
         )
@@ -456,30 +513,28 @@
     def sent(sums):
         return [sums[far - k] for k in shifts]
 
-    dq_odd, dq_odd_send, *odd_sums = attend(1, slots_of(odd, even, odd_got), odd_qg)
+    dq_odd, dq_odd_send, *odd_sums = attend(1, (odd_got, even, odd), odd_qg)
     odd_back = along_z(sent(odd_sums), odd_route, back=True)
-    dq_even, dq_send, *even_sums = attend(0, slots_of(even, rim, even_got), even_qg, (dq_odd,))
-    dq_odd_got = lax.ppermute(dq_odd_send, both, routes[1])
+    dq_even, dq_send, *even_sums = attend(0, slots_of(even, rim, even_got), even_qg, dq_odd_send)
     odd_total, even_total, dq_send, *even_sent = vmem_call(
         functools.partial(odd_sum_kernel, n_out, len(shifts)),
         [sum_shape, sum_shape],
         (odd_sums[far], *odd_back, *([odd_sums[0]] if whole_ring else [])),
-        after=(dq_odd_got,),
         through=[dq_send, *sent(even_sums)],
         name="odd_sum",
     )
-    dq_even_got = lax.ppermute(dq_send, both, routes[1])
+    dq_got = lax.ppermute(dq_send, both, routes[1])
+    rim_home = (along_x(even_sums[0], -2),) if whole_ring else ()
     even_back = along_z(even_sent, even_route, back=True)
-    rim_home = (along_x(even_sums[0], -2),) if whole_ring else ()
     home = vmem_call(
         functools.partial(home_kernel, n_out, len(shifts)),
         [shape(tok, 2 * kv_width, F32)] + [shape(tok, 2 * kv_width)] * 3,
-        (even_sums[far], odd_total, even_total, *even_back, *rim_home),
+        (even_sums[far], odd_total, even_total, *rim_home, *even_back),
         scratch=[pltpu.VMEM((2, pair, 2 * kv_width), F32)],
         name="home",
     )
     kv_home = to_partners(home[1:])
-    dq_parts = (dq_odd, dq_odd_got, dq_even, dq_even_got)
+    dq_parts = (dq_odd, dq_even, dq_got)
     (dq_cross,) = vmem_call(cross_kernel, [shape(tok, 2 * q_width)], dq_parts, after=(home[0],), name="cross")
     return vmem_call(
         finish_kernel,

time: 85.7 us -> 81 us (0.945); the launches traced: 84.3 us -> 80.5 us
  Pallas kernels: 22.9 us -> 15.4 us
  starting transfers between devices: 39.9 us -> 43.3 us
  other arithmetic: 0 us -> 1.2 us
    pallas_call x10 -> x8, Pallas kernels: 22.9 us -> 15.4 us  [vmem_call(): pl.pallas_call(run, out_shape=list(out_shapes) + [jax.ShapeDtypeStruct(t....]
    ppermute x1, starting transfers between devices: 8.01 us -> 3.1 us  [body(): lax.ppermute(dq_cross, both, routes[0])]
    all_to_all x0 -> x1, starting transfers between devices: none -> 4.59 us  [gathered(): lax.all_to_all(pieces.reshape(n_out, pair, -1), 'swap', 0, 0, axis_index_...]
    unnamed x10 -> x2, local copies, waits for them, and re-layouts: 4.26 us -> 0.01 us
    ppermute x12 -> x9, starting transfers between devices: 21.2 us -> 24.6 us  [along_z(): lax.ppermute(part, both, [(b, a) for a, b in route] if back else route)]
    slice x0 -> x1, local copies, waits for them, and re-layouts: none -> 2.59 us  [halves(): x[:, i * q_width:(i + 1) * q_width]]
    ppermute x1, waiting for transfers between devices: 2.31 us -> 0.01 us  [body(): crossed = lax.ppermute(other, both, routes[0])]
    ppermute x1, waiting for transfers between devices: 0.01 us -> 1.81 us  [body(): odd_qg = (odd_qg, lax.ppermute(odd_send, both, routes[1]))]
  transfers between devices with their start and end apart: 26 -> 23, of which waited for: 8 -> 6; matrix products, arithmetic and copies ran while one was open for 0% -> 5% of each run, Pallas kernels for 25% -> 16%
where the time goes in v3:
time: 81 us; the launch traced here: 80.5 us
  starting transfers between devices  43.3 us (53%)
  waiting for transfers between devices  16.2 us (20%)
  Pallas kernels  15.4 us (19%)
  local copies, waits for them, and re-layouts  3.51 us (4%)
  other arithmetic  1.2 us (1%)
  between operations  0.89 us (1%)
    ppermute x9, starting transfers between devices, along_z(): lax.ppermute(part, both, [(b, a) for a, b in route] if back else route)  24.6 us
    pallas_call x8, Pallas kernels, vmem_call(): pl.pallas_call(run, out_shape=list(out_shapes) + [jax.ShapeDtypeStruct(t....  15.4 us
    ppermute x9, waiting for transfers between devices, along_z(): lax.ppermute(part, both, [(b, a) for a, b in route] if back else route)  10.2 us
    ppermute x6, starting transfers between devices, to_partners(): lax.ppermute(part, both, route)  4.66 us
    all_to_all x1, starting transfers between devices, gathered(): lax.all_to_all(pieces.reshape(n_out, pair, -1), 'swap', 0, 0, axis_index_...  4.59 us
    ppermute x6, waiting for transfers between devices, to_partners(): lax.ppermute(part, both, route)  4.24 us
    ppermute x1, starting transfers between devices, body(): lax.ppermute(dq_cross, both, routes[0])  3.1 us
    slice x1, local copies, waits for them, and re-layouts, halves(): x[:, i * q_width:(i + 1) * q_width]  2.59 us
  transfers between devices with their start and end apart: 23, of which 6 were waited for; matrix products, arithmetic and copies ran while one was open for 5% of the time, Pallas kernels for 16%

profile of v3, /device:TPU:3, one launch (start us, length us, event | category | flops | bytes accessed | tf_op | source)
XLA Modules:
  0.0 80.5 jit_solution(6538486900936962021)
XLA Ops:
  0.7 0.9 %constant_dynamic-slice_fusion.6 = (bf16[128,128]{1,0:T(8,128)(2,1)S(1)}, bf16[128,128]{1,0:T(8,128)(2,1)S(1)}, bf16[128,128]{1,0:T(8,128)(2,1)S(1)}, bf16[128,1...) fusion(bf16[128,512]{1,0:T(8,128)(2,1)} %param.7, ...), kind=kLoop, calls=%fused_computation.12 | loop fusion | bytes 524304 | tf_op jit(solution)/shard_map/dynamic_slice | solution.py:444
  1.6 0.7 collective-permute-start
  2.3 1.3 %collective-permute-start.1 = (bf16[128,256]{1,0:T(8,128)(2,1)S(1)}, bf16[128,256]{1,0:T(8,128)(2,1)S(1)}, u32[]{:S(2)}, u32[]{:S(2)}) collective-permute-start(bf16[128,256]{1,0:T(8,128)(2,1)S(1)} %pad_maximum_fusion.4), channel_id=1, source_target_pairs={{0,4},{4,0},{8,12},{12,8},{16,20},{20,16},{24,28},{28,24},{1,5},{5... | collective-permute-start | bytes 196616 | tf_op jit(solution)/shard_map/ppermute | solution.py:389
  3.7 0.5 collective-permute-start.2
  4.1 2.6 %constant_dynamic-slice_fusion = (bf16[128,1024]{1,0:T(8,128)(2,1)S(1)}, bf16[128,1024]{1,0:T(8,128)(2,1)S(1)}, bf16[128,1024]{1,0:T(8,128)(2,1)S(1)}, bf16[128,...) fusion(bf16[128,4096]{1,0:T(8,128)(2,1)} %param.8, ...), kind=kLoop, calls=%fused_computation.6 | loop fusion | bytes 4194320 | tf_op jit(solution)/shard_map/slice | solution.py:454
  6.7 0.1 pad_maximum_fusion.1.refs_4_
  6.8 0.0 collective-permute-done.refs_1_
  6.8 0.9 %collective-permute-done.2.refs_3_ = bf16[128,256]{1,0:T(8,128)(2,1)S(1)} collective-permute-done((bf16[128,256]{1,0:T(8,128)(2,1)S(1)}, bf16[128,256]{1,0:T(8,128)(2,1)S(1)}, u32[]{:S(2)}, u32[]{:S(2)}) %collective-permute-start.2) | collective-permute-done | bytes 65568 | tf_op jit(solution)/shard_map/ppermute | solution.py:389
  7.7 1.0 %payload.1 = (bf16[256,256]{1,0:T(8,128)(2,1)S(1)}, bf16[256,256]{1,0:T(8,128)(2,1)}, bf16[1024,256]{1,0:T(8,128)(2,1)}, bf16[256,256]{1,0:T(8,128)(2,1)S(1)}, b...) custom-call(bf16[128,256]{1,0:T(8,128)(2,1)S(1)} %pad_maximum_fusion, ...), custom_call_target="tpu_custom_call", output_to_operand_aliasing={{6}: (4, {})} | custom-call | tf_op jit(solution)/shard_map/payload/pallas_call | solution.py:41
  8.7 0.4 collective-permute-start.3
  9.1 4.6 %all-to-all-start = ((bf16[4,256,256]{2,1,0:T(8,128)(2,1)}), bf16[4,256,256]{2,1,0:T(8,128)(2,1)S(1)}, u32[]{:S(2)}, u32[]{:S(2)}) async-start(bf16[4,256,256]{2,1,0:T(8,128)(2,1)} %bitcast.1), calls=%async_computation | async-start | bytes 1048576 | tf_op jit(solution)/shard_map/all_to_all | solution.py:411
  13.7 1.1 %pad_maximum_fusion.refs_0_ = bf16[128,4096]{1,0:T(8,128)(2,1)S(1)} fusion(bf16[128,1024]{1,0:T(8,128)(2,1)S(1)} %get-tuple-element.80, bf16[128,1024]{1,0:T(8,128)(2,1)} %get-tuple-element.89, bf16[128,1024]{1,0:T(8,128)(2,1)S(1)} %get-tuple-element.78, bf16[128,1024]{1,0:T(8,128)(2,1)} %get-tuple-element.91), kind=kLoop, calls=%fused_computation | loop fusion | flops 4194304 | bytes 2097152 | tf_op jit(solution)/shard_map/concatenate | solution.py:453
  14.8 0.0 copy-start
  14.8 0.2 choose_qg.1
  15.0 1.1 %collective-permute-start.4 = (bf16[128,2048]{1,0:T(8,128)(2,1)S(1)}, bf16[128,2048]{1,0:T(8,128)(2,1)S(1)}, u32[]{:S(2)}, u32[]{:S(2)}) collective-permute-start(bf16[128,2048]{1,0:T(8,128)(2,1)S(1)} %get-tuple-element.41), channel_id=1, source_target_pairs={{0,4},{4,0},{8,12},{12,8},{16,20},{20,16},{24,28},{28,24},{1,5},{5... | collective-permute-start | bytes 1572872 | tf_op jit(solution)/shard_map/ppermute | solution.py:472
  16.1 1.3 %collective-permute-start.6 = (bf16[256,256]{1,0:T(8,128)(2,1)}, bf16[256,256]{1,0:T(8,128)(2,1)}, u32[]{:S(2)}, u32[]{:S(2)}) collective-permute-start(bf16[256,256]{1,0:T(8,128)(2,1)} %get-tuple-element.43.refs_6_), channel_id=1, source_target_pairs={{0,2},{1,3},{4,6},{5,7},{8,10},{9,11},{12,14},{13,15},{16,18},{17,... | collective-permute-start | bytes 393224 | tf_op jit(solution)/shard_map/ppermute | solution.py:417
  17.4 5.2 %collective-permute-start.7 = (bf16[256,256]{1,0:T(8,128)(2,1)}, bf16[256,256]{1,0:T(8,128)(2,1)}, u32[]{:S(2)}, u32[]{:S(2)}) collective-permute-start(bf16[256,256]{1,0:T(8,128)(2,1)} %get-tuple-element.47), channel_id=1, source_target_pairs={{0,24},{4,28},{8,2},{12,6},{16,10},{20,14},{24,18},{28,22},{1,25},... | collective-permute-start | bytes 393224 | tf_op jit(solution)/shard_map/ppermute | solution.py:406
  22.6 1.9 %collective-permute-start.8 = (bf16[256,256]{1,0:T(8,128)(2,1)S(1)}, bf16[256,256]{1,0:T(8,128)(2,1)}, u32[]{:S(2)}, u32[]{:S(2)}) collective-permute-start(bf16[256,256]{1,0:T(8,128)(2,1)S(1)} %get-tuple-element.48), channel_id=1, source_target_pairs={{0,16},{4,20},{8,24},{12,28},{16,2},{20,6},{24,10},{28,14},{1,17},... | collective-permute-start | bytes 393224 | tf_op jit(solution)/shard_map/ppermute | solution.py:406
  24.5 1.9 %collective-permute-start.9 = (bf16[256,256]{1,0:T(8,128)(2,1)S(1)}, bf16[256,256]{1,0:T(8,128)(2,1)}, u32[]{:S(2)}, u32[]{:S(2)}) collective-permute-start(bf16[256,256]{1,0:T(8,128)(2,1)S(1)} %get-tuple-element.49), channel_id=1, source_target_pairs={{0,8},{4,12},{8,16},{12,20},{16,24},{20,28},{24,2},{28,6},{1,9},{5... | collective-permute-start | bytes 393224 | tf_op jit(solution)/shard_map/ppermute | solution.py:406
  26.4 1.8 %collective-permute-done.4.refs_1_ = bf16[128,2048]{1,0:T(8,128)(2,1)S(1)} collective-permute-done((bf16[128,2048]{1,0:T(8,128)(2,1)S(1)}, bf16[128,2048]{1,0:T(8,128)(2,1)S(1)}, u32[]{:S(2)}, u32[]{:S(2)}) %collective-permute-start.4) | collective-permute-done | bytes 524320 | tf_op jit(solution)/shard_map/ppermute | solution.py:472
  28.2 0.9 %collective-permute-start.5 = (bf16[128,2048]{1,0:T(8,128)(2,1)S(1)}, bf16[128,2048]{1,0:T(8,128)(2,1)S(1)}, u32[]{:S(2)}, u32[]{:S(2)}) collective-permute-start(bf16[128,2048]{1,0:T(8,128)(2,1)S(1)} %get-tuple-element.46), channel_id=1, source_target_pairs={{0,4},{4,0},{8,12},{12,8},{16,20},{20,16},{24,28},{28,24},{1,5},{5... | collective-permute-start | bytes 1572872 | tf_op jit(solution)/shard_map/ppermute | solution.py:474
  29.1 0.0 all-to-all-done
  29.1 6.2 %attend_odd.1 = (bf16[128,1024]{1,0:T(8,128)(2,1)S(1)}, bf16[128,1024]{1,0:T(8,128)(2,1)S(1)}, f32[256,256]{1,0:T(8,128)S(1)}, bf16[256,256]{1,0:T(8,128)(2,1)S(...) custom-call(bf16[128,2048]{1,0:T(8,128)(2,1)S(1)} %get-tuple-element.40.refs_0_, ...), custom_call_target="tpu_custom_call" | custom-call | flops 6000000000 | tf_op jit(solution)/shard_map/attend_odd/pallas_call | solution.py:41
  35.3 5.6 %collective-permute-start.10 = (bf16[256,256]{1,0:T(8,128)(2,1)S(1)}, bf16[256,256]{1,0:T(8,128)(2,1)S(1)}, u32[]{:S(2)}, u32[]{:S(2)}) collective-permute-start(bf16[256,256]{1,0:T(8,128)(2,1)S(1)} %get-tuple-element.53), channel_id=1, source_target_pairs={{8,0},{12,4},{16,8},{20,12},{24,16},{28,20},{0,24},{4,28},{9,1},{1... | collective-permute-start | bytes 393224 | tf_op jit(solution)/shard_map/ppermute | solution.py:406
  40.9 0.0 collective-permute-done.8.refs_6_
  40.9 0.4 collective-permute-start.12
  41.3 0.0 collective-permute-done.9.refs_7_
  41.3 0.0 collective-permute-done.5.refs_1_
  41.3 6.4 %attend_even.1 = (bf16[128,1024]{1,0:T(8,128)(2,1)S(1)}, bf16[256,1024]{1,0:T(8,128)(2,1)S(1)}, bf16[256,256]{1,0:T(8,128)(2,1)S(1)}, bf16[256,256]{1,0:T(8,128)...) custom-call(bf16[128,2048]{1,0:T(8,128)(2,1)S(1)} %get-tuple-element.45.refs_0_, ...), custom_call_target="tpu_custom_call" | custom-call | flops 6000000000 | tf_op jit(solution)/shard_map/attend_even/pallas_call | solution.py:41
  47.7 0.0 collective-permute-done.10.refs_1_
  47.7 3.3 %collective-permute-done.11.refs_2_ = bf16[256,256]{1,0:T(8,128)(2,1)S(1)} collective-permute-done((bf16[256,256]{1,0:T(8,128)(2,1)S(1)}, bf16[256,256]{1,0:T(8,128)(2,1)S(1)}, u32[]{:S(2)}, u32[]{:S(2)}) %collective-permute-start.11) | collective-permute-done | bytes 131104 | tf_op jit(solution)/shard_map/ppermute | solution.py:406
  51.0 0.0 collective-permute-done.12.refs_3_
  51.0 0.2 odd_sum.1
  51.2 1.4 %collective-permute-start.13 = (bf16[256,1024]{1,0:T(8,128)(2,1)S(1)}, bf16[256,1024]{1,0:T(8,128)(2,1)S(1)}, u32[]{:S(2)}, u32[]{:S(2)}) collective-permute-start(bf16[256,1024]{1,0:T(8,128)(2,1)S(1)} %get-tuple-element.61), channel_id=1, source_target_pairs={{0,4},{4,0},{8,12},{12,8},{16,20},{20,16},{24,28},{28,24},{1,5},{5... | collective-permute-start | bytes 1572872 | tf_op jit(solution)/shard_map/ppermute | solution.py:526
  52.6 1.3 %collective-permute-start.14 = (bf16[256,256]{1,0:T(8,128)(2,1)S(1)}, bf16[256,256]{1,0:T(8,128)(2,1)S(1)}, u32[]{:S(2)}, u32[]{:S(2)}) collective-permute-start(bf16[256,256]{1,0:T(8,128)(2,1)S(1)} %get-tuple-element.65), channel_id=1, source_target_pairs={{2,0},{3,1},{6,4},{7,5},{10,8},{11,9},{14,12},{15,13},{18,16},{19,... | collective-permute-start | bytes 393224 | tf_op jit(solution)/shard_map/ppermute | solution.py:417
  53.8 5.2 %collective-permute-start.15 = (bf16[256,256]{1,0:T(8,128)(2,1)S(1)}, bf16[256,256]{1,0:T(8,128)(2,1)S(1)}, u32[]{:S(2)}, u32[]{:S(2)}) collective-permute-start(bf16[256,256]{1,0:T(8,128)(2,1)S(1)} %get-tuple-element.66), channel_id=1, source_target_pairs={{8,0},{12,4},{16,8},{20,12},{24,16},{28,20},{2,24},{6,28},{9,1},{1... | collective-permute-start | bytes 393224 | tf_op jit(solution)/shard_map/ppermute | solution.py:406
  59.1 2.5 %collective-permute-start.16 = (bf16[256,256]{1,0:T(8,128)(2,1)S(1)}, bf16[256,256]{1,0:T(8,128)(2,1)S(1)}, u32[]{:S(2)}, u32[]{:S(2)}) collective-permute-start(bf16[256,256]{1,0:T(8,128)(2,1)S(1)} %get-tuple-element.67), channel_id=1, source_target_pairs={{16,0},{20,4},{24,8},{28,12},{2,16},{6,20},{10,24},{14,28},{17,1},... | collective-permute-start | bytes 393224 | tf_op jit(solution)/shard_map/ppermute | solution.py:406
  61.6 1.9 %collective-permute-start.17 = (bf16[256,256]{1,0:T(8,128)(2,1)S(1)}, bf16[256,256]{1,0:T(8,128)(2,1)S(1)}, u32[]{:S(2)}, u32[]{:S(2)}) collective-permute-start(bf16[256,256]{1,0:T(8,128)(2,1)S(1)} %get-tuple-element.68), channel_id=1, source_target_pairs={{24,0},{28,4},{2,8},{6,12},{10,16},{14,20},{18,24},{22,28},{25,1},... | collective-permute-start | bytes 393224 | tf_op jit(solution)/shard_map/ppermute | solution.py:406
  63.5 6.8 %collective-permute-done.16.refs_5_ = bf16[256,256]{1,0:T(8,128)(2,1)S(1)} collective-permute-done((bf16[256,256]{1,0:T(8,128)(2,1)S(1)}, bf16[256,256]{1,0:T(8,128)(2,1)S(1)}, u32[]{:S(2)}, u32[]{:S(2)}) %collective-permute-start.16) | collective-permute-done | bytes 131104 | tf_op jit(solution)/shard_map/ppermute | solution.py:406
  70.4 0.3 home.1
  70.7 0.1 cross.1
  70.8 3.1 %collective-permute-start.18 = (bf16[128,2048]{1,0:T(8,128)(2,1)S(1)}, bf16[128,2048]{1,0:T(8,128)(2,1)S(1)}, u32[]{:S(2)}, u32[]{:S(2)}) collective-permute-start(bf16[128,2048]{1,0:T(8,128)(2,1)S(1)} %cross.1), channel_id=1, source_target_pairs={{0,1},{4,5},{8,9},{12,13},{16,17},{20,21},{24,25},{28,29},{1,0},{5... | collective-permute-start | bytes 1572872 | tf_op jit(solution)/shard_map/ppermute | solution.py:542
  73.9 0.1 collective-permute-start.19
  73.9 0.5 collective-permute-start.20
  74.4 1.6 %collective-permute-start.21 = (bf16[128,256]{1,0:T(8,128)(2,1)S(1)}, bf16[128,256]{1,0:T(8,128)(2,1)S(1)}, u32[]{:S(2)}, u32[]{:S(2)}) collective-permute-start(bf16[128,256]{1,0:T(8,128)(2,1)S(1)} %get-tuple-element.72), channel_id=1, source_target_pairs={{0,5},{4,1},{8,13},{12,9},{16,21},{20,17},{24,29},{28,25},{1,4},{5... | collective-permute-start | bytes 196616 | tf_op jit(solution)/shard_map/ppermute | solution.py:389
  76.0 1.0 %collective-permute-done.20.refs_6_ = bf16[128,256]{1,0:T(8,128)(2,1)S(1)} collective-permute-done((bf16[128,256]{1,0:T(8,128)(2,1)S(1)}, bf16[128,256]{1,0:T(8,128)(2,1)S(1)}, u32[]{:S(2)}, u32[]{:S(2)}) %collective-permute-start.20) | collective-permute-done | bytes 65568 | tf_op jit(solution)/shard_map/ppermute | solution.py:389
  77.1 2.3 %collective-permute-done.21.refs_7_ = bf16[128,256]{1,0:T(8,128)(2,1)S(1)} collective-permute-done((bf16[128,256]{1,0:T(8,128)(2,1)S(1)}, bf16[128,256]{1,0:T(8,128)(2,1)S(1)}, u32[]{:S(2)}, u32[]{:S(2)}) %collective-permute-start.21) | collective-permute-done | bytes 65568 | tf_op jit(solution)/shard_map/ppermute | solution.py:389
  79.4 1.2 %finish.1 = (bf16[128,4096]{1,0:T(8,128)(2,1)}, bf16[128,512]{1,0:T(8,128)(2,1)}, bf16[128,512]{1,0:T(8,128)(2,1)}) custom-call(bf16[128,1024]{1,0:T(8,128)(2,1)S(1)} %get-tuple-element.44.refs_0_, bf16[128,1024]{1,0:T(8,128)(2,1)S(1)} %get-tuple-element.51.refs_1_, bf16[256,1024]{1,0:T(8,128)(2,1)S(1)} %collective-permute-done.13.refs_2_, ...), custom_call_target="tpu_custom_call" | custom-call | tf_op jit(solution)/shard_map/finish/pallas_call | solution.py:41
  (16 shorter events, 0.1 us)
Async XLA Ops:
  1.6 5.2 %collective-permute-start = (bf16[128,256]{1,0:T(8,128)(2,1)S(1)}, bf16[128,256]{1,0:T(8,128)(2,1)S(1)}, u32[]{:S(2)}, u32[]{:S(2)}) collective-permute-start(bf16[128,256]{1,0:T(8,128)(2,1)S(1)} %pad_maximum_fusion.3), channel_id=1, source_target_pairs={{0,1},{4,5},{8,9},{12,13},{16,17},{20,21},{24,25},{28,29},{1,0},{5... | collective-permute-start | bytes 196616 | tf_op jit(solution)/shard_map/ppermute | solution.py:389
  2.3 4.5 %collective-permute-start.1 = (bf16[128,256]{1,0:T(8,128)(2,1)S(1)}, bf16[128,256]{1,0:T(8,128)(2,1)S(1)}, u32[]{:S(2)}, u32[]{:S(2)}) collective-permute-start(bf16[128,256]{1,0:T(8,128)(2,1)S(1)} %pad_maximum_fusion.4), channel_id=1, source_target_pairs={{0,4},{4,0},{8,12},{12,8},{16,20},{20,16},{24,28},{28,24},{1,5},{5... | collective-permute-start | bytes 196616 | tf_op jit(solution)/shard_map/ppermute | solution.py:389
  3.7 4.1 %collective-permute-start.2 = (bf16[128,256]{1,0:T(8,128)(2,1)S(1)}, bf16[128,256]{1,0:T(8,128)(2,1)S(1)}, u32[]{:S(2)}, u32[]{:S(2)}) collective-permute-start(bf16[128,256]{1,0:T(8,128)(2,1)S(1)} %pad_maximum_fusion.5), channel_id=1, source_target_pairs={{0,5},{4,1},{8,13},{12,9},{16,21},{20,17},{24,29},{28,25},{1,4},{5... | collective-permute-start | bytes 196616 | tf_op jit(solution)/shard_map/ppermute | solution.py:389
  8.7 6.1 %collective-permute-start.3 = (bf16[128,4096]{1,0:T(8,128)(2,1)S(1)}, bf16[128,4096]{1,0:T(8,128)(2,1)S(1)}, u32[]{:S(2)}, u32[]{:S(2)}) collective-permute-start(bf16[128,4096]{1,0:T(8,128)(2,1)S(1)} %get-tuple-element.38), channel_id=1, source_target_pairs={{0,1},{4,5},{8,9},{12,13},{16,17},{20,21},{24,25},{28,29},{1,0},{5... | collective-permute-start | bytes 3145736 | tf_op jit(solution)/shard_map/ppermute | solution.py:466
  9.1 20.0 %all-to-all-start = ((bf16[4,256,256]{2,1,0:T(8,128)(2,1)}), bf16[4,256,256]{2,1,0:T(8,128)(2,1)S(1)}, u32[]{:S(2)}, u32[]{:S(2)}) async-start(bf16[4,256,256]{2,1,0:T(8,128)(2,1)} %bitcast.1), calls=%async_computation | async-start | bytes 1048576 | tf_op jit(solution)/shard_map/all_to_all | solution.py:411
  14.8 14.3 %copy-start = (s32[4096]{0:T(1024)S(1)}, s32[4096]{0:T(1024)}, u32[]{:S(2)}) copy-start(s32[4096]{0:T(1024)} %refs_3_.3) | copy-start | bytes 49156
  15.0 13.2 %collective-permute-start.4 = (bf16[128,2048]{1,0:T(8,128)(2,1)S(1)}, bf16[128,2048]{1,0:T(8,128)(2,1)S(1)}, u32[]{:S(2)}, u32[]{:S(2)}) collective-permute-start(bf16[128,2048]{1,0:T(8,128)(2,1)S(1)} %get-tuple-element.41), channel_id=1, source_target_pairs={{0,4},{4,0},{8,12},{12,8},{16,20},{20,16},{24,28},{28,24},{1,5},{5... | collective-permute-start | bytes 1572872 | tf_op jit(solution)/shard_map/ppermute | solution.py:472
  16.1 19.2 %collective-permute-start.6 = (bf16[256,256]{1,0:T(8,128)(2,1)}, bf16[256,256]{1,0:T(8,128)(2,1)}, u32[]{:S(2)}, u32[]{:S(2)}) collective-permute-start(bf16[256,256]{1,0:T(8,128)(2,1)} %get-tuple-element.43.refs_6_), channel_id=1, source_target_pairs={{0,2},{1,3},{4,6},{5,7},{8,10},{9,11},{12,14},{13,15},{16,18},{17,... | collective-permute-start | bytes 393224 | tf_op jit(solution)/shard_map/ppermute | solution.py:417
  17.4 23.5 %collective-permute-start.7 = (bf16[256,256]{1,0:T(8,128)(2,1)}, bf16[256,256]{1,0:T(8,128)(2,1)}, u32[]{:S(2)}, u32[]{:S(2)}) collective-permute-start(bf16[256,256]{1,0:T(8,128)(2,1)} %get-tuple-element.47), channel_id=1, source_target_pairs={{0,24},{4,28},{8,2},{12,6},{16,10},{20,14},{24,18},{28,22},{1,25},... | collective-permute-start | bytes 393224 | tf_op jit(solution)/shard_map/ppermute | solution.py:406
  22.6 18.4 %collective-permute-start.8 = (bf16[256,256]{1,0:T(8,128)(2,1)S(1)}, bf16[256,256]{1,0:T(8,128)(2,1)}, u32[]{:S(2)}, u32[]{:S(2)}) collective-permute-start(bf16[256,256]{1,0:T(8,128)(2,1)S(1)} %get-tuple-element.48), channel_id=1, source_target_pairs={{0,16},{4,20},{8,24},{12,28},{16,2},{20,6},{24,10},{28,14},{1,17},... | collective-permute-start | bytes 393224 | tf_op jit(solution)/shard_map/ppermute | solution.py:406
  24.5 16.8 %collective-permute-start.9 = (bf16[256,256]{1,0:T(8,128)(2,1)S(1)}, bf16[256,256]{1,0:T(8,128)(2,1)}, u32[]{:S(2)}, u32[]{:S(2)}) collective-permute-start(bf16[256,256]{1,0:T(8,128)(2,1)S(1)} %get-tuple-element.49), channel_id=1, source_target_pairs={{0,8},{4,12},{8,16},{12,20},{16,24},{20,28},{24,2},{28,6},{1,9},{5... | collective-permute-start | bytes 393224 | tf_op jit(solution)/shard_map/ppermute | solution.py:406
  28.2 13.1 %collective-permute-start.5 = (bf16[128,2048]{1,0:T(8,128)(2,1)S(1)}, bf16[128,2048]{1,0:T(8,128)(2,1)S(1)}, u32[]{:S(2)}, u32[]{:S(2)}) collective-permute-start(bf16[128,2048]{1,0:T(8,128)(2,1)S(1)} %get-tuple-element.46), channel_id=1, source_target_pairs={{0,4},{4,0},{8,12},{12,8},{16,20},{20,16},{24,28},{28,24},{1,5},{5... | collective-permute-start | bytes 1572872 | tf_op jit(solution)/shard_map/ppermute | solution.py:474
  35.3 12.4 %collective-permute-start.10 = (bf16[256,256]{1,0:T(8,128)(2,1)S(1)}, bf16[256,256]{1,0:T(8,128)(2,1)S(1)}, u32[]{:S(2)}, u32[]{:S(2)}) collective-permute-start(bf16[256,256]{1,0:T(8,128)(2,1)S(1)} %get-tuple-element.53), channel_id=1, source_target_pairs={{8,0},{12,4},{16,8},{20,12},{24,16},{28,20},{0,24},{4,28},{9,1},{1... | collective-permute-start | bytes 393224 | tf_op jit(solution)/shard_map/ppermute | solution.py:406
  40.9 10.1 %collective-permute-start.11 = (bf16[256,256]{1,0:T(8,128)(2,1)S(1)}, bf16[256,256]{1,0:T(8,128)(2,1)S(1)}, u32[]{:S(2)}, u32[]{:S(2)}) collective-permute-start(bf16[256,256]{1,0:T(8,128)(2,1)S(1)} %get-tuple-element.54), channel_id=1, source_target_pairs={{16,0},{20,4},{24,8},{28,12},{0,16},{4,20},{8,24},{12,28},{17,1},{... | collective-permute-start | bytes 393224 | tf_op jit(solution)/shard_map/ppermute | solution.py:406
  40.9 10.1 %collective-permute-start.12 = (bf16[256,256]{1,0:T(8,128)(2,1)S(1)}, bf16[256,256]{1,0:T(8,128)(2,1)S(1)}, u32[]{:S(2)}, u32[]{:S(2)}) collective-permute-start(bf16[256,256]{1,0:T(8,128)(2,1)S(1)} %get-tuple-element.55), channel_id=1, source_target_pairs={{24,0},{28,4},{0,8},{4,12},{8,16},{12,20},{16,24},{20,28},{25,1},{... | collective-permute-start | bytes 393224 | tf_op jit(solution)/shard_map/ppermute | solution.py:406
  51.2 19.5 %collective-permute-start.13 = (bf16[256,1024]{1,0:T(8,128)(2,1)S(1)}, bf16[256,1024]{1,0:T(8,128)(2,1)S(1)}, u32[]{:S(2)}, u32[]{:S(2)}) collective-permute-start(bf16[256,1024]{1,0:T(8,128)(2,1)S(1)} %get-tuple-element.61), channel_id=1, source_target_pairs={{0,4},{4,0},{8,12},{12,8},{16,20},{20,16},{24,28},{28,24},{1,5},{5... | collective-permute-start | bytes 1572872 | tf_op jit(solution)/shard_map/ppermute | solution.py:526
  52.6 11.0 %collective-permute-start.14 = (bf16[256,256]{1,0:T(8,128)(2,1)S(1)}, bf16[256,256]{1,0:T(8,128)(2,1)S(1)}, u32[]{:S(2)}, u32[]{:S(2)}) collective-permute-start(bf16[256,256]{1,0:T(8,128)(2,1)S(1)} %get-tuple-element.65), channel_id=1, source_target_pairs={{2,0},{3,1},{6,4},{7,5},{10,8},{11,9},{14,12},{15,13},{18,16},{19,... | collective-permute-start | bytes 393224 | tf_op jit(solution)/shard_map/ppermute | solution.py:417
  53.8 9.7 %collective-permute-start.15 = (bf16[256,256]{1,0:T(8,128)(2,1)S(1)}, bf16[256,256]{1,0:T(8,128)(2,1)S(1)}, u32[]{:S(2)}, u32[]{:S(2)}) collective-permute-start(bf16[256,256]{1,0:T(8,128)(2,1)S(1)} %get-tuple-element.66), channel_id=1, source_target_pairs={{8,0},{12,4},{16,8},{20,12},{24,16},{28,20},{2,24},{6,28},{9,1},{1... | collective-permute-start | bytes 393224 | tf_op jit(solution)/shard_map/ppermute | solution.py:406
  59.1 11.3 %collective-permute-start.16 = (bf16[256,256]{1,0:T(8,128)(2,1)S(1)}, bf16[256,256]{1,0:T(8,128)(2,1)S(1)}, u32[]{:S(2)}, u32[]{:S(2)}) collective-permute-start(bf16[256,256]{1,0:T(8,128)(2,1)S(1)} %get-tuple-element.67), channel_id=1, source_target_pairs={{16,0},{20,4},{24,8},{28,12},{2,16},{6,20},{10,24},{14,28},{17,1},... | collective-permute-start | bytes 393224 | tf_op jit(solution)/shard_map/ppermute | solution.py:406
  61.6 8.8 %collective-permute-start.17 = (bf16[256,256]{1,0:T(8,128)(2,1)S(1)}, bf16[256,256]{1,0:T(8,128)(2,1)S(1)}, u32[]{:S(2)}, u32[]{:S(2)}) collective-permute-start(bf16[256,256]{1,0:T(8,128)(2,1)S(1)} %get-tuple-element.68), channel_id=1, source_target_pairs={{24,0},{28,4},{2,8},{6,12},{10,16},{14,20},{18,24},{22,28},{25,1},... | collective-permute-start | bytes 393224 | tf_op jit(solution)/shard_map/ppermute | solution.py:406
  70.8 8.6 %collective-permute-start.18 = (bf16[128,2048]{1,0:T(8,128)(2,1)S(1)}, bf16[128,2048]{1,0:T(8,128)(2,1)S(1)}, u32[]{:S(2)}, u32[]{:S(2)}) collective-permute-start(bf16[128,2048]{1,0:T(8,128)(2,1)S(1)} %cross.1), channel_id=1, source_target_pairs={{0,1},{4,5},{8,9},{12,13},{16,17},{20,21},{24,25},{28,29},{1,0},{5... | collective-permute-start | bytes 1572872 | tf_op jit(solution)/shard_map/ppermute | solution.py:542
  73.9 2.1 %collective-permute-start.19 = (bf16[128,256]{1,0:T(8,128)(2,1)S(1)}, bf16[128,256]{1,0:T(8,128)(2,1)S(1)}, u32[]{:S(2)}, u32[]{:S(2)}) collective-permute-start(bf16[128,256]{1,0:T(8,128)(2,1)S(1)} %get-tuple-element.70), channel_id=1, source_target_pairs={{0,1},{4,5},{8,9},{12,13},{16,17},{20,21},{24,25},{28,29},{1,0},{5... | collective-permute-start | bytes 196616 | tf_op jit(solution)/shard_map/ppermute | solution.py:389
  73.9 3.1 %collective-permute-start.20 = (bf16[128,256]{1,0:T(8,128)(2,1)S(1)}, bf16[128,256]{1,0:T(8,128)(2,1)S(1)}, u32[]{:S(2)}, u32[]{:S(2)}) collective-permute-start(bf16[128,256]{1,0:T(8,128)(2,1)S(1)} %get-tuple-element.71), channel_id=1, source_target_pairs={{0,4},{4,0},{8,12},{12,8},{16,20},{20,16},{24,28},{28,24},{1,5},{5... | collective-permute-start | bytes 196616 | tf_op jit(solution)/shard_map/ppermute | solution.py:389
  74.4 5.0 %collective-permute-start.21 = (bf16[128,256]{1,0:T(8,128)(2,1)S(1)}, bf16[128,256]{1,0:T(8,128)(2,1)S(1)}, u32[]{:S(2)}, u32[]{:S(2)}) collective-permute-start(bf16[128,256]{1,0:T(8,128)(2,1)S(1)} %get-tuple-element.72), channel_id=1, source_target_pairs={{0,5},{4,1},{8,13},{12,9},{16,21},{20,17},{24,29},{28,25},{1,4},{5... | collective-permute-start | bytes 196616 | tf_op jit(solution)/shard_map/ppermute | solution.py:389

commit v4 on v3

--- a/solution.py
+++ b/solution.py
@@ -301,6 +301,10 @@
             out[...] = jnp.zeros_like(out)
 
 
+def swapped(parts):
+    return [*parts[1:2], *parts[:1], *parts[2:]]
+
+
 def add_terms(n_out, up, down, terms):
     _, _, z = place()
     for k, term in enumerate(terms, 1):
@@ -312,7 +316,7 @@
 
 
 def odd_sum_kernel(n_out, n_terms, own_odd, *refs):
-    terms, own_even, (odd_out, even_out) = refs[:n_terms], refs[n_terms:-2], refs[-2:]
+    terms, own_even, (odd_out, even_out) = swapped(refs[:n_terms]), refs[n_terms:-2], refs[-2:]
     even = own_even[0][...] if own_even else jnp.zeros(even_out.shape, F32)
     odd_out[...], even_out[...] = add_terms(n_out, own_odd[...], even, terms)
 
@@ -320,6 +324,7 @@
 def home_kernel(n_out, n_terms, own_even, odd_total, even_total, *refs):
     outs, total = refs[-5:-1], refs[-1]
     rim, terms = refs[: -5 - n_terms], refs[-5 - n_terms : -5]
+    terms = swapped(terms)
     tok = own_even.shape[0] // 2
     odd = odd_total[...]
     if rim:
@@ -519,7 +524,7 @@
     odd_total, even_total, dq_send, *even_sent = vmem_call(
         functools.partial(odd_sum_kernel, n_out, len(shifts)),
         [sum_shape, sum_shape],
-        (odd_sums[far], *odd_back, *([odd_sums[0]] if whole_ring else [])),
+        (odd_sums[far], *swapped(odd_back), *([odd_sums[0]] if whole_ring else [])),
         through=[dq_send, *sent(even_sums)],
         name="odd_sum",
     )
@@ -529,7 +534,7 @@
     home = vmem_call(
         functools.partial(home_kernel, n_out, len(shifts)),
         [shape(tok, 2 * kv_width, F32)] + [shape(tok, 2 * kv_width)] * 3,
-        (even_sums[far], odd_total, even_total, *rim_home, *even_back),
+        (even_sums[far], odd_total, even_total, *rim_home, *swapped(even_back)),
         scratch=[pltpu.VMEM((2, pair, 2 * kv_width), F32)],
         name="home",
     )

time: 81 us -> 77.9 us (0.962)
  starting transfers between devices: 43.3 us -> 39.1 us
  Pallas kernels: 15.4 us -> 17.8 us
  waiting for transfers between devices: 16.2 us -> 14.6 us
    ppermute x9, starting transfers between devices: 24.6 us -> 20.6 us  [along_z(): lax.ppermute(part, both, [(b, a) for a, b in route] if back else route)]
    pallas_call x8, Pallas kernels: 15.4 us -> 17.8 us  [vmem_call(): pl.pallas_call(run, out_shape=list(out_shapes) + [jax.ShapeDtypeStruct(t....]
    ppermute x9, waiting for transfers between devices: 10.2 us -> 8.58 us  [along_z(): lax.ppermute(part, both, [(b, a) for a, b in route] if back else route)]
  transfers between devices with their start and end apart: 23 -> 23, of which waited for: 6 -> 7; matrix products, arithmetic and copies ran while one was open for 5% -> 5% of each run, Pallas kernels for 16% -> 20%
where the time goes in v4:
time: 77.9 us; the launch traced here: 77.1 us
  starting transfers between devices  39.1 us (50%)
  Pallas kernels  17.8 us (23%)
  waiting for transfers between devices  14.6 us (19%)
  local copies, waits for them, and re-layouts  3.51 us (5%)
  other arithmetic  1.2 us (2%)
  between operations  0.87 us (1%)
    ppermute x9, starting transfers between devices, along_z(): lax.ppermute(part, both, [(b, a) for a, b in route] if back else route)  20.6 us
    pallas_call x8, Pallas kernels, vmem_call(): pl.pallas_call(run, out_shape=list(out_shapes) + [jax.ShapeDtypeStruct(t....  17.8 us
    ppermute x9, waiting for transfers between devices, along_z(): lax.ppermute(part, both, [(b, a) for a, b in route] if back else route)  8.58 us
    ppermute x6, starting transfers between devices, to_partners(): lax.ppermute(part, both, route)  4.66 us
    all_to_all x1, starting transfers between devices, gathered(): lax.all_to_all(pieces.reshape(n_out, pair, -1), 'swap', 0, 0, axis_index_...  4.59 us
    ppermute x6, waiting for transfers between devices, to_partners(): lax.ppermute(part, both, route)  4.24 us
    ppermute x1, starting transfers between devices, body(): lax.ppermute(dq_cross, both, routes[0])  3.35 us
    slice x1, local copies, waits for them, and re-layouts, halves(): x[:, i * q_width:(i + 1) * q_width]  2.59 us
  transfers between devices with their start and end apart: 23, of which 7 were waited for; matrix products, arithmetic and copies ran while one was open for 5% of the time, Pallas kernels for 20%

profile of v4, /device:TPU:3, one launch (start us, length us, event | category | flops | bytes accessed | tf_op | source)
XLA Modules:
  0.0 77.1 jit_solution(5905134110389954097)
XLA Ops:
  0.7 0.9 %constant_dynamic-slice_fusion.6 = (bf16[128,128]{1,0:T(8,128)(2,1)S(1)}, bf16[128,128]{1,0:T(8,128)(2,1)S(1)}, bf16[128,128]{1,0:T(8,128)(2,1)S(1)}, bf16[128,1...) fusion(bf16[128,512]{1,0:T(8,128)(2,1)} %param.7, ...), kind=kLoop, calls=%fused_computation.12 | loop fusion | bytes 524304 | tf_op jit(solution)/shard_map/dynamic_slice | solution.py:449
  1.6 0.7 collective-permute-start
  2.3 1.3 %collective-permute-start.1 = (bf16[128,256]{1,0:T(8,128)(2,1)S(1)}, bf16[128,256]{1,0:T(8,128)(2,1)S(1)}, u32[]{:S(2)}, u32[]{:S(2)}) collective-permute-start(bf16[128,256]{1,0:T(8,128)(2,1)S(1)} %pad_maximum_fusion.4), channel_id=1, source_target_pairs={{0,4},{4,0},{8,12},{12,8},{16,20},{20,16},{24,28},{28,24},{1,5},{5... | collective-permute-start | bytes 196616 | tf_op jit(solution)/shard_map/ppermute | solution.py:394
  3.7 0.5 collective-permute-start.2
  4.1 2.6 %constant_dynamic-slice_fusion = (bf16[128,1024]{1,0:T(8,128)(2,1)S(1)}, bf16[128,1024]{1,0:T(8,128)(2,1)S(1)}, bf16[128,1024]{1,0:T(8,128)(2,1)S(1)}, bf16[128,...) fusion(bf16[128,4096]{1,0:T(8,128)(2,1)} %param.8, ...), kind=kLoop, calls=%fused_computation.6 | loop fusion | bytes 4194320 | tf_op jit(solution)/shard_map/slice | solution.py:459
  6.7 0.1 pad_maximum_fusion.1.refs_4_
  6.8 0.0 collective-permute-done.refs_1_
  6.8 0.9 %collective-permute-done.2.refs_3_ = bf16[128,256]{1,0:T(8,128)(2,1)S(1)} collective-permute-done((bf16[128,256]{1,0:T(8,128)(2,1)S(1)}, bf16[128,256]{1,0:T(8,128)(2,1)S(1)}, u32[]{:S(2)}, u32[]{:S(2)}) %collective-permute-start.2) | collective-permute-done | bytes 65568 | tf_op jit(solution)/shard_map/ppermute | solution.py:394
  7.7 1.0 %payload.1 = (bf16[256,256]{1,0:T(8,128)(2,1)S(1)}, bf16[256,256]{1,0:T(8,128)(2,1)}, bf16[1024,256]{1,0:T(8,128)(2,1)}, bf16[256,256]{1,0:T(8,128)(2,1)S(1)}, b...) custom-call(bf16[128,256]{1,0:T(8,128)(2,1)S(1)} %pad_maximum_fusion, ...), custom_call_target="tpu_custom_call", output_to_operand_aliasing={{6}: (4, {})} | custom-call | tf_op jit(solution)/shard_map/payload/pallas_call | solution.py:41
  8.7 0.4 collective-permute-start.3
  9.1 4.6 %all-to-all-start = ((bf16[4,256,256]{2,1,0:T(8,128)(2,1)}), bf16[4,256,256]{2,1,0:T(8,128)(2,1)S(1)}, u32[]{:S(2)}, u32[]{:S(2)}) async-start(bf16[4,256,256]{2,1,0:T(8,128)(2,1)} %bitcast.1), calls=%async_computation | async-start | bytes 1048576 | tf_op jit(solution)/shard_map/all_to_all | solution.py:416
  13.7 1.1 %pad_maximum_fusion.refs_0_ = bf16[128,4096]{1,0:T(8,128)(2,1)S(1)} fusion(bf16[128,1024]{1,0:T(8,128)(2,1)S(1)} %get-tuple-element.80, bf16[128,1024]{1,0:T(8,128)(2,1)} %get-tuple-element.89, bf16[128,1024]{1,0:T(8,128)(2,1)S(1)} %get-tuple-element.78, bf16[128,1024]{1,0:T(8,128)(2,1)} %get-tuple-element.91), kind=kLoop, calls=%fused_computation | loop fusion | flops 4194304 | bytes 2097152 | tf_op jit(solution)/shard_map/concatenate | solution.py:458
  14.8 0.0 collective-permute-done.3.refs_1_
  14.8 0.0 copy-start
  14.8 0.2 choose_qg.1
  15.0 1.1 %collective-permute-start.4 = (bf16[128,2048]{1,0:T(8,128)(2,1)S(1)}, bf16[128,2048]{1,0:T(8,128)(2,1)S(1)}, u32[]{:S(2)}, u32[]{:S(2)}) collective-permute-start(bf16[128,2048]{1,0:T(8,128)(2,1)S(1)} %get-tuple-element.41), channel_id=1, source_target_pairs={{0,4},{4,0},{8,12},{12,8},{16,20},{20,16},{24,28},{28,24},{1,5},{5... | collective-permute-start | bytes 1572872 | tf_op jit(solution)/shard_map/ppermute | solution.py:477
  16.1 1.3 %collective-permute-start.6 = (bf16[256,256]{1,0:T(8,128)(2,1)}, bf16[256,256]{1,0:T(8,128)(2,1)}, u32[]{:S(2)}, u32[]{:S(2)}) collective-permute-start(bf16[256,256]{1,0:T(8,128)(2,1)} %get-tuple-element.43.refs_6_), channel_id=1, source_target_pairs={{0,2},{1,3},{4,6},{5,7},{8,10},{9,11},{12,14},{13,15},{16,18},{17,... | collective-permute-start | bytes 393224 | tf_op jit(solution)/shard_map/ppermute | solution.py:422
  17.4 5.2 %collective-permute-start.7 = (bf16[256,256]{1,0:T(8,128)(2,1)}, bf16[256,256]{1,0:T(8,128)(2,1)}, u32[]{:S(2)}, u32[]{:S(2)}) collective-permute-start(bf16[256,256]{1,0:T(8,128)(2,1)} %get-tuple-element.47), channel_id=1, source_target_pairs={{0,24},{4,28},{8,2},{12,6},{16,10},{20,14},{24,18},{28,22},{1,25},... | collective-permute-start | bytes 393224 | tf_op jit(solution)/shard_map/ppermute | solution.py:411
  22.6 1.9 %collective-permute-start.8 = (bf16[256,256]{1,0:T(8,128)(2,1)S(1)}, bf16[256,256]{1,0:T(8,128)(2,1)}, u32[]{:S(2)}, u32[]{:S(2)}) collective-permute-start(bf16[256,256]{1,0:T(8,128)(2,1)S(1)} %get-tuple-element.48), channel_id=1, source_target_pairs={{0,16},{4,20},{8,24},{12,28},{16,2},{20,6},{24,10},{28,14},{1,17},... | collective-permute-start | bytes 393224 | tf_op jit(solution)/shard_map/ppermute | solution.py:411
  24.5 1.9 %collective-permute-start.9 = (bf16[256,256]{1,0:T(8,128)(2,1)S(1)}, bf16[256,256]{1,0:T(8,128)(2,1)}, u32[]{:S(2)}, u32[]{:S(2)}) collective-permute-start(bf16[256,256]{1,0:T(8,128)(2,1)S(1)} %get-tuple-element.49), channel_id=1, source_target_pairs={{0,8},{4,12},{8,16},{12,20},{16,24},{20,28},{24,2},{28,6},{1,9},{5... | collective-permute-start | bytes 393224 | tf_op jit(solution)/shard_map/ppermute | solution.py:411
  26.4 1.8 %collective-permute-done.4.refs_1_ = bf16[128,2048]{1,0:T(8,128)(2,1)S(1)} collective-permute-done((bf16[128,2048]{1,0:T(8,128)(2,1)S(1)}, bf16[128,2048]{1,0:T(8,128)(2,1)S(1)}, u32[]{:S(2)}, u32[]{:S(2)}) %collective-permute-start.4) | collective-permute-done | bytes 524320 | tf_op jit(solution)/shard_map/ppermute | solution.py:477
  28.2 0.9 %collective-permute-start.5 = (bf16[128,2048]{1,0:T(8,128)(2,1)S(1)}, bf16[128,2048]{1,0:T(8,128)(2,1)S(1)}, u32[]{:S(2)}, u32[]{:S(2)}) collective-permute-start(bf16[128,2048]{1,0:T(8,128)(2,1)S(1)} %get-tuple-element.46), channel_id=1, source_target_pairs={{0,4},{4,0},{8,12},{12,8},{16,20},{20,16},{24,28},{28,24},{1,5},{5... | collective-permute-start | bytes 1572872 | tf_op jit(solution)/shard_map/ppermute | solution.py:479
  29.1 0.0 all-to-all-done
  29.1 9.4 %attend_odd.1 = (bf16[128,1024]{1,0:T(8,128)(2,1)S(1)}, bf16[128,1024]{1,0:T(8,128)(2,1)S(1)}, f32[256,256]{1,0:T(8,128)S(1)}, bf16[256,256]{1,0:T(8,128)(2,1)S(...) custom-call(bf16[128,2048]{1,0:T(8,128)(2,1)S(1)} %get-tuple-element.40.refs_0_, ...), custom_call_target="tpu_custom_call" | custom-call | flops 6000000000 | tf_op jit(solution)/shard_map/attend_odd/pallas_call | solution.py:41
  38.5 0.0 collective-permute-done.6.refs_4_
  38.5 1.1 %collective-permute-start.10 = (bf16[256,256]{1,0:T(8,128)(2,1)S(1)}, bf16[256,256]{1,0:T(8,128)(2,1)S(1)}, u32[]{:S(2)}, u32[]{:S(2)}) collective-permute-start(bf16[256,256]{1,0:T(8,128)(2,1)S(1)} %get-tuple-element.53), channel_id=1, source_target_pairs={{16,0},{20,4},{24,8},{28,12},{0,16},{4,20},{8,24},{12,28},{17,1},{... | collective-permute-start | bytes 393224 | tf_op jit(solution)/shard_map/ppermute | solution.py:411
  39.7 1.4 %collective-permute-start.11 = (bf16[256,256]{1,0:T(8,128)(2,1)S(1)}, bf16[256,256]{1,0:T(8,128)(2,1)S(1)}, u32[]{:S(2)}, u32[]{:S(2)}) collective-permute-start(bf16[256,256]{1,0:T(8,128)(2,1)S(1)} %get-tuple-element.54), channel_id=1, source_target_pairs={{8,0},{12,4},{16,8},{20,12},{24,16},{28,20},{0,24},{4,28},{9,1},{1... | collective-permute-start | bytes 393224 | tf_op jit(solution)/shard_map/ppermute | solution.py:411
  41.0 0.3 collective-permute-start.12
  41.3 5.6 %attend_even.1 = (bf16[128,1024]{1,0:T(8,128)(2,1)S(1)}, bf16[256,1024]{1,0:T(8,128)(2,1)S(1)}, bf16[256,256]{1,0:T(8,128)(2,1)S(1)}, bf16[256,256]{1,0:T(8,128)...) custom-call(bf16[128,2048]{1,0:T(8,128)(2,1)S(1)} %get-tuple-element.45.refs_0_, ...), custom_call_target="tpu_custom_call" | custom-call | flops 6000000000 | tf_op jit(solution)/shard_map/attend_even/pallas_call | solution.py:41
  46.9 1.6 %collective-permute-done.10.refs_1_ = bf16[256,256]{1,0:T(8,128)(2,1)S(1)} collective-permute-done((bf16[256,256]{1,0:T(8,128)(2,1)S(1)}, bf16[256,256]{1,0:T(8,128)(2,1)S(1)}, u32[]{:S(2)}, u32[]{:S(2)}) %collective-permute-start.10) | collective-permute-done | bytes 131104 | tf_op jit(solution)/shard_map/ppermute | solution.py:411
  48.5 0.2 odd_sum.1
  48.6 0.9 %collective-permute-start.13 = (bf16[256,1024]{1,0:T(8,128)(2,1)S(1)}, bf16[256,1024]{1,0:T(8,128)(2,1)S(1)}, u32[]{:S(2)}, u32[]{:S(2)}) collective-permute-start(bf16[256,1024]{1,0:T(8,128)(2,1)S(1)} %get-tuple-element.61), channel_id=1, source_target_pairs={{0,4},{4,0},{8,12},{12,8},{16,20},{20,16},{24,28},{28,24},{1,5},{5... | collective-permute-start | bytes 1572872 | tf_op jit(solution)/shard_map/ppermute | solution.py:531
  49.6 1.3 %collective-permute-start.14 = (bf16[256,256]{1,0:T(8,128)(2,1)S(1)}, bf16[256,256]{1,0:T(8,128)(2,1)S(1)}, u32[]{:S(2)}, u32[]{:S(2)}) collective-permute-start(bf16[256,256]{1,0:T(8,128)(2,1)S(1)} %get-tuple-element.65), channel_id=1, source_target_pairs={{2,0},{3,1},{6,4},{7,5},{10,8},{11,9},{14,12},{15,13},{18,16},{19,... | collective-permute-start | bytes 393224 | tf_op jit(solution)/shard_map/ppermute | solution.py:422
  50.9 3.8 %collective-permute-start.15 = (bf16[256,256]{1,0:T(8,128)(2,1)S(1)}, bf16[256,256]{1,0:T(8,128)(2,1)S(1)}, u32[]{:S(2)}, u32[]{:S(2)}) collective-permute-start(bf16[256,256]{1,0:T(8,128)(2,1)S(1)} %get-tuple-element.66), channel_id=1, source_target_pairs={{16,0},{20,4},{24,8},{28,12},{2,16},{6,20},{10,24},{14,28},{17,1},... | collective-permute-start | bytes 393224 | tf_op jit(solution)/shard_map/ppermute | solution.py:411
  54.7 3.1 %collective-permute-start.16 = (bf16[256,256]{1,0:T(8,128)(2,1)S(1)}, bf16[256,256]{1,0:T(8,128)(2,1)S(1)}, u32[]{:S(2)}, u32[]{:S(2)}) collective-permute-start(bf16[256,256]{1,0:T(8,128)(2,1)S(1)} %get-tuple-element.67), channel_id=1, source_target_pairs={{8,0},{12,4},{16,8},{20,12},{24,16},{28,20},{2,24},{6,28},{9,1},{1... | collective-permute-start | bytes 393224 | tf_op jit(solution)/shard_map/ppermute | solution.py:411
  57.8 1.9 %collective-permute-start.17 = (bf16[256,256]{1,0:T(8,128)(2,1)S(1)}, bf16[256,256]{1,0:T(8,128)(2,1)S(1)}, u32[]{:S(2)}, u32[]{:S(2)}) collective-permute-start(bf16[256,256]{1,0:T(8,128)(2,1)S(1)} %get-tuple-element.68), channel_id=1, source_target_pairs={{24,0},{28,4},{2,8},{6,12},{10,16},{14,20},{18,24},{22,28},{25,1},... | collective-permute-start | bytes 393224 | tf_op jit(solution)/shard_map/ppermute | solution.py:411
  59.7 0.0 collective-permute-done.15.refs_4_
  59.7 2.3 %collective-permute-done.16.refs_5_ = bf16[256,256]{1,0:T(8,128)(2,1)S(1)} collective-permute-done((bf16[256,256]{1,0:T(8,128)(2,1)S(1)}, bf16[256,256]{1,0:T(8,128)(2,1)S(1)}, u32[]{:S(2)}, u32[]{:S(2)}) %collective-permute-start.16) | collective-permute-done | bytes 131104 | tf_op jit(solution)/shard_map/ppermute | solution.py:411
  62.1 4.6 %collective-permute-done.17.refs_6_ = bf16[256,256]{1,0:T(8,128)(2,1)S(1)} collective-permute-done((bf16[256,256]{1,0:T(8,128)(2,1)S(1)}, bf16[256,256]{1,0:T(8,128)(2,1)S(1)}, u32[]{:S(2)}, u32[]{:S(2)}) %collective-permute-start.17) | collective-permute-done | bytes 131104 | tf_op jit(solution)/shard_map/ppermute | solution.py:411
  66.7 0.3 home.1
  67.0 0.1 cross.1
  67.1 3.4 %collective-permute-start.18 = (bf16[128,2048]{1,0:T(8,128)(2,1)S(1)}, bf16[128,2048]{1,0:T(8,128)(2,1)S(1)}, u32[]{:S(2)}, u32[]{:S(2)}) collective-permute-start(bf16[128,2048]{1,0:T(8,128)(2,1)S(1)} %cross.1), channel_id=1, source_target_pairs={{0,1},{4,5},{8,9},{12,13},{16,17},{20,21},{24,25},{28,29},{1,0},{5... | collective-permute-start | bytes 1572872 | tf_op jit(solution)/shard_map/ppermute | solution.py:547
  70.5 0.1 collective-permute-start.19
  70.5 0.5 collective-permute-start.20
  71.0 1.6 %collective-permute-start.21 = (bf16[128,256]{1,0:T(8,128)(2,1)S(1)}, bf16[128,256]{1,0:T(8,128)(2,1)S(1)}, u32[]{:S(2)}, u32[]{:S(2)}) collective-permute-start(bf16[128,256]{1,0:T(8,128)(2,1)S(1)} %get-tuple-element.72), channel_id=1, source_target_pairs={{0,5},{4,1},{8,13},{12,9},{16,21},{20,17},{24,29},{28,25},{1,4},{5... | collective-permute-start | bytes 196616 | tf_op jit(solution)/shard_map/ppermute | solution.py:394
  72.6 1.0 %collective-permute-done.20.refs_6_ = bf16[128,256]{1,0:T(8,128)(2,1)S(1)} collective-permute-done((bf16[128,256]{1,0:T(8,128)(2,1)S(1)}, bf16[128,256]{1,0:T(8,128)(2,1)S(1)}, u32[]{:S(2)}, u32[]{:S(2)}) %collective-permute-start.20) | collective-permute-done | bytes 65568 | tf_op jit(solution)/shard_map/ppermute | solution.py:394
  73.7 2.3 %collective-permute-done.21.refs_7_ = bf16[128,256]{1,0:T(8,128)(2,1)S(1)} collective-permute-done((bf16[128,256]{1,0:T(8,128)(2,1)S(1)}, bf16[128,256]{1,0:T(8,128)(2,1)S(1)}, u32[]{:S(2)}, u32[]{:S(2)}) %collective-permute-start.21) | collective-permute-done | bytes 65568 | tf_op jit(solution)/shard_map/ppermute | solution.py:394
  76.0 1.2 %finish.1 = (bf16[128,4096]{1,0:T(8,128)(2,1)}, bf16[128,512]{1,0:T(8,128)(2,1)}, bf16[128,512]{1,0:T(8,128)(2,1)}) custom-call(bf16[128,1024]{1,0:T(8,128)(2,1)S(1)} %get-tuple-element.44.refs_0_, bf16[128,1024]{1,0:T(8,128)(2,1)S(1)} %get-tuple-element.51.refs_1_, bf16[256,1024]{1,0:T(8,128)(2,1)S(1)} %collective-permute-done.13.refs_2_, ...), custom_call_target="tpu_custom_call" | custom-call | tf_op jit(solution)/shard_map/finish/pallas_call | solution.py:41
  (16 shorter events, 0.1 us)
Async XLA Ops:
  1.6 5.2 %collective-permute-start = (bf16[128,256]{1,0:T(8,128)(2,1)S(1)}, bf16[128,256]{1,0:T(8,128)(2,1)S(1)}, u32[]{:S(2)}, u32[]{:S(2)}) collective-permute-start(bf16[128,256]{1,0:T(8,128)(2,1)S(1)} %pad_maximum_fusion.3), channel_id=1, source_target_pairs={{0,1},{4,5},{8,9},{12,13},{16,17},{20,21},{24,25},{28,29},{1,0},{5... | collective-permute-start | bytes 196616 | tf_op jit(solution)/shard_map/ppermute | solution.py:394
  2.3 4.5 %collective-permute-start.1 = (bf16[128,256]{1,0:T(8,128)(2,1)S(1)}, bf16[128,256]{1,0:T(8,128)(2,1)S(1)}, u32[]{:S(2)}, u32[]{:S(2)}) collective-permute-start(bf16[128,256]{1,0:T(8,128)(2,1)S(1)} %pad_maximum_fusion.4), channel_id=1, source_target_pairs={{0,4},{4,0},{8,12},{12,8},{16,20},{20,16},{24,28},{28,24},{1,5},{5... | collective-permute-start | bytes 196616 | tf_op jit(solution)/shard_map/ppermute | solution.py:394
  3.7 4.1 %collective-permute-start.2 = (bf16[128,256]{1,0:T(8,128)(2,1)S(1)}, bf16[128,256]{1,0:T(8,128)(2,1)S(1)}, u32[]{:S(2)}, u32[]{:S(2)}) collective-permute-start(bf16[128,256]{1,0:T(8,128)(2,1)S(1)} %pad_maximum_fusion.5), channel_id=1, source_target_pairs={{0,5},{4,1},{8,13},{12,9},{16,21},{20,17},{24,29},{28,25},{1,4},{5... | collective-permute-start | bytes 196616 | tf_op jit(solution)/shard_map/ppermute | solution.py:394
  8.7 6.1 %collective-permute-start.3 = (bf16[128,4096]{1,0:T(8,128)(2,1)S(1)}, bf16[128,4096]{1,0:T(8,128)(2,1)S(1)}, u32[]{:S(2)}, u32[]{:S(2)}) collective-permute-start(bf16[128,4096]{1,0:T(8,128)(2,1)S(1)} %get-tuple-element.38), channel_id=1, source_target_pairs={{0,1},{4,5},{8,9},{12,13},{16,17},{20,21},{24,25},{28,29},{1,0},{5... | collective-permute-start | bytes 3145736 | tf_op jit(solution)/shard_map/ppermute | solution.py:471
  9.1 20.0 %all-to-all-start = ((bf16[4,256,256]{2,1,0:T(8,128)(2,1)}), bf16[4,256,256]{2,1,0:T(8,128)(2,1)S(1)}, u32[]{:S(2)}, u32[]{:S(2)}) async-start(bf16[4,256,256]{2,1,0:T(8,128)(2,1)} %bitcast.1), calls=%async_computation | async-start | bytes 1048576 | tf_op jit(solution)/shard_map/all_to_all | solution.py:416
  14.8 14.3 %copy-start = (s32[4096]{0:T(1024)S(1)}, s32[4096]{0:T(1024)}, u32[]{:S(2)}) copy-start(s32[4096]{0:T(1024)} %refs_3_.3) | copy-start | bytes 49156
  15.0 13.2 %collective-permute-start.4 = (bf16[128,2048]{1,0:T(8,128)(2,1)S(1)}, bf16[128,2048]{1,0:T(8,128)(2,1)S(1)}, u32[]{:S(2)}, u32[]{:S(2)}) collective-permute-start(bf16[128,2048]{1,0:T(8,128)(2,1)S(1)} %get-tuple-element.41), channel_id=1, source_target_pairs={{0,4},{4,0},{8,12},{12,8},{16,20},{20,16},{24,28},{28,24},{1,5},{5... | collective-permute-start | bytes 1572872 | tf_op jit(solution)/shard_map/ppermute | solution.py:477
  16.1 22.4 %collective-permute-start.6 = (bf16[256,256]{1,0:T(8,128)(2,1)}, bf16[256,256]{1,0:T(8,128)(2,1)}, u32[]{:S(2)}, u32[]{:S(2)}) collective-permute-start(bf16[256,256]{1,0:T(8,128)(2,1)} %get-tuple-element.43.refs_6_), channel_id=1, source_target_pairs={{0,2},{1,3},{4,6},{5,7},{8,10},{9,11},{12,14},{13,15},{16,18},{17,... | collective-permute-start | bytes 393224 | tf_op jit(solution)/shard_map/ppermute | solution.py:422
  17.4 22.3 %collective-permute-start.7 = (bf16[256,256]{1,0:T(8,128)(2,1)}, bf16[256,256]{1,0:T(8,128)(2,1)}, u32[]{:S(2)}, u32[]{:S(2)}) collective-permute-start(bf16[256,256]{1,0:T(8,128)(2,1)} %get-tuple-element.47), channel_id=1, source_target_pairs={{0,24},{4,28},{8,2},{12,6},{16,10},{20,14},{24,18},{28,22},{1,25},... | collective-permute-start | bytes 393224 | tf_op jit(solution)/shard_map/ppermute | solution.py:411
  22.6 18.4 %collective-permute-start.8 = (bf16[256,256]{1,0:T(8,128)(2,1)S(1)}, bf16[256,256]{1,0:T(8,128)(2,1)}, u32[]{:S(2)}, u32[]{:S(2)}) collective-permute-start(bf16[256,256]{1,0:T(8,128)(2,1)S(1)} %get-tuple-element.48), channel_id=1, source_target_pairs={{0,16},{4,20},{8,24},{12,28},{16,2},{20,6},{24,10},{28,14},{1,17},... | collective-permute-start | bytes 393224 | tf_op jit(solution)/shard_map/ppermute | solution.py:411
  24.5 16.8 %collective-permute-start.9 = (bf16[256,256]{1,0:T(8,128)(2,1)S(1)}, bf16[256,256]{1,0:T(8,128)(2,1)}, u32[]{:S(2)}, u32[]{:S(2)}) collective-permute-start(bf16[256,256]{1,0:T(8,128)(2,1)S(1)} %get-tuple-element.49), channel_id=1, source_target_pairs={{0,8},{4,12},{8,16},{12,20},{16,24},{20,28},{24,2},{28,6},{1,9},{5... | collective-permute-start | bytes 393224 | tf_op jit(solution)/shard_map/ppermute | solution.py:411
  28.2 13.1 %collective-permute-start.5 = (bf16[128,2048]{1,0:T(8,128)(2,1)S(1)}, bf16[128,2048]{1,0:T(8,128)(2,1)S(1)}, u32[]{:S(2)}, u32[]{:S(2)}) collective-permute-start(bf16[128,2048]{1,0:T(8,128)(2,1)S(1)} %get-tuple-element.46), channel_id=1, source_target_pairs={{0,4},{4,0},{8,12},{12,8},{16,20},{20,16},{24,28},{28,24},{1,5},{5... | collective-permute-start | bytes 1572872 | tf_op jit(solution)/shard_map/ppermute | solution.py:479
  38.5 9.9 %collective-permute-start.10 = (bf16[256,256]{1,0:T(8,128)(2,1)S(1)}, bf16[256,256]{1,0:T(8,128)(2,1)S(1)}, u32[]{:S(2)}, u32[]{:S(2)}) collective-permute-start(bf16[256,256]{1,0:T(8,128)(2,1)S(1)} %get-tuple-element.53), channel_id=1, source_target_pairs={{16,0},{20,4},{24,8},{28,12},{0,16},{4,20},{8,24},{12,28},{17,1},{... | collective-permute-start | bytes 393224 | tf_op jit(solution)/shard_map/ppermute | solution.py:411
  39.7 8.8 %collective-permute-start.11 = (bf16[256,256]{1,0:T(8,128)(2,1)S(1)}, bf16[256,256]{1,0:T(8,128)(2,1)S(1)}, u32[]{:S(2)}, u32[]{:S(2)}) collective-permute-start(bf16[256,256]{1,0:T(8,128)(2,1)S(1)} %get-tuple-element.54), channel_id=1, source_target_pairs={{8,0},{12,4},{16,8},{20,12},{24,16},{28,20},{0,24},{4,28},{9,1},{1... | collective-permute-start | bytes 393224 | tf_op jit(solution)/shard_map/ppermute | solution.py:411
  41.0 7.4 %collective-permute-start.12 = (bf16[256,256]{1,0:T(8,128)(2,1)S(1)}, bf16[256,256]{1,0:T(8,128)(2,1)S(1)}, u32[]{:S(2)}, u32[]{:S(2)}) collective-permute-start(bf16[256,256]{1,0:T(8,128)(2,1)S(1)} %get-tuple-element.55), channel_id=1, source_target_pairs={{24,0},{28,4},{0,8},{4,12},{8,16},{12,20},{16,24},{20,28},{25,1},{... | collective-permute-start | bytes 393224 | tf_op jit(solution)/shard_map/ppermute | solution.py:411
  48.6 18.4 %collective-permute-start.13 = (bf16[256,1024]{1,0:T(8,128)(2,1)S(1)}, bf16[256,1024]{1,0:T(8,128)(2,1)S(1)}, u32[]{:S(2)}, u32[]{:S(2)}) collective-permute-start(bf16[256,1024]{1,0:T(8,128)(2,1)S(1)} %get-tuple-element.61), channel_id=1, source_target_pairs={{0,4},{4,0},{8,12},{12,8},{16,20},{20,16},{24,28},{28,24},{1,5},{5... | collective-permute-start | bytes 1572872 | tf_op jit(solution)/shard_map/ppermute | solution.py:531
  49.6 10.1 %collective-permute-start.14 = (bf16[256,256]{1,0:T(8,128)(2,1)S(1)}, bf16[256,256]{1,0:T(8,128)(2,1)S(1)}, u32[]{:S(2)}, u32[]{:S(2)}) collective-permute-start(bf16[256,256]{1,0:T(8,128)(2,1)S(1)} %get-tuple-element.65), channel_id=1, source_target_pairs={{2,0},{3,1},{6,4},{7,5},{10,8},{11,9},{14,12},{15,13},{18,16},{19,... | collective-permute-start | bytes 393224 | tf_op jit(solution)/shard_map/ppermute | solution.py:422
  50.9 8.9 %collective-permute-start.15 = (bf16[256,256]{1,0:T(8,128)(2,1)S(1)}, bf16[256,256]{1,0:T(8,128)(2,1)S(1)}, u32[]{:S(2)}, u32[]{:S(2)}) collective-permute-start(bf16[256,256]{1,0:T(8,128)(2,1)S(1)} %get-tuple-element.66), channel_id=1, source_target_pairs={{16,0},{20,4},{24,8},{28,12},{2,16},{6,20},{10,24},{14,28},{17,1},... | collective-permute-start | bytes 393224 | tf_op jit(solution)/shard_map/ppermute | solution.py:411
  54.7 7.4 %collective-permute-start.16 = (bf16[256,256]{1,0:T(8,128)(2,1)S(1)}, bf16[256,256]{1,0:T(8,128)(2,1)S(1)}, u32[]{:S(2)}, u32[]{:S(2)}) collective-permute-start(bf16[256,256]{1,0:T(8,128)(2,1)S(1)} %get-tuple-element.67), channel_id=1, source_target_pairs={{8,0},{12,4},{16,8},{20,12},{24,16},{28,20},{2,24},{6,28},{9,1},{1... | collective-permute-start | bytes 393224 | tf_op jit(solution)/shard_map/ppermute | solution.py:411
  57.8 8.9 %collective-permute-start.17 = (bf16[256,256]{1,0:T(8,128)(2,1)S(1)}, bf16[256,256]{1,0:T(8,128)(2,1)S(1)}, u32[]{:S(2)}, u32[]{:S(2)}) collective-permute-start(bf16[256,256]{1,0:T(8,128)(2,1)S(1)} %get-tuple-element.68), channel_id=1, source_target_pairs={{24,0},{28,4},{2,8},{6,12},{10,16},{14,20},{18,24},{22,28},{25,1},... | collective-permute-start | bytes 393224 | tf_op jit(solution)/shard_map/ppermute | solution.py:411
  67.1 8.8 %collective-permute-start.18 = (bf16[128,2048]{1,0:T(8,128)(2,1)S(1)}, bf16[128,2048]{1,0:T(8,128)(2,1)S(1)}, u32[]{:S(2)}, u32[]{:S(2)}) collective-permute-start(bf16[128,2048]{1,0:T(8,128)(2,1)S(1)} %cross.1), channel_id=1, source_target_pairs={{0,1},{4,5},{8,9},{12,13},{16,17},{20,21},{24,25},{28,29},{1,0},{5... | collective-permute-start | bytes 1572872 | tf_op jit(solution)/shard_map/ppermute | solution.py:547
  70.5 2.1 %collective-permute-start.19 = (bf16[128,256]{1,0:T(8,128)(2,1)S(1)}, bf16[128,256]{1,0:T(8,128)(2,1)S(1)}, u32[]{:S(2)}, u32[]{:S(2)}) collective-permute-start(bf16[128,256]{1,0:T(8,128)(2,1)S(1)} %get-tuple-element.70), channel_id=1, source_target_pairs={{0,1},{4,5},{8,9},{12,13},{16,17},{20,21},{24,25},{28,29},{1,0},{5... | collective-permute-start | bytes 196616 | tf_op jit(solution)/shard_map/ppermute | solution.py:394
  70.5 3.1 %collective-permute-start.20 = (bf16[128,256]{1,0:T(8,128)(2,1)S(1)}, bf16[128,256]{1,0:T(8,128)(2,1)S(1)}, u32[]{:S(2)}, u32[]{:S(2)}) collective-permute-start(bf16[128,256]{1,0:T(8,128)(2,1)S(1)} %get-tuple-element.71), channel_id=1, source_target_pairs={{0,4},{4,0},{8,12},{12,8},{16,20},{20,16},{24,28},{28,24},{1,5},{5... | collective-permute-start | bytes 196616 | tf_op jit(solution)/shard_map/ppermute | solution.py:394
  71.0 4.9 %collective-permute-start.21 = (bf16[128,256]{1,0:T(8,128)(2,1)S(1)}, bf16[128,256]{1,0:T(8,128)(2,1)S(1)}, u32[]{:S(2)}, u32[]{:S(2)}) collective-permute-start(bf16[128,256]{1,0:T(8,128)(2,1)S(1)} %get-tuple-element.72), channel_id=1, source_target_pairs={{0,5},{4,1},{8,13},{12,9},{16,21},{20,17},{24,29},{28,25},{1,4},{5... | collective-permute-start | bytes 196616 | tf_op jit(solution)/shard_map/ppermute | solution.py:394

commit v5 on v4

--- a/solution.py
+++ b/solution.py
@@ -195,8 +195,8 @@
     begin = lax.div(doc_scalars[first] - base, pair)
     begin_last = lax.div(doc_scalars[first + tok] - base, pair)
 
-    def rows_of(j):
-        return pl.ds(pl.multiple_of(j * pair, pair), pair)
+    def rows_of(j, count):
+        return pl.ds(pl.multiple_of(j * pair, pair), count * pair)
 
     def cols_of(n):
         return slice(n * step_cols, (n + 1) * step_cols)
@@ -212,24 +212,31 @@
     stats[2] = jnp.zeros(stats.shape[1:], F32)
     dq_cols[...] = jnp.zeros_like(dq_cols)
     t = lax.broadcasted_iota(jnp.int32, (1, tok), 1)
-    key_place = lax.broadcasted_iota(jnp.int32, (pair, tok), 0)
     lows = [starts[pl.ds(lax.div(first, 128) + unit, 1), :] for unit in (0, 1)]
 
     def columns_of(units):
         return [n for n in range(n_steps) if unit_of(n) in units]
 
     def over_slots(step):
-        lax.fori_loop(begin, begin_last, functools.partial(step, (0,)), 0)
-        lax.fori_loop(begin_last, n_slots, functools.partial(step, (0, 1)), 0)
-
-    def score_step(units, j, carry):
-        place_j = key_place + (base + j * pair)
+        def run(units, start, stop, sizes):
+            for size, larger in zip(sizes, (*sizes[1:], None)):
+                left = stop - start
+                steps = lax.div(left if larger is None else lax.rem(left, larger), size)
+                lax.fori_loop(0, steps, lambda i, c: step(units, size, start + size * i, c), 0)
+                start = start + size * steps
+
+        run((0,), begin, begin_last, (1, 2))
+        run((0, 1), begin_last, n_slots, (1, 2))
+
+    def score_step(units, count, j, carry):
+        rows = rows_of(j, count)
+        place_j = lax.broadcasted_iota(jnp.int32, (count * pair, tok), 0) + (base + j * pair)
         for unit in units:
             allowed = (place_j >= lows[unit]) & (place_j <= t + (first + unit * tok))
-            keys[unit, rows_of(j), HEAD_DIM:] = jnp.where(allowed, 0.0, -1e30).astype(BF16)
+            keys[unit, rows, HEAD_DIM:] = jnp.where(allowed, 0.0, -1e30).astype(BF16)
         for n in columns_of(units):
-            s = dot(keys[unit_of(n), rows_of(j), :], q_rows[cols_of(n), :], NT)
-            scores[rows_of(j), cols_of(n)] = s
+            s = dot(keys[unit_of(n), rows, :], q_rows[cols_of(n), :], NT)
+            scores[rows, cols_of(n)] = s
             stats[0, :, cols_of(n)] = jnp.maximum(stats[0, :, cols_of(n)], fold(jnp.max, s))
         return carry
 
@@ -238,12 +245,13 @@
         top = jnp.max(stats[0, :, cols_of(n)], axis=0, keepdims=True)
         stats[0, :, cols_of(n)] = jnp.broadcast_to(top, (8, step_cols))
 
-    def weight_step(units, j, carry):
+    def weight_step(units, count, j, carry):
+        rows = rows_of(j, count)
         for n in columns_of(units):
-            p = jnp.exp2((scores[rows_of(j), cols_of(n)] - stats[0, 0:1, cols_of(n)]) * scale)
-            scores[rows_of(j), cols_of(n)] = p
+            p = jnp.exp2((scores[rows, cols_of(n)] - stats[0, 0:1, cols_of(n)]) * scale)
+            scores[rows, cols_of(n)] = p
             stats[1, :, cols_of(n)] += fold(jnp.sum, p)
-            dweights[rows_of(j), cols_of(n)] = dot(vals[rows_of(j), :], g_rows[cols_of(n), :], NT)
+            dweights[rows, cols_of(n)] = dot(vals[rows, :], g_rows[cols_of(n), :], NT)
         return carry
 
     over_slots(weight_step)
@@ -251,16 +259,17 @@
         inv = 1.0 / jnp.sum(stats[1, :, cols_of(n)], axis=0, keepdims=True)
         stats[1, :, cols_of(n)] = jnp.broadcast_to(inv, (8, step_cols))
 
-    def value_step(units, j, carry):
-        total = jnp.zeros((pair, HEAD_DIM), F32)
+    def value_step(units, count, j, carry):
+        rows = rows_of(j, count)
+        total = jnp.zeros((count * pair, HEAD_DIM), F32)
         for n in columns_of(units):
-            d = dweights[rows_of(j), cols_of(n)]
-            w = scores[rows_of(j), cols_of(n)] * stats[1, 0:1, cols_of(n)]
+            d = dweights[rows, cols_of(n)]
+            w = scores[rows, cols_of(n)] * stats[1, 0:1, cols_of(n)]
             wb = w.astype(BF16)
             total = total + dot(wb, g_rows[cols_of(n), :], NN)
-            scores[rows_of(j), cols_of(n)] = w
+            scores[rows, cols_of(n)] = w
             stats[2, :, cols_of(n)] += fold(jnp.sum, wb.astype(F32) * d)
-        acc[rows_of(j), HEAD_DIM:] = total
+        acc[rows, HEAD_DIM:] = total
         return carry
 
     over_slots(value_step)
@@ -268,15 +277,16 @@
         rowdot = jnp.sum(stats[2, :, cols_of(n)], axis=0, keepdims=True)
         stats[2, :, cols_of(n)] = jnp.broadcast_to(rowdot, (8, step_cols))
 
-    def grad_step(units, j, carry):
-        total = jnp.zeros((pair, HEAD_DIM), F32)
-        k_cols = keys[0, rows_of(j), :HEAD_DIM].T
+    def grad_step(units, count, j, carry):
+        rows = rows_of(j, count)
+        total = jnp.zeros((count * pair, HEAD_DIM), F32)
+        k_cols = keys[0, rows, :HEAD_DIM].T
         for n in columns_of(units):
-            rest = dweights[rows_of(j), cols_of(n)] - stats[2, 0:1, cols_of(n)]
-            ds = (scores[rows_of(j), cols_of(n)] * rest).astype(BF16)
+            rest = dweights[rows, cols_of(n)] - stats[2, 0:1, cols_of(n)]
+            ds = (scores[rows, cols_of(n)] * rest).astype(BF16)
             total = total + dot(ds, q_rows[cols_of(n), :HEAD_DIM], NN)
             dq_cols[:, cols_of(n)] += dot(k_cols, ds, NN)
-        acc[rows_of(j), :HEAD_DIM] = total * inv_root
+        acc[rows, :HEAD_DIM] = total * inv_root
         return carry
 
     over_slots(grad_step)

time: 77.9 us -> 79.8 us (1.024)
  starting transfers between devices: 39.1 us -> 45.8 us
  Pallas kernels: 17.8 us -> 14.6 us
  waiting for transfers between devices: 14.6 us -> 13.8 us
    ppermute x9, starting transfers between devices: 20.6 us -> 24.2 us  [along_z(): lax.ppermute(part, both, [(b, a) for a, b in route] if back else route)]
    pallas_call x8, Pallas kernels: 17.8 us -> 14.6 us  [vmem_call(): pl.pallas_call(run, out_shape=list(out_shapes) + [jax.ShapeDtypeStruct(t....]
    ppermute x1, starting transfers between devices: 3.35 us -> 4.89 us  [body(): lax.ppermute(dq_cross, both, routes[0])]
    ppermute x2, starting transfers between devices: 2.57 us -> 4.09 us  [along_x(): lax.ppermute(part, 'blk', [(b, b + step) for b in range(n_blk) if 0 <= b...]
  transfers between devices with their start and end apart: 23 -> 23, of which waited for: 7 -> 7; matrix products, arithmetic and copies ran while one was open for 5% -> 5% of each run, Pallas kernels for 20% -> 15%
where the time goes in v5:
time: 79.8 us
  starting transfers between devices  45.8 us (57%)
  Pallas kernels  14.6 us (18%)
  waiting for transfers between devices  13.8 us (17%)
  local copies, waits for them, and re-layouts  3.51 us (4%)
  other arithmetic  1.2 us (2%)
  between operations  0.89 us (1%)
    ppermute x9, starting transfers between devices, along_z(): lax.ppermute(part, both, [(b, a) for a, b in route] if back else route)  24.2 us
    pallas_call x8, Pallas kernels, vmem_call(): pl.pallas_call(run, out_shape=list(out_shapes) + [jax.ShapeDtypeStruct(t....  14.6 us
    ppermute x9, waiting for transfers between devices, along_z(): lax.ppermute(part, both, [(b, a) for a, b in route] if back else route)  7.94 us
    ppermute x1, starting transfers between devices, body(): lax.ppermute(dq_cross, both, routes[0])  4.89 us
    ppermute x6, starting transfers between devices, to_partners(): lax.ppermute(part, both, route)  4.66 us
    all_to_all x1, starting transfers between devices, gathered(): lax.all_to_all(pieces.reshape(n_out, pair, -1), 'swap', 0, 0, axis_index_...  4.59 us
    ppermute x2, starting transfers between devices, along_x(): lax.ppermute(part, 'blk', [(b, b + step) for b in range(n_blk) if 0 <= b...  4.09 us
    ppermute x6, waiting for transfers between devices, to_partners(): lax.ppermute(part, both, route)  4.05 us
  transfers between devices with their start and end apart: 23, of which 7 were waited for; matrix products, arithmetic and copies ran while one was open for 5% of the time, Pallas kernels for 15%

profile of v5, /device:TPU:3, one launch (start us, length us, event | category | flops | bytes accessed | tf_op | source)
XLA Modules:
  0.0 79.8 jit_solution(13711198230494705334)
XLA Ops:
  0.7 0.9 %constant_dynamic-slice_fusion.6 = (bf16[128,128]{1,0:T(8,128)(2,1)S(1)}, bf16[128,128]{1,0:T(8,128)(2,1)S(1)}, bf16[128,128]{1,0:T(8,128)(2,1)S(1)}, bf16[128,1...) fusion(bf16[128,512]{1,0:T(8,128)(2,1)} %param.7, ...), kind=kLoop, calls=%fused_computation.12 | loop fusion | bytes 524304 | tf_op jit(solution)/shard_map/dynamic_slice | solution.py:459
  1.6 0.7 collective-permute-start
  2.3 1.3 %collective-permute-start.1 = (bf16[128,256]{1,0:T(8,128)(2,1)S(1)}, bf16[128,256]{1,0:T(8,128)(2,1)S(1)}, u32[]{:S(2)}, u32[]{:S(2)}) collective-permute-start(bf16[128,256]{1,0:T(8,128)(2,1)S(1)} %pad_maximum_fusion.4), channel_id=1, source_target_pairs={{0,4},{4,0},{8,12},{12,8},{16,20},{20,16},{24,28},{28,24},{1,5},{5... | collective-permute-start | bytes 196616 | tf_op jit(solution)/shard_map/ppermute | solution.py:404
  3.7 0.5 collective-permute-start.2
  4.1 2.6 %constant_dynamic-slice_fusion = (bf16[128,1024]{1,0:T(8,128)(2,1)S(1)}, bf16[128,1024]{1,0:T(8,128)(2,1)S(1)}, bf16[128,1024]{1,0:T(8,128)(2,1)S(1)}, bf16[128,...) fusion(bf16[128,4096]{1,0:T(8,128)(2,1)} %param.8, ...), kind=kLoop, calls=%fused_computation.6 | loop fusion | bytes 4194320 | tf_op jit(solution)/shard_map/slice | solution.py:469
  6.7 0.1 pad_maximum_fusion.1.refs_4_
  6.8 0.0 collective-permute-done.refs_1_
  6.8 0.0 collective-permute-done.1.refs_2_
  6.8 0.9 %collective-permute-done.2.refs_3_ = bf16[128,256]{1,0:T(8,128)(2,1)S(1)} collective-permute-done((bf16[128,256]{1,0:T(8,128)(2,1)S(1)}, bf16[128,256]{1,0:T(8,128)(2,1)S(1)}, u32[]{:S(2)}, u32[]{:S(2)}) %collective-permute-start.2) | collective-permute-done | bytes 65568 | tf_op jit(solution)/shard_map/ppermute | solution.py:404
  7.7 1.0 %payload.1 = (bf16[256,256]{1,0:T(8,128)(2,1)S(1)}, bf16[256,256]{1,0:T(8,128)(2,1)}, bf16[1024,256]{1,0:T(8,128)(2,1)}, bf16[256,256]{1,0:T(8,128)(2,1)S(1)}, b...) custom-call(bf16[128,256]{1,0:T(8,128)(2,1)S(1)} %pad_maximum_fusion, ...), custom_call_target="tpu_custom_call", output_to_operand_aliasing={{6}: (4, {})} | custom-call | tf_op jit(solution)/shard_map/payload/pallas_call | solution.py:41
  8.7 0.4 collective-permute-start.3
  9.1 4.6 %all-to-all-start = ((bf16[4,256,256]{2,1,0:T(8,128)(2,1)}), bf16[4,256,256]{2,1,0:T(8,128)(2,1)S(1)}, u32[]{:S(2)}, u32[]{:S(2)}) async-start(bf16[4,256,256]{2,1,0:T(8,128)(2,1)} %bitcast.1), calls=%async_computation | async-start | bytes 1048576 | tf_op jit(solution)/shard_map/all_to_all | solution.py:426
  13.7 1.1 %pad_maximum_fusion.refs_0_ = bf16[128,4096]{1,0:T(8,128)(2,1)S(1)} fusion(bf16[128,1024]{1,0:T(8,128)(2,1)S(1)} %get-tuple-element.80, bf16[128,1024]{1,0:T(8,128)(2,1)} %get-tuple-element.89, bf16[128,1024]{1,0:T(8,128)(2,1)S(1)} %get-tuple-element.78, bf16[128,1024]{1,0:T(8,128)(2,1)} %get-tuple-element.91), kind=kLoop, calls=%fused_computation | loop fusion | flops 4194304 | bytes 2097152 | tf_op jit(solution)/shard_map/concatenate | solution.py:468
  14.8 0.0 collective-permute-done.3.refs_1_
  14.8 0.0 copy-start
  14.8 0.2 choose_qg.1
  15.0 1.1 %collective-permute-start.4 = (bf16[128,2048]{1,0:T(8,128)(2,1)S(1)}, bf16[128,2048]{1,0:T(8,128)(2,1)S(1)}, u32[]{:S(2)}, u32[]{:S(2)}) collective-permute-start(bf16[128,2048]{1,0:T(8,128)(2,1)S(1)} %get-tuple-element.41), channel_id=1, source_target_pairs={{0,4},{4,0},{8,12},{12,8},{16,20},{20,16},{24,28},{28,24},{1,5},{5... | collective-permute-start | bytes 1572872 | tf_op jit(solution)/shard_map/ppermute | solution.py:487
  16.1 1.3 %collective-permute-start.6 = (bf16[256,256]{1,0:T(8,128)(2,1)}, bf16[256,256]{1,0:T(8,128)(2,1)}, u32[]{:S(2)}, u32[]{:S(2)}) collective-permute-start(bf16[256,256]{1,0:T(8,128)(2,1)} %get-tuple-element.43.refs_6_), channel_id=1, source_target_pairs={{0,2},{1,3},{4,6},{5,7},{8,10},{9,11},{12,14},{13,15},{16,18},{17,... | collective-permute-start | bytes 393224 | tf_op jit(solution)/shard_map/ppermute | solution.py:432
  17.4 5.2 %collective-permute-start.7 = (bf16[256,256]{1,0:T(8,128)(2,1)}, bf16[256,256]{1,0:T(8,128)(2,1)}, u32[]{:S(2)}, u32[]{:S(2)}) collective-permute-start(bf16[256,256]{1,0:T(8,128)(2,1)} %get-tuple-element.47), channel_id=1, source_target_pairs={{0,24},{4,28},{8,2},{12,6},{16,10},{20,14},{24,18},{28,22},{1,25},... | collective-permute-start | bytes 393224 | tf_op jit(solution)/shard_map/ppermute | solution.py:421
  22.6 1.9 %collective-permute-start.8 = (bf16[256,256]{1,0:T(8,128)(2,1)S(1)}, bf16[256,256]{1,0:T(8,128)(2,1)}, u32[]{:S(2)}, u32[]{:S(2)}) collective-permute-start(bf16[256,256]{1,0:T(8,128)(2,1)S(1)} %get-tuple-element.48), channel_id=1, source_target_pairs={{0,16},{4,20},{8,24},{12,28},{16,2},{20,6},{24,10},{28,14},{1,17},... | collective-permute-start | bytes 393224 | tf_op jit(solution)/shard_map/ppermute | solution.py:421
  24.5 1.9 %collective-permute-start.9 = (bf16[256,256]{1,0:T(8,128)(2,1)S(1)}, bf16[256,256]{1,0:T(8,128)(2,1)}, u32[]{:S(2)}, u32[]{:S(2)}) collective-permute-start(bf16[256,256]{1,0:T(8,128)(2,1)S(1)} %get-tuple-element.49), channel_id=1, source_target_pairs={{0,8},{4,12},{8,16},{12,20},{16,24},{20,28},{24,2},{28,6},{1,9},{5... | collective-permute-start | bytes 393224 | tf_op jit(solution)/shard_map/ppermute | solution.py:421
  26.4 1.8 %collective-permute-done.4.refs_1_ = bf16[128,2048]{1,0:T(8,128)(2,1)S(1)} collective-permute-done((bf16[128,2048]{1,0:T(8,128)(2,1)S(1)}, bf16[128,2048]{1,0:T(8,128)(2,1)S(1)}, u32[]{:S(2)}, u32[]{:S(2)}) %collective-permute-start.4) | collective-permute-done | bytes 524320 | tf_op jit(solution)/shard_map/ppermute | solution.py:487
  28.2 0.9 %collective-permute-start.5 = (bf16[128,2048]{1,0:T(8,128)(2,1)S(1)}, bf16[128,2048]{1,0:T(8,128)(2,1)S(1)}, u32[]{:S(2)}, u32[]{:S(2)}) collective-permute-start(bf16[128,2048]{1,0:T(8,128)(2,1)S(1)} %get-tuple-element.46), channel_id=1, source_target_pairs={{0,4},{4,0},{8,12},{12,8},{16,20},{20,16},{24,28},{28,24},{1,5},{5... | collective-permute-start | bytes 1572872 | tf_op jit(solution)/shard_map/ppermute | solution.py:489
  29.1 6.1 %attend_odd.1 = (bf16[128,1024]{1,0:T(8,128)(2,1)S(1)}, bf16[128,1024]{1,0:T(8,128)(2,1)S(1)}, f32[256,256]{1,0:T(8,128)S(1)}, bf16[256,256]{1,0:T(8,128)(2,1)S(...) custom-call(bf16[128,2048]{1,0:T(8,128)(2,1)S(1)} %get-tuple-element.40.refs_0_, ...), custom_call_target="tpu_custom_call" | custom-call | flops 6000000000 | tf_op jit(solution)/shard_map/attend_odd/pallas_call | solution.py:41
  35.3 0.0 collective-permute-done.6.refs_4_
  35.3 2.2 %collective-permute-start.10 = (bf16[256,256]{1,0:T(8,128)(2,1)S(1)}, bf16[256,256]{1,0:T(8,128)(2,1)S(1)}, u32[]{:S(2)}, u32[]{:S(2)}) collective-permute-start(bf16[256,256]{1,0:T(8,128)(2,1)S(1)} %get-tuple-element.53), channel_id=1, source_target_pairs={{16,0},{20,4},{24,8},{28,12},{0,16},{4,20},{8,24},{12,28},{17,1},{... | collective-permute-start | bytes 393224 | tf_op jit(solution)/shard_map/ppermute | solution.py:421
  37.5 2.9 %collective-permute-start.11 = (bf16[256,256]{1,0:T(8,128)(2,1)S(1)}, bf16[256,256]{1,0:T(8,128)(2,1)S(1)}, u32[]{:S(2)}, u32[]{:S(2)}) collective-permute-start(bf16[256,256]{1,0:T(8,128)(2,1)S(1)} %get-tuple-element.54), channel_id=1, source_target_pairs={{8,0},{12,4},{16,8},{20,12},{24,16},{28,20},{0,24},{4,28},{9,1},{1... | collective-permute-start | bytes 393224 | tf_op jit(solution)/shard_map/ppermute | solution.py:421
  40.4 0.0 collective-permute-done.8.refs_6_
  40.4 0.4 collective-permute-start.12
  40.8 0.0 collective-permute-done.5.refs_1_
  40.8 5.6 %attend_even.1 = (bf16[128,1024]{1,0:T(8,128)(2,1)S(1)}, bf16[256,1024]{1,0:T(8,128)(2,1)S(1)}, bf16[256,256]{1,0:T(8,128)(2,1)S(1)}, bf16[256,256]{1,0:T(8,128)...) custom-call(bf16[128,2048]{1,0:T(8,128)(2,1)S(1)} %get-tuple-element.45.refs_0_, ...), custom_call_target="tpu_custom_call" | custom-call | flops 6000000000 | tf_op jit(solution)/shard_map/attend_even/pallas_call | solution.py:41
  46.5 1.0 %collective-permute-done.12.refs_3_ = bf16[256,256]{1,0:T(8,128)(2,1)S(1)} collective-permute-done((bf16[256,256]{1,0:T(8,128)(2,1)S(1)}, bf16[256,256]{1,0:T(8,128)(2,1)S(1)}, u32[]{:S(2)}, u32[]{:S(2)}) %collective-permute-start.12) | collective-permute-done | bytes 131104 | tf_op jit(solution)/shard_map/ppermute | solution.py:421
  47.5 0.2 odd_sum.1
  47.6 1.0 %collective-permute-start.13 = (bf16[256,1024]{1,0:T(8,128)(2,1)S(1)}, bf16[256,1024]{1,0:T(8,128)(2,1)S(1)}, u32[]{:S(2)}, u32[]{:S(2)}) collective-permute-start(bf16[256,1024]{1,0:T(8,128)(2,1)S(1)} %get-tuple-element.61), channel_id=1, source_target_pairs={{0,4},{4,0},{8,12},{12,8},{16,20},{20,16},{24,28},{28,24},{1,5},{5... | collective-permute-start | bytes 1572872 | tf_op jit(solution)/shard_map/ppermute | solution.py:541
  48.6 2.8 %collective-permute-start.14 = (bf16[256,256]{1,0:T(8,128)(2,1)S(1)}, bf16[256,256]{1,0:T(8,128)(2,1)S(1)}, u32[]{:S(2)}, u32[]{:S(2)}) collective-permute-start(bf16[256,256]{1,0:T(8,128)(2,1)S(1)} %get-tuple-element.65), channel_id=1, source_target_pairs={{2,0},{3,1},{6,4},{7,5},{10,8},{11,9},{14,12},{15,13},{18,16},{19,... | collective-permute-start | bytes 393224 | tf_op jit(solution)/shard_map/ppermute | solution.py:432
  51.5 5.1 %collective-permute-start.15 = (bf16[256,256]{1,0:T(8,128)(2,1)S(1)}, bf16[256,256]{1,0:T(8,128)(2,1)S(1)}, u32[]{:S(2)}, u32[]{:S(2)}) collective-permute-start(bf16[256,256]{1,0:T(8,128)(2,1)S(1)} %get-tuple-element.66), channel_id=1, source_target_pairs={{16,0},{20,4},{24,8},{28,12},{2,16},{6,20},{10,24},{14,28},{17,1},... | collective-permute-start | bytes 393224 | tf_op jit(solution)/shard_map/ppermute | solution.py:421
  56.6 2.6 %collective-permute-start.16 = (bf16[256,256]{1,0:T(8,128)(2,1)S(1)}, bf16[256,256]{1,0:T(8,128)(2,1)S(1)}, u32[]{:S(2)}, u32[]{:S(2)}) collective-permute-start(bf16[256,256]{1,0:T(8,128)(2,1)S(1)} %get-tuple-element.67), channel_id=1, source_target_pairs={{8,0},{12,4},{16,8},{20,12},{24,16},{28,20},{2,24},{6,28},{9,1},{1... | collective-permute-start | bytes 393224 | tf_op jit(solution)/shard_map/ppermute | solution.py:421
  59.2 1.9 %collective-permute-start.17 = (bf16[256,256]{1,0:T(8,128)(2,1)S(1)}, bf16[256,256]{1,0:T(8,128)(2,1)S(1)}, u32[]{:S(2)}, u32[]{:S(2)}) collective-permute-start(bf16[256,256]{1,0:T(8,128)(2,1)S(1)} %get-tuple-element.68), channel_id=1, source_target_pairs={{24,0},{28,4},{2,8},{6,12},{10,16},{14,20},{18,24},{22,28},{25,1},... | collective-permute-start | bytes 393224 | tf_op jit(solution)/shard_map/ppermute | solution.py:421
  61.1 2.3 %collective-permute-done.16.refs_5_ = bf16[256,256]{1,0:T(8,128)(2,1)S(1)} collective-permute-done((bf16[256,256]{1,0:T(8,128)(2,1)S(1)}, bf16[256,256]{1,0:T(8,128)(2,1)S(1)}, u32[]{:S(2)}, u32[]{:S(2)}) %collective-permute-start.16) | collective-permute-done | bytes 131104 | tf_op jit(solution)/shard_map/ppermute | solution.py:421
  63.4 4.6 %collective-permute-done.17.refs_6_ = bf16[256,256]{1,0:T(8,128)(2,1)S(1)} collective-permute-done((bf16[256,256]{1,0:T(8,128)(2,1)S(1)}, bf16[256,256]{1,0:T(8,128)(2,1)S(1)}, u32[]{:S(2)}, u32[]{:S(2)}) %collective-permute-start.17) | collective-permute-done | bytes 131104 | tf_op jit(solution)/shard_map/ppermute | solution.py:421
  68.1 0.3 home.1
  68.4 0.1 cross.1
  68.4 4.9 %collective-permute-start.18 = (bf16[128,2048]{1,0:T(8,128)(2,1)S(1)}, bf16[128,2048]{1,0:T(8,128)(2,1)S(1)}, u32[]{:S(2)}, u32[]{:S(2)}) collective-permute-start(bf16[128,2048]{1,0:T(8,128)(2,1)S(1)} %cross.1), channel_id=1, source_target_pairs={{0,1},{4,5},{8,9},{12,13},{16,17},{20,21},{24,25},{28,29},{1,0},{5... | collective-permute-start | bytes 1572872 | tf_op jit(solution)/shard_map/ppermute | solution.py:557
  73.3 0.1 collective-permute-start.19
  73.4 2.1 %collective-permute-start.21 = (bf16[128,256]{1,0:T(8,128)(2,1)S(1)}, bf16[128,256]{1,0:T(8,128)(2,1)S(1)}, u32[]{:S(2)}, u32[]{:S(2)}) collective-permute-start(bf16[128,256]{1,0:T(8,128)(2,1)S(1)} %get-tuple-element.72), channel_id=1, source_target_pairs={{0,5},{4,1},{8,13},{12,9},{16,21},{20,17},{24,29},{28,25},{1,4},{5... | collective-permute-start | bytes 196616 | tf_op jit(solution)/shard_map/ppermute | solution.py:404
  75.5 1.0 %collective-permute-done.20.refs_6_ = bf16[128,256]{1,0:T(8,128)(2,1)S(1)} collective-permute-done((bf16[128,256]{1,0:T(8,128)(2,1)S(1)}, bf16[128,256]{1,0:T(8,128)(2,1)S(1)}, u32[]{:S(2)}, u32[]{:S(2)}) %collective-permute-start.20) | collective-permute-done | bytes 65568 | tf_op jit(solution)/shard_map/ppermute | solution.py:404
  76.5 2.1 %collective-permute-done.21.refs_7_ = bf16[128,256]{1,0:T(8,128)(2,1)S(1)} collective-permute-done((bf16[128,256]{1,0:T(8,128)(2,1)S(1)}, bf16[128,256]{1,0:T(8,128)(2,1)S(1)}, u32[]{:S(2)}, u32[]{:S(2)}) %collective-permute-start.21) | collective-permute-done | bytes 65568 | tf_op jit(solution)/shard_map/ppermute | solution.py:404
  78.6 1.2 %finish.1 = (bf16[128,4096]{1,0:T(8,128)(2,1)}, bf16[128,512]{1,0:T(8,128)(2,1)}, bf16[128,512]{1,0:T(8,128)(2,1)}) custom-call(bf16[128,1024]{1,0:T(8,128)(2,1)S(1)} %get-tuple-element.44.refs_0_, bf16[128,1024]{1,0:T(8,128)(2,1)S(1)} %get-tuple-element.51.refs_1_, bf16[256,1024]{1,0:T(8,128)(2,1)S(1)} %collective-permute-done.13.refs_2_, ...), custom_call_target="tpu_custom_call" | custom-call | tf_op jit(solution)/shard_map/finish/pallas_call | solution.py:41
  (16 shorter events, 0.1 us)
Async XLA Ops:
  1.6 5.2 %collective-permute-start = (bf16[128,256]{1,0:T(8,128)(2,1)S(1)}, bf16[128,256]{1,0:T(8,128)(2,1)S(1)}, u32[]{:S(2)}, u32[]{:S(2)}) collective-permute-start(bf16[128,256]{1,0:T(8,128)(2,1)S(1)} %pad_maximum_fusion.3), channel_id=1, source_target_pairs={{0,1},{4,5},{8,9},{12,13},{16,17},{20,21},{24,25},{28,29},{1,0},{5... | collective-permute-start | bytes 196616 | tf_op jit(solution)/shard_map/ppermute | solution.py:404
  2.3 4.5 %collective-permute-start.1 = (bf16[128,256]{1,0:T(8,128)(2,1)S(1)}, bf16[128,256]{1,0:T(8,128)(2,1)S(1)}, u32[]{:S(2)}, u32[]{:S(2)}) collective-permute-start(bf16[128,256]{1,0:T(8,128)(2,1)S(1)} %pad_maximum_fusion.4), channel_id=1, source_target_pairs={{0,4},{4,0},{8,12},{12,8},{16,20},{20,16},{24,28},{28,24},{1,5},{5... | collective-permute-start | bytes 196616 | tf_op jit(solution)/shard_map/ppermute | solution.py:404
  3.7 4.1 %collective-permute-start.2 = (bf16[128,256]{1,0:T(8,128)(2,1)S(1)}, bf16[128,256]{1,0:T(8,128)(2,1)S(1)}, u32[]{:S(2)}, u32[]{:S(2)}) collective-permute-start(bf16[128,256]{1,0:T(8,128)(2,1)S(1)} %pad_maximum_fusion.5), channel_id=1, source_target_pairs={{0,5},{4,1},{8,13},{12,9},{16,21},{20,17},{24,29},{28,25},{1,4},{5... | collective-permute-start | bytes 196616 | tf_op jit(solution)/shard_map/ppermute | solution.py:404
  8.7 6.1 %collective-permute-start.3 = (bf16[128,4096]{1,0:T(8,128)(2,1)S(1)}, bf16[128,4096]{1,0:T(8,128)(2,1)S(1)}, u32[]{:S(2)}, u32[]{:S(2)}) collective-permute-start(bf16[128,4096]{1,0:T(8,128)(2,1)S(1)} %get-tuple-element.38), channel_id=1, source_target_pairs={{0,1},{4,5},{8,9},{12,13},{16,17},{20,21},{24,25},{28,29},{1,0},{5... | collective-permute-start | bytes 3145736 | tf_op jit(solution)/shard_map/ppermute | solution.py:481
  9.1 20.0 %all-to-all-start = ((bf16[4,256,256]{2,1,0:T(8,128)(2,1)}), bf16[4,256,256]{2,1,0:T(8,128)(2,1)S(1)}, u32[]{:S(2)}, u32[]{:S(2)}) async-start(bf16[4,256,256]{2,1,0:T(8,128)(2,1)} %bitcast.1), calls=%async_computation | async-start | bytes 1048576 | tf_op jit(solution)/shard_map/all_to_all | solution.py:426
  14.8 14.3 %copy-start = (s32[4096]{0:T(1024)S(1)}, s32[4096]{0:T(1024)}, u32[]{:S(2)}) copy-start(s32[4096]{0:T(1024)} %refs_3_.3) | copy-start | bytes 49156
  15.0 13.2 %collective-permute-start.4 = (bf16[128,2048]{1,0:T(8,128)(2,1)S(1)}, bf16[128,2048]{1,0:T(8,128)(2,1)S(1)}, u32[]{:S(2)}, u32[]{:S(2)}) collective-permute-start(bf16[128,2048]{1,0:T(8,128)(2,1)S(1)} %get-tuple-element.41), channel_id=1, source_target_pairs={{0,4},{4,0},{8,12},{12,8},{16,20},{20,16},{24,28},{28,24},{1,5},{5... | collective-permute-start | bytes 1572872 | tf_op jit(solution)/shard_map/ppermute | solution.py:487
  16.1 19.2 %collective-permute-start.6 = (bf16[256,256]{1,0:T(8,128)(2,1)}, bf16[256,256]{1,0:T(8,128)(2,1)}, u32[]{:S(2)}, u32[]{:S(2)}) collective-permute-start(bf16[256,256]{1,0:T(8,128)(2,1)} %get-tuple-element.43.refs_6_), channel_id=1, source_target_pairs={{0,2},{1,3},{4,6},{5,7},{8,10},{9,11},{12,14},{13,15},{16,18},{17,... | collective-permute-start | bytes 393224 | tf_op jit(solution)/shard_map/ppermute | solution.py:432
  17.4 20.1 %collective-permute-start.7 = (bf16[256,256]{1,0:T(8,128)(2,1)}, bf16[256,256]{1,0:T(8,128)(2,1)}, u32[]{:S(2)}, u32[]{:S(2)}) collective-permute-start(bf16[256,256]{1,0:T(8,128)(2,1)} %get-tuple-element.47), channel_id=1, source_target_pairs={{0,24},{4,28},{8,2},{12,6},{16,10},{20,14},{24,18},{28,22},{1,25},... | collective-permute-start | bytes 393224 | tf_op jit(solution)/shard_map/ppermute | solution.py:421
  22.6 17.8 %collective-permute-start.8 = (bf16[256,256]{1,0:T(8,128)(2,1)S(1)}, bf16[256,256]{1,0:T(8,128)(2,1)}, u32[]{:S(2)}, u32[]{:S(2)}) collective-permute-start(bf16[256,256]{1,0:T(8,128)(2,1)S(1)} %get-tuple-element.48), channel_id=1, source_target_pairs={{0,16},{4,20},{8,24},{12,28},{16,2},{20,6},{24,10},{28,14},{1,17},... | collective-permute-start | bytes 393224 | tf_op jit(solution)/shard_map/ppermute | solution.py:421
  24.5 16.3 %collective-permute-start.9 = (bf16[256,256]{1,0:T(8,128)(2,1)S(1)}, bf16[256,256]{1,0:T(8,128)(2,1)}, u32[]{:S(2)}, u32[]{:S(2)}) collective-permute-start(bf16[256,256]{1,0:T(8,128)(2,1)S(1)} %get-tuple-element.49), channel_id=1, source_target_pairs={{0,8},{4,12},{8,16},{12,20},{16,24},{20,28},{24,2},{28,6},{1,9},{5... | collective-permute-start | bytes 393224 | tf_op jit(solution)/shard_map/ppermute | solution.py:421
  28.2 12.6 %collective-permute-start.5 = (bf16[128,2048]{1,0:T(8,128)(2,1)S(1)}, bf16[128,2048]{1,0:T(8,128)(2,1)S(1)}, u32[]{:S(2)}, u32[]{:S(2)}) collective-permute-start(bf16[128,2048]{1,0:T(8,128)(2,1)S(1)} %get-tuple-element.46), channel_id=1, source_target_pairs={{0,4},{4,0},{8,12},{12,8},{16,20},{20,16},{24,28},{28,24},{1,5},{5... | collective-permute-start | bytes 1572872 | tf_op jit(solution)/shard_map/ppermute | solution.py:489
  35.3 11.2 %collective-permute-start.10 = (bf16[256,256]{1,0:T(8,128)(2,1)S(1)}, bf16[256,256]{1,0:T(8,128)(2,1)S(1)}, u32[]{:S(2)}, u32[]{:S(2)}) collective-permute-start(bf16[256,256]{1,0:T(8,128)(2,1)S(1)} %get-tuple-element.53), channel_id=1, source_target_pairs={{16,0},{20,4},{24,8},{28,12},{0,16},{4,20},{8,24},{12,28},{17,1},{... | collective-permute-start | bytes 393224 | tf_op jit(solution)/shard_map/ppermute | solution.py:421
  37.5 9.0 %collective-permute-start.11 = (bf16[256,256]{1,0:T(8,128)(2,1)S(1)}, bf16[256,256]{1,0:T(8,128)(2,1)S(1)}, u32[]{:S(2)}, u32[]{:S(2)}) collective-permute-start(bf16[256,256]{1,0:T(8,128)(2,1)S(1)} %get-tuple-element.54), channel_id=1, source_target_pairs={{8,0},{12,4},{16,8},{20,12},{24,16},{28,20},{0,24},{4,28},{9,1},{1... | collective-permute-start | bytes 393224 | tf_op jit(solution)/shard_map/ppermute | solution.py:421
  40.4 7.1 %collective-permute-start.12 = (bf16[256,256]{1,0:T(8,128)(2,1)S(1)}, bf16[256,256]{1,0:T(8,128)(2,1)S(1)}, u32[]{:S(2)}, u32[]{:S(2)}) collective-permute-start(bf16[256,256]{1,0:T(8,128)(2,1)S(1)} %get-tuple-element.55), channel_id=1, source_target_pairs={{24,0},{28,4},{0,8},{4,12},{8,16},{12,20},{16,24},{20,28},{25,1},{... | collective-permute-start | bytes 393224 | tf_op jit(solution)/shard_map/ppermute | solution.py:421
  47.6 20.7 %collective-permute-start.13 = (bf16[256,1024]{1,0:T(8,128)(2,1)S(1)}, bf16[256,1024]{1,0:T(8,128)(2,1)S(1)}, u32[]{:S(2)}, u32[]{:S(2)}) collective-permute-start(bf16[256,1024]{1,0:T(8,128)(2,1)S(1)} %get-tuple-element.61), channel_id=1, source_target_pairs={{0,4},{4,0},{8,12},{12,8},{16,20},{20,16},{24,28},{28,24},{1,5},{5... | collective-permute-start | bytes 1572872 | tf_op jit(solution)/shard_map/ppermute | solution.py:541
  48.6 12.5 %collective-permute-start.14 = (bf16[256,256]{1,0:T(8,128)(2,1)S(1)}, bf16[256,256]{1,0:T(8,128)(2,1)S(1)}, u32[]{:S(2)}, u32[]{:S(2)}) collective-permute-start(bf16[256,256]{1,0:T(8,128)(2,1)S(1)} %get-tuple-element.65), channel_id=1, source_target_pairs={{2,0},{3,1},{6,4},{7,5},{10,8},{11,9},{14,12},{15,13},{18,16},{19,... | collective-permute-start | bytes 393224 | tf_op jit(solution)/shard_map/ppermute | solution.py:432
  51.5 9.7 %collective-permute-start.15 = (bf16[256,256]{1,0:T(8,128)(2,1)S(1)}, bf16[256,256]{1,0:T(8,128)(2,1)S(1)}, u32[]{:S(2)}, u32[]{:S(2)}) collective-permute-start(bf16[256,256]{1,0:T(8,128)(2,1)S(1)} %get-tuple-element.66), channel_id=1, source_target_pairs={{16,0},{20,4},{24,8},{28,12},{2,16},{6,20},{10,24},{14,28},{17,1},... | collective-permute-start | bytes 393224 | tf_op jit(solution)/shard_map/ppermute | solution.py:421
  56.6 6.9 %collective-permute-start.16 = (bf16[256,256]{1,0:T(8,128)(2,1)S(1)}, bf16[256,256]{1,0:T(8,128)(2,1)S(1)}, u32[]{:S(2)}, u32[]{:S(2)}) collective-permute-start(bf16[256,256]{1,0:T(8,128)(2,1)S(1)} %get-tuple-element.67), channel_id=1, source_target_pairs={{8,0},{12,4},{16,8},{20,12},{24,16},{28,20},{2,24},{6,28},{9,1},{1... | collective-permute-start | bytes 393224 | tf_op jit(solution)/shard_map/ppermute | solution.py:421
  59.2 8.9 %collective-permute-start.17 = (bf16[256,256]{1,0:T(8,128)(2,1)S(1)}, bf16[256,256]{1,0:T(8,128)(2,1)S(1)}, u32[]{:S(2)}, u32[]{:S(2)}) collective-permute-start(bf16[256,256]{1,0:T(8,128)(2,1)S(1)} %get-tuple-element.68), channel_id=1, source_target_pairs={{24,0},{28,4},{2,8},{6,12},{10,16},{14,20},{18,24},{22,28},{25,1},... | collective-permute-start | bytes 393224 | tf_op jit(solution)/shard_map/ppermute | solution.py:421
  68.4 10.2 %collective-permute-start.18 = (bf16[128,2048]{1,0:T(8,128)(2,1)S(1)}, bf16[128,2048]{1,0:T(8,128)(2,1)S(1)}, u32[]{:S(2)}, u32[]{:S(2)}) collective-permute-start(bf16[128,2048]{1,0:T(8,128)(2,1)S(1)} %cross.1), channel_id=1, source_target_pairs={{0,1},{4,5},{8,9},{12,13},{16,17},{20,21},{24,25},{28,29},{1,0},{5... | collective-permute-start | bytes 1572872 | tf_op jit(solution)/shard_map/ppermute | solution.py:557
  73.3 2.1 %collective-permute-start.19 = (bf16[128,256]{1,0:T(8,128)(2,1)S(1)}, bf16[128,256]{1,0:T(8,128)(2,1)S(1)}, u32[]{:S(2)}, u32[]{:S(2)}) collective-permute-start(bf16[128,256]{1,0:T(8,128)(2,1)S(1)} %get-tuple-element.70), channel_id=1, source_target_pairs={{0,1},{4,5},{8,9},{12,13},{16,17},{20,21},{24,25},{28,29},{1,0},{5... | collective-permute-start | bytes 196616 | tf_op jit(solution)/shard_map/ppermute | solution.py:404
  73.4 3.1 %collective-permute-start.20 = (bf16[128,256]{1,0:T(8,128)(2,1)S(1)}, bf16[128,256]{1,0:T(8,128)(2,1)S(1)}, u32[]{:S(2)}, u32[]{:S(2)}) collective-permute-start(bf16[128,256]{1,0:T(8,128)(2,1)S(1)} %get-tuple-element.71), channel_id=1, source_target_pairs={{0,4},{4,0},{8,12},{12,8},{16,20},{20,16},{24,28},{28,24},{1,5},{5... | collective-permute-start | bytes 196616 | tf_op jit(solution)/shard_map/ppermute | solution.py:404
  73.4 5.2 %collective-permute-start.21 = (bf16[128,256]{1,0:T(8,128)(2,1)S(1)}, bf16[128,256]{1,0:T(8,128)(2,1)S(1)}, u32[]{:S(2)}, u32[]{:S(2)}) collective-permute-start(bf16[128,256]{1,0:T(8,128)(2,1)S(1)} %get-tuple-element.72), channel_id=1, source_target_pairs={{0,5},{4,1},{8,13},{12,9},{16,21},{20,17},{24,29},{28,25},{1,4},{5... | collective-permute-start | bytes 196616 | tf_op jit(solution)/shard_map/ppermute | solution.py:404

commit v6 on v5

--- a/solution.py
+++ b/solution.py
@@ -293,8 +293,8 @@
 
     for h in range(2 * heads):
         unit, head = h // heads, h % heads
-        dq = (dq_cols[:, h * tok : (h + 1) * tok] * inv_root).T
-        dq_both[unit, :, head * HEAD_DIM : (head + 1) * HEAD_DIM] = dq.astype(BF16)
+        dq = (dq_cols[:, h * tok : (h + 1) * tok] * inv_root).astype(BF16).T
+        dq_both[unit, :, head * HEAD_DIM : (head + 1) * HEAD_DIM] = dq
     dq_keep[...] = dq_both[y]
     dq_send[:tok, :] = dq_both[1 - y]
     if not odd:

time: 79.8 us -> 78.2 us (0.980)
  starting transfers between devices: 45.8 us -> 41.6 us
  Pallas kernels: 14.6 us -> 18.7 us
  waiting for transfers between devices: 13.8 us -> 12.5 us
    pallas_call x8, Pallas kernels: 14.6 us -> 18.7 us  [vmem_call(): pl.pallas_call(run, out_shape=list(out_shapes) + [jax.ShapeDtypeStruct(t....]
    ppermute x9, starting transfers between devices: 24.2 us -> 22.1 us  [along_z(): lax.ppermute(part, both, [(b, a) for a, b in route] if back else route)]
    ppermute x2, starting transfers between devices: 4.09 us -> 2.57 us  [along_x(): lax.ppermute(part, 'blk', [(b, b + step) for b in range(n_blk) if 0 <= b...]
    ppermute x9, waiting for transfers between devices: 7.94 us -> 6.62 us  [along_z(): lax.ppermute(part, both, [(b, a) for a, b in route] if back else route)]
  transfers between devices with their start and end apart: 23 -> 23, of which waited for: 7 -> 6; matrix products, arithmetic and copies ran while one was open for 5% -> 5% of each run, Pallas kernels for 15% -> 21%
where the time goes in v6:
time: 78.2 us; the launch traced here: 78.4 us
  starting transfers between devices  41.6 us (53%)
  Pallas kernels  18.7 us (24%)
  waiting for transfers between devices  12.5 us (16%)
  local copies, waits for them, and re-layouts  3.51 us (4%)
  other arithmetic  1.2 us (2%)
  between operations  0.92 us (1%)
    ppermute x9, starting transfers between devices, along_z(): lax.ppermute(part, both, [(b, a) for a, b in route] if back else route)  22.1 us
    pallas_call x8, Pallas kernels, vmem_call(): pl.pallas_call(run, out_shape=list(out_shapes) + [jax.ShapeDtypeStruct(t....  18.7 us
    ppermute x9, waiting for transfers between devices, along_z(): lax.ppermute(part, both, [(b, a) for a, b in route] if back else route)  6.62 us
    ppermute x6, starting transfers between devices, to_partners(): lax.ppermute(part, both, route)  4.66 us
    all_to_all x1, starting transfers between devices, gathered(): lax.all_to_all(pieces.reshape(n_out, pair, -1), 'swap', 0, 0, axis_index_...  4.59 us
    ppermute x1, starting transfers between devices, body(): lax.ppermute(dq_cross, both, routes[0])  4.29 us
    ppermute x6, waiting for transfers between devices, to_partners(): lax.ppermute(part, both, route)  4.05 us
    slice x1, local copies, waits for them, and re-layouts, halves(): x[:, i * q_width:(i + 1) * q_width]  2.59 us
  transfers between devices with their start and end apart: 23, of which 6 were waited for; matrix products, arithmetic and copies ran while one was open for 5% of the time, Pallas kernels for 21%

profile of v6, /device:TPU:3, one launch (start us, length us, event | category | flops | bytes accessed | tf_op | source)
XLA Modules:
  0.0 78.4 jit_solution(5811120404460620294)
XLA Ops:
  0.7 0.9 %constant_dynamic-slice_fusion.6 = (bf16[128,128]{1,0:T(8,128)(2,1)S(1)}, bf16[128,128]{1,0:T(8,128)(2,1)S(1)}, bf16[128,128]{1,0:T(8,128)(2,1)S(1)}, bf16[128,1...) fusion(bf16[128,512]{1,0:T(8,128)(2,1)} %param.7, ...), kind=kLoop, calls=%fused_computation.12 | loop fusion | bytes 524304 | tf_op jit(solution)/shard_map/dynamic_slice | solution.py:459
  1.6 0.7 collective-permute-start
  2.3 1.3 %collective-permute-start.1 = (bf16[128,256]{1,0:T(8,128)(2,1)S(1)}, bf16[128,256]{1,0:T(8,128)(2,1)S(1)}, u32[]{:S(2)}, u32[]{:S(2)}) collective-permute-start(bf16[128,256]{1,0:T(8,128)(2,1)S(1)} %pad_maximum_fusion.4), channel_id=1, source_target_pairs={{0,4},{4,0},{8,12},{12,8},{16,20},{20,16},{24,28},{28,24},{1,5},{5... | collective-permute-start | bytes 196616 | tf_op jit(solution)/shard_map/ppermute | solution.py:404
  3.7 0.5 collective-permute-start.2
  4.1 2.6 %constant_dynamic-slice_fusion = (bf16[128,1024]{1,0:T(8,128)(2,1)S(1)}, bf16[128,1024]{1,0:T(8,128)(2,1)S(1)}, bf16[128,1024]{1,0:T(8,128)(2,1)S(1)}, bf16[128,...) fusion(bf16[128,4096]{1,0:T(8,128)(2,1)} %param.8, ...), kind=kLoop, calls=%fused_computation.6 | loop fusion | bytes 4194320 | tf_op jit(solution)/shard_map/slice | solution.py:469
  6.7 0.1 pad_maximum_fusion.1.refs_4_
  6.8 0.0 collective-permute-done.refs_1_
  6.8 0.9 %collective-permute-done.2.refs_3_ = bf16[128,256]{1,0:T(8,128)(2,1)S(1)} collective-permute-done((bf16[128,256]{1,0:T(8,128)(2,1)S(1)}, bf16[128,256]{1,0:T(8,128)(2,1)S(1)}, u32[]{:S(2)}, u32[]{:S(2)}) %collective-permute-start.2) | collective-permute-done | bytes 65568 | tf_op jit(solution)/shard_map/ppermute | solution.py:404
  7.7 1.0 %payload.1 = (bf16[256,256]{1,0:T(8,128)(2,1)S(1)}, bf16[256,256]{1,0:T(8,128)(2,1)}, bf16[1024,256]{1,0:T(8,128)(2,1)}, bf16[256,256]{1,0:T(8,128)(2,1)S(1)}, b...) custom-call(bf16[128,256]{1,0:T(8,128)(2,1)S(1)} %pad_maximum_fusion, ...), custom_call_target="tpu_custom_call", output_to_operand_aliasing={{6}: (4, {})} | custom-call | tf_op jit(solution)/shard_map/payload/pallas_call | solution.py:41
  8.7 0.4 collective-permute-start.3
  9.1 4.6 %all-to-all-start = ((bf16[4,256,256]{2,1,0:T(8,128)(2,1)}), bf16[4,256,256]{2,1,0:T(8,128)(2,1)S(1)}, u32[]{:S(2)}, u32[]{:S(2)}) async-start(bf16[4,256,256]{2,1,0:T(8,128)(2,1)} %bitcast.1), calls=%async_computation | async-start | bytes 1048576 | tf_op jit(solution)/shard_map/all_to_all | solution.py:426
  13.7 1.1 %pad_maximum_fusion.refs_0_ = bf16[128,4096]{1,0:T(8,128)(2,1)S(1)} fusion(bf16[128,1024]{1,0:T(8,128)(2,1)S(1)} %get-tuple-element.80, bf16[128,1024]{1,0:T(8,128)(2,1)} %get-tuple-element.89, bf16[128,1024]{1,0:T(8,128)(2,1)S(1)} %get-tuple-element.78, bf16[128,1024]{1,0:T(8,128)(2,1)} %get-tuple-element.91), kind=kLoop, calls=%fused_computation | loop fusion | flops 4194304 | bytes 2097152 | tf_op jit(solution)/shard_map/concatenate | solution.py:468
  14.8 0.0 collective-permute-done.3.refs_1_
  14.8 0.0 copy-start
  14.8 0.2 choose_qg.1
  15.0 1.1 %collective-permute-start.4 = (bf16[128,2048]{1,0:T(8,128)(2,1)S(1)}, bf16[128,2048]{1,0:T(8,128)(2,1)S(1)}, u32[]{:S(2)}, u32[]{:S(2)}) collective-permute-start(bf16[128,2048]{1,0:T(8,128)(2,1)S(1)} %get-tuple-element.41), channel_id=1, source_target_pairs={{0,4},{4,0},{8,12},{12,8},{16,20},{20,16},{24,28},{28,24},{1,5},{5... | collective-permute-start | bytes 1572872 | tf_op jit(solution)/shard_map/ppermute | solution.py:487
  16.1 1.3 %collective-permute-start.6 = (bf16[256,256]{1,0:T(8,128)(2,1)}, bf16[256,256]{1,0:T(8,128)(2,1)}, u32[]{:S(2)}, u32[]{:S(2)}) collective-permute-start(bf16[256,256]{1,0:T(8,128)(2,1)} %get-tuple-element.43.refs_6_), channel_id=1, source_target_pairs={{0,2},{1,3},{4,6},{5,7},{8,10},{9,11},{12,14},{13,15},{16,18},{17,... | collective-permute-start | bytes 393224 | tf_op jit(solution)/shard_map/ppermute | solution.py:432
  17.4 5.2 %collective-permute-start.7 = (bf16[256,256]{1,0:T(8,128)(2,1)}, bf16[256,256]{1,0:T(8,128)(2,1)}, u32[]{:S(2)}, u32[]{:S(2)}) collective-permute-start(bf16[256,256]{1,0:T(8,128)(2,1)} %get-tuple-element.47), channel_id=1, source_target_pairs={{0,24},{4,28},{8,2},{12,6},{16,10},{20,14},{24,18},{28,22},{1,25},... | collective-permute-start | bytes 393224 | tf_op jit(solution)/shard_map/ppermute | solution.py:421
  22.6 1.9 %collective-permute-start.8 = (bf16[256,256]{1,0:T(8,128)(2,1)S(1)}, bf16[256,256]{1,0:T(8,128)(2,1)}, u32[]{:S(2)}, u32[]{:S(2)}) collective-permute-start(bf16[256,256]{1,0:T(8,128)(2,1)S(1)} %get-tuple-element.48), channel_id=1, source_target_pairs={{0,16},{4,20},{8,24},{12,28},{16,2},{20,6},{24,10},{28,14},{1,17},... | collective-permute-start | bytes 393224 | tf_op jit(solution)/shard_map/ppermute | solution.py:421
  24.5 1.9 %collective-permute-start.9 = (bf16[256,256]{1,0:T(8,128)(2,1)S(1)}, bf16[256,256]{1,0:T(8,128)(2,1)}, u32[]{:S(2)}, u32[]{:S(2)}) collective-permute-start(bf16[256,256]{1,0:T(8,128)(2,1)S(1)} %get-tuple-element.49), channel_id=1, source_target_pairs={{0,8},{4,12},{8,16},{12,20},{16,24},{20,28},{24,2},{28,6},{1,9},{5... | collective-permute-start | bytes 393224 | tf_op jit(solution)/shard_map/ppermute | solution.py:421
  26.4 1.8 %collective-permute-done.4.refs_1_ = bf16[128,2048]{1,0:T(8,128)(2,1)S(1)} collective-permute-done((bf16[128,2048]{1,0:T(8,128)(2,1)S(1)}, bf16[128,2048]{1,0:T(8,128)(2,1)S(1)}, u32[]{:S(2)}, u32[]{:S(2)}) %collective-permute-start.4) | collective-permute-done | bytes 524320 | tf_op jit(solution)/shard_map/ppermute | solution.py:487
  28.2 0.9 %collective-permute-start.5 = (bf16[128,2048]{1,0:T(8,128)(2,1)S(1)}, bf16[128,2048]{1,0:T(8,128)(2,1)S(1)}, u32[]{:S(2)}, u32[]{:S(2)}) collective-permute-start(bf16[128,2048]{1,0:T(8,128)(2,1)S(1)} %get-tuple-element.46), channel_id=1, source_target_pairs={{0,4},{4,0},{8,12},{12,8},{16,20},{20,16},{24,28},{28,24},{1,5},{5... | collective-permute-start | bytes 1572872 | tf_op jit(solution)/shard_map/ppermute | solution.py:489
  29.1 8.2 %attend_odd.1 = (bf16[128,1024]{1,0:T(8,128)(2,1)S(1)}, bf16[128,1024]{1,0:T(8,128)(2,1)S(1)}, f32[256,256]{1,0:T(8,128)S(1)}, bf16[256,256]{1,0:T(8,128)(2,1)S(...) custom-call(bf16[128,2048]{1,0:T(8,128)(2,1)S(1)} %get-tuple-element.40.refs_0_, ...), custom_call_target="tpu_custom_call" | custom-call | flops 6000000000 | tf_op jit(solution)/shard_map/attend_odd/pallas_call | solution.py:41
  37.3 0.1 collective-permute-start.10
  37.4 0.0 collective-permute-done.7.refs_5_
  37.4 5.1 %collective-permute-start.11 = (bf16[256,256]{1,0:T(8,128)(2,1)S(1)}, bf16[256,256]{1,0:T(8,128)(2,1)S(1)}, u32[]{:S(2)}, u32[]{:S(2)}) collective-permute-start(bf16[256,256]{1,0:T(8,128)(2,1)S(1)} %get-tuple-element.54), channel_id=1, source_target_pairs={{8,0},{12,4},{16,8},{20,12},{24,16},{28,20},{0,24},{4,28},{9,1},{1... | collective-permute-start | bytes 393224 | tf_op jit(solution)/shard_map/ppermute | solution.py:421
  42.5 0.0 collective-permute-done.8.refs_6_
  42.5 0.4 collective-permute-start.12
  42.9 7.6 %attend_even.1 = (bf16[128,1024]{1,0:T(8,128)(2,1)S(1)}, bf16[256,1024]{1,0:T(8,128)(2,1)S(1)}, bf16[256,256]{1,0:T(8,128)(2,1)S(1)}, bf16[256,256]{1,0:T(8,128)...) custom-call(bf16[128,2048]{1,0:T(8,128)(2,1)S(1)} %get-tuple-element.45.refs_0_, ...), custom_call_target="tpu_custom_call" | custom-call | flops 6000000000 | tf_op jit(solution)/shard_map/attend_even/pallas_call | solution.py:41
  50.6 0.0 collective-permute-done.10.refs_1_
  50.6 0.0 collective-permute-done.11.refs_2_
  50.6 0.2 odd_sum.1
  50.8 1.0 %collective-permute-start.13 = (bf16[256,1024]{1,0:T(8,128)(2,1)S(1)}, bf16[256,1024]{1,0:T(8,128)(2,1)S(1)}, u32[]{:S(2)}, u32[]{:S(2)}) collective-permute-start(bf16[256,1024]{1,0:T(8,128)(2,1)S(1)} %get-tuple-element.61), channel_id=1, source_target_pairs={{0,4},{4,0},{8,12},{12,8},{16,20},{20,16},{24,28},{28,24},{1,5},{5... | collective-permute-start | bytes 1572872 | tf_op jit(solution)/shard_map/ppermute | solution.py:541
  51.8 1.3 %collective-permute-start.14 = (bf16[256,256]{1,0:T(8,128)(2,1)S(1)}, bf16[256,256]{1,0:T(8,128)(2,1)S(1)}, u32[]{:S(2)}, u32[]{:S(2)}) collective-permute-start(bf16[256,256]{1,0:T(8,128)(2,1)S(1)} %get-tuple-element.65), channel_id=1, source_target_pairs={{2,0},{3,1},{6,4},{7,5},{10,8},{11,9},{14,12},{15,13},{18,16},{19,... | collective-permute-start | bytes 393224 | tf_op jit(solution)/shard_map/ppermute | solution.py:432
  53.1 3.5 %collective-permute-start.15 = (bf16[256,256]{1,0:T(8,128)(2,1)S(1)}, bf16[256,256]{1,0:T(8,128)(2,1)S(1)}, u32[]{:S(2)}, u32[]{:S(2)}) collective-permute-start(bf16[256,256]{1,0:T(8,128)(2,1)S(1)} %get-tuple-element.66), channel_id=1, source_target_pairs={{16,0},{20,4},{24,8},{28,12},{2,16},{6,20},{10,24},{14,28},{17,1},... | collective-permute-start | bytes 393224 | tf_op jit(solution)/shard_map/ppermute | solution.py:421
  56.6 2.1 %collective-permute-start.16 = (bf16[256,256]{1,0:T(8,128)(2,1)S(1)}, bf16[256,256]{1,0:T(8,128)(2,1)S(1)}, u32[]{:S(2)}, u32[]{:S(2)}) collective-permute-start(bf16[256,256]{1,0:T(8,128)(2,1)S(1)} %get-tuple-element.67), channel_id=1, source_target_pairs={{8,0},{12,4},{16,8},{20,12},{24,16},{28,20},{2,24},{6,28},{9,1},{1... | collective-permute-start | bytes 393224 | tf_op jit(solution)/shard_map/ppermute | solution.py:421
  58.7 1.9 %collective-permute-start.17 = (bf16[256,256]{1,0:T(8,128)(2,1)S(1)}, bf16[256,256]{1,0:T(8,128)(2,1)S(1)}, u32[]{:S(2)}, u32[]{:S(2)}) collective-permute-start(bf16[256,256]{1,0:T(8,128)(2,1)S(1)} %get-tuple-element.68), channel_id=1, source_target_pairs={{24,0},{28,4},{2,8},{6,12},{10,16},{14,20},{18,24},{22,28},{25,1},... | collective-permute-start | bytes 393224 | tf_op jit(solution)/shard_map/ppermute | solution.py:421
  60.6 0.0 collective-permute-done.15.refs_4_
  60.7 2.4 %collective-permute-done.16.refs_5_ = bf16[256,256]{1,0:T(8,128)(2,1)S(1)} collective-permute-done((bf16[256,256]{1,0:T(8,128)(2,1)S(1)}, bf16[256,256]{1,0:T(8,128)(2,1)S(1)}, u32[]{:S(2)}, u32[]{:S(2)}) %collective-permute-start.16) | collective-permute-done | bytes 131104 | tf_op jit(solution)/shard_map/ppermute | solution.py:421
  63.0 4.2 %collective-permute-done.17.refs_6_ = bf16[256,256]{1,0:T(8,128)(2,1)S(1)} collective-permute-done((bf16[256,256]{1,0:T(8,128)(2,1)S(1)}, bf16[256,256]{1,0:T(8,128)(2,1)S(1)}, u32[]{:S(2)}, u32[]{:S(2)}) %collective-permute-start.17) | collective-permute-done | bytes 131104 | tf_op jit(solution)/shard_map/ppermute | solution.py:421
  67.3 0.3 home.1
  67.6 0.1 cross.1
  67.6 4.3 %collective-permute-start.18 = (bf16[128,2048]{1,0:T(8,128)(2,1)S(1)}, bf16[128,2048]{1,0:T(8,128)(2,1)S(1)}, u32[]{:S(2)}, u32[]{:S(2)}) collective-permute-start(bf16[128,2048]{1,0:T(8,128)(2,1)S(1)} %cross.1), channel_id=1, source_target_pairs={{0,1},{4,5},{8,9},{12,13},{16,17},{20,21},{24,25},{28,29},{1,0},{5... | collective-permute-start | bytes 1572872 | tf_op jit(solution)/shard_map/ppermute | solution.py:557
  71.9 0.1 collective-permute-start.19
  72.0 2.1 %collective-permute-start.21 = (bf16[128,256]{1,0:T(8,128)(2,1)S(1)}, bf16[128,256]{1,0:T(8,128)(2,1)S(1)}, u32[]{:S(2)}, u32[]{:S(2)}) collective-permute-start(bf16[128,256]{1,0:T(8,128)(2,1)S(1)} %get-tuple-element.72), channel_id=1, source_target_pairs={{0,5},{4,1},{8,13},{12,9},{16,21},{20,17},{24,29},{28,25},{1,4},{5... | collective-permute-start | bytes 196616 | tf_op jit(solution)/shard_map/ppermute | solution.py:404
  74.1 1.0 %collective-permute-done.20.refs_6_ = bf16[128,256]{1,0:T(8,128)(2,1)S(1)} collective-permute-done((bf16[128,256]{1,0:T(8,128)(2,1)S(1)}, bf16[128,256]{1,0:T(8,128)(2,1)S(1)}, u32[]{:S(2)}, u32[]{:S(2)}) %collective-permute-start.20) | collective-permute-done | bytes 65568 | tf_op jit(solution)/shard_map/ppermute | solution.py:404
  75.1 2.1 %collective-permute-done.21.refs_7_ = bf16[128,256]{1,0:T(8,128)(2,1)S(1)} collective-permute-done((bf16[128,256]{1,0:T(8,128)(2,1)S(1)}, bf16[128,256]{1,0:T(8,128)(2,1)S(1)}, u32[]{:S(2)}, u32[]{:S(2)}) %collective-permute-start.21) | collective-permute-done | bytes 65568 | tf_op jit(solution)/shard_map/ppermute | solution.py:404
  77.2 1.2 %finish.1 = (bf16[128,4096]{1,0:T(8,128)(2,1)}, bf16[128,512]{1,0:T(8,128)(2,1)}, bf16[128,512]{1,0:T(8,128)(2,1)}) custom-call(bf16[128,1024]{1,0:T(8,128)(2,1)S(1)} %get-tuple-element.44.refs_0_, bf16[128,1024]{1,0:T(8,128)(2,1)S(1)} %get-tuple-element.51.refs_1_, bf16[256,1024]{1,0:T(8,128)(2,1)S(1)} %collective-permute-done.13.refs_2_, ...), custom_call_target="tpu_custom_call" | custom-call | tf_op jit(solution)/shard_map/finish/pallas_call | solution.py:41
  (16 shorter events, 0.1 us)
Async XLA Ops:
  1.6 5.2 %collective-permute-start = (bf16[128,256]{1,0:T(8,128)(2,1)S(1)}, bf16[128,256]{1,0:T(8,128)(2,1)S(1)}, u32[]{:S(2)}, u32[]{:S(2)}) collective-permute-start(bf16[128,256]{1,0:T(8,128)(2,1)S(1)} %pad_maximum_fusion.3), channel_id=1, source_target_pairs={{0,1},{4,5},{8,9},{12,13},{16,17},{20,21},{24,25},{28,29},{1,0},{5... | collective-permute-start | bytes 196616 | tf_op jit(solution)/shard_map/ppermute | solution.py:404
  2.3 4.5 %collective-permute-start.1 = (bf16[128,256]{1,0:T(8,128)(2,1)S(1)}, bf16[128,256]{1,0:T(8,128)(2,1)S(1)}, u32[]{:S(2)}, u32[]{:S(2)}) collective-permute-start(bf16[128,256]{1,0:T(8,128)(2,1)S(1)} %pad_maximum_fusion.4), channel_id=1, source_target_pairs={{0,4},{4,0},{8,12},{12,8},{16,20},{20,16},{24,28},{28,24},{1,5},{5... | collective-permute-start | bytes 196616 | tf_op jit(solution)/shard_map/ppermute | solution.py:404
  3.7 4.1 %collective-permute-start.2 = (bf16[128,256]{1,0:T(8,128)(2,1)S(1)}, bf16[128,256]{1,0:T(8,128)(2,1)S(1)}, u32[]{:S(2)}, u32[]{:S(2)}) collective-permute-start(bf16[128,256]{1,0:T(8,128)(2,1)S(1)} %pad_maximum_fusion.5), channel_id=1, source_target_pairs={{0,5},{4,1},{8,13},{12,9},{16,21},{20,17},{24,29},{28,25},{1,4},{5... | collective-permute-start | bytes 196616 | tf_op jit(solution)/shard_map/ppermute | solution.py:404
  8.7 6.1 %collective-permute-start.3 = (bf16[128,4096]{1,0:T(8,128)(2,1)S(1)}, bf16[128,4096]{1,0:T(8,128)(2,1)S(1)}, u32[]{:S(2)}, u32[]{:S(2)}) collective-permute-start(bf16[128,4096]{1,0:T(8,128)(2,1)S(1)} %get-tuple-element.38), channel_id=1, source_target_pairs={{0,1},{4,5},{8,9},{12,13},{16,17},{20,21},{24,25},{28,29},{1,0},{5... | collective-permute-start | bytes 3145736 | tf_op jit(solution)/shard_map/ppermute | solution.py:481
  9.1 20.0 %all-to-all-start = ((bf16[4,256,256]{2,1,0:T(8,128)(2,1)}), bf16[4,256,256]{2,1,0:T(8,128)(2,1)S(1)}, u32[]{:S(2)}, u32[]{:S(2)}) async-start(bf16[4,256,256]{2,1,0:T(8,128)(2,1)} %bitcast.1), calls=%async_computation | async-start | bytes 1048576 | tf_op jit(solution)/shard_map/all_to_all | solution.py:426
  14.8 14.3 %copy-start = (s32[4096]{0:T(1024)S(1)}, s32[4096]{0:T(1024)}, u32[]{:S(2)}) copy-start(s32[4096]{0:T(1024)} %refs_3_.3) | copy-start | bytes 49156
  15.0 13.2 %collective-permute-start.4 = (bf16[128,2048]{1,0:T(8,128)(2,1)S(1)}, bf16[128,2048]{1,0:T(8,128)(2,1)S(1)}, u32[]{:S(2)}, u32[]{:S(2)}) collective-permute-start(bf16[128,2048]{1,0:T(8,128)(2,1)S(1)} %get-tuple-element.41), channel_id=1, source_target_pairs={{0,4},{4,0},{8,12},{12,8},{16,20},{20,16},{24,28},{28,24},{1,5},{5... | collective-permute-start | bytes 1572872 | tf_op jit(solution)/shard_map/ppermute | solution.py:487
  16.1 21.2 %collective-permute-start.6 = (bf16[256,256]{1,0:T(8,128)(2,1)}, bf16[256,256]{1,0:T(8,128)(2,1)}, u32[]{:S(2)}, u32[]{:S(2)}) collective-permute-start(bf16[256,256]{1,0:T(8,128)(2,1)} %get-tuple-element.43.refs_6_), channel_id=1, source_target_pairs={{0,2},{1,3},{4,6},{5,7},{8,10},{9,11},{12,14},{13,15},{16,18},{17,... | collective-permute-start | bytes 393224 | tf_op jit(solution)/shard_map/ppermute | solution.py:432
  17.4 20.0 %collective-permute-start.7 = (bf16[256,256]{1,0:T(8,128)(2,1)}, bf16[256,256]{1,0:T(8,128)(2,1)}, u32[]{:S(2)}, u32[]{:S(2)}) collective-permute-start(bf16[256,256]{1,0:T(8,128)(2,1)} %get-tuple-element.47), channel_id=1, source_target_pairs={{0,24},{4,28},{8,2},{12,6},{16,10},{20,14},{24,18},{28,22},{1,25},... | collective-permute-start | bytes 393224 | tf_op jit(solution)/shard_map/ppermute | solution.py:421
  22.6 19.9 %collective-permute-start.8 = (bf16[256,256]{1,0:T(8,128)(2,1)S(1)}, bf16[256,256]{1,0:T(8,128)(2,1)}, u32[]{:S(2)}, u32[]{:S(2)}) collective-permute-start(bf16[256,256]{1,0:T(8,128)(2,1)S(1)} %get-tuple-element.48), channel_id=1, source_target_pairs={{0,16},{4,20},{8,24},{12,28},{16,2},{20,6},{24,10},{28,14},{1,17},... | collective-permute-start | bytes 393224 | tf_op jit(solution)/shard_map/ppermute | solution.py:421
  24.5 18.4 %collective-permute-start.9 = (bf16[256,256]{1,0:T(8,128)(2,1)S(1)}, bf16[256,256]{1,0:T(8,128)(2,1)}, u32[]{:S(2)}, u32[]{:S(2)}) collective-permute-start(bf16[256,256]{1,0:T(8,128)(2,1)S(1)} %get-tuple-element.49), channel_id=1, source_target_pairs={{0,8},{4,12},{8,16},{12,20},{16,24},{20,28},{24,2},{28,6},{1,9},{5... | collective-permute-start | bytes 393224 | tf_op jit(solution)/shard_map/ppermute | solution.py:421
  28.2 14.7 %collective-permute-start.5 = (bf16[128,2048]{1,0:T(8,128)(2,1)S(1)}, bf16[128,2048]{1,0:T(8,128)(2,1)S(1)}, u32[]{:S(2)}, u32[]{:S(2)}) collective-permute-start(bf16[128,2048]{1,0:T(8,128)(2,1)S(1)} %get-tuple-element.46), channel_id=1, source_target_pairs={{0,4},{4,0},{8,12},{12,8},{16,20},{20,16},{24,28},{28,24},{1,5},{5... | collective-permute-start | bytes 1572872 | tf_op jit(solution)/shard_map/ppermute | solution.py:489
  37.3 13.3 %collective-permute-start.10 = (bf16[256,256]{1,0:T(8,128)(2,1)S(1)}, bf16[256,256]{1,0:T(8,128)(2,1)S(1)}, u32[]{:S(2)}, u32[]{:S(2)}) collective-permute-start(bf16[256,256]{1,0:T(8,128)(2,1)S(1)} %get-tuple-element.53), channel_id=1, source_target_pairs={{16,0},{20,4},{24,8},{28,12},{0,16},{4,20},{8,24},{12,28},{17,1},{... | collective-permute-start | bytes 393224 | tf_op jit(solution)/shard_map/ppermute | solution.py:421
  37.4 13.2 %collective-permute-start.11 = (bf16[256,256]{1,0:T(8,128)(2,1)S(1)}, bf16[256,256]{1,0:T(8,128)(2,1)S(1)}, u32[]{:S(2)}, u32[]{:S(2)}) collective-permute-start(bf16[256,256]{1,0:T(8,128)(2,1)S(1)} %get-tuple-element.54), channel_id=1, source_target_pairs={{8,0},{12,4},{16,8},{20,12},{24,16},{28,20},{0,24},{4,28},{9,1},{1... | collective-permute-start | bytes 393224 | tf_op jit(solution)/shard_map/ppermute | solution.py:421
  42.5 8.1 %collective-permute-start.12 = (bf16[256,256]{1,0:T(8,128)(2,1)S(1)}, bf16[256,256]{1,0:T(8,128)(2,1)S(1)}, u32[]{:S(2)}, u32[]{:S(2)}) collective-permute-start(bf16[256,256]{1,0:T(8,128)(2,1)S(1)} %get-tuple-element.55), channel_id=1, source_target_pairs={{24,0},{28,4},{0,8},{4,12},{8,16},{12,20},{16,24},{20,28},{25,1},{... | collective-permute-start | bytes 393224 | tf_op jit(solution)/shard_map/ppermute | solution.py:421
  50.8 16.8 %collective-permute-start.13 = (bf16[256,1024]{1,0:T(8,128)(2,1)S(1)}, bf16[256,1024]{1,0:T(8,128)(2,1)S(1)}, u32[]{:S(2)}, u32[]{:S(2)}) collective-permute-start(bf16[256,1024]{1,0:T(8,128)(2,1)S(1)} %get-tuple-element.61), channel_id=1, source_target_pairs={{0,4},{4,0},{8,12},{12,8},{16,20},{20,16},{24,28},{28,24},{1,5},{5... | collective-permute-start | bytes 1572872 | tf_op jit(solution)/shard_map/ppermute | solution.py:541
  51.8 8.8 %collective-permute-start.14 = (bf16[256,256]{1,0:T(8,128)(2,1)S(1)}, bf16[256,256]{1,0:T(8,128)(2,1)S(1)}, u32[]{:S(2)}, u32[]{:S(2)}) collective-permute-start(bf16[256,256]{1,0:T(8,128)(2,1)S(1)} %get-tuple-element.65), channel_id=1, source_target_pairs={{2,0},{3,1},{6,4},{7,5},{10,8},{11,9},{14,12},{15,13},{18,16},{19,... | collective-permute-start | bytes 393224 | tf_op jit(solution)/shard_map/ppermute | solution.py:432
  53.1 7.6 %collective-permute-start.15 = (bf16[256,256]{1,0:T(8,128)(2,1)S(1)}, bf16[256,256]{1,0:T(8,128)(2,1)S(1)}, u32[]{:S(2)}, u32[]{:S(2)}) collective-permute-start(bf16[256,256]{1,0:T(8,128)(2,1)S(1)} %get-tuple-element.66), channel_id=1, source_target_pairs={{16,0},{20,4},{24,8},{28,12},{2,16},{6,20},{10,24},{14,28},{17,1},... | collective-permute-start | bytes 393224 | tf_op jit(solution)/shard_map/ppermute | solution.py:421
  56.6 6.4 %collective-permute-start.16 = (bf16[256,256]{1,0:T(8,128)(2,1)S(1)}, bf16[256,256]{1,0:T(8,128)(2,1)S(1)}, u32[]{:S(2)}, u32[]{:S(2)}) collective-permute-start(bf16[256,256]{1,0:T(8,128)(2,1)S(1)} %get-tuple-element.67), channel_id=1, source_target_pairs={{8,0},{12,4},{16,8},{20,12},{24,16},{28,20},{2,24},{6,28},{9,1},{1... | collective-permute-start | bytes 393224 | tf_op jit(solution)/shard_map/ppermute | solution.py:421
  58.7 8.6 %collective-permute-start.17 = (bf16[256,256]{1,0:T(8,128)(2,1)S(1)}, bf16[256,256]{1,0:T(8,128)(2,1)S(1)}, u32[]{:S(2)}, u32[]{:S(2)}) collective-permute-start(bf16[256,256]{1,0:T(8,128)(2,1)S(1)} %get-tuple-element.68), channel_id=1, source_target_pairs={{24,0},{28,4},{2,8},{6,12},{10,16},{14,20},{18,24},{22,28},{25,1},... | collective-permute-start | bytes 393224 | tf_op jit(solution)/shard_map/ppermute | solution.py:421
  67.6 9.6 %collective-permute-start.18 = (bf16[128,2048]{1,0:T(8,128)(2,1)S(1)}, bf16[128,2048]{1,0:T(8,128)(2,1)S(1)}, u32[]{:S(2)}, u32[]{:S(2)}) collective-permute-start(bf16[128,2048]{1,0:T(8,128)(2,1)S(1)} %cross.1), channel_id=1, source_target_pairs={{0,1},{4,5},{8,9},{12,13},{16,17},{20,21},{24,25},{28,29},{1,0},{5... | collective-permute-start | bytes 1572872 | tf_op jit(solution)/shard_map/ppermute | solution.py:557
  71.9 2.1 %collective-permute-start.19 = (bf16[128,256]{1,0:T(8,128)(2,1)S(1)}, bf16[128,256]{1,0:T(8,128)(2,1)S(1)}, u32[]{:S(2)}, u32[]{:S(2)}) collective-permute-start(bf16[128,256]{1,0:T(8,128)(2,1)S(1)} %get-tuple-element.70), channel_id=1, source_target_pairs={{0,1},{4,5},{8,9},{12,13},{16,17},{20,21},{24,25},{28,29},{1,0},{5... | collective-permute-start | bytes 196616 | tf_op jit(solution)/shard_map/ppermute | solution.py:404
  72.0 3.1 %collective-permute-start.20 = (bf16[128,256]{1,0:T(8,128)(2,1)S(1)}, bf16[128,256]{1,0:T(8,128)(2,1)S(1)}, u32[]{:S(2)}, u32[]{:S(2)}) collective-permute-start(bf16[128,256]{1,0:T(8,128)(2,1)S(1)} %get-tuple-element.71), channel_id=1, source_target_pairs={{0,4},{4,0},{8,12},{12,8},{16,20},{20,16},{24,28},{28,24},{1,5},{5... | collective-permute-start | bytes 196616 | tf_op jit(solution)/shard_map/ppermute | solution.py:404
  72.0 5.2 %collective-permute-start.21 = (bf16[128,256]{1,0:T(8,128)(2,1)S(1)}, bf16[128,256]{1,0:T(8,128)(2,1)S(1)}, u32[]{:S(2)}, u32[]{:S(2)}) collective-permute-start(bf16[128,256]{1,0:T(8,128)(2,1)S(1)} %get-tuple-element.72), channel_id=1, source_target_pairs={{0,5},{4,1},{8,13},{12,9},{16,21},{20,17},{24,29},{28,25},{1,4},{5... | collective-permute-start | bytes 196616 | tf_op jit(solution)/shard_map/ppermute | solution.py:404
